TPU v7x, 32 devices: a whole 2x2x4 slice. The times are simulated.
32 devices in a mesh: patch: 2 (over y), sky: 4 (over z), exp: 2 (over core), band: 2 (over x).
Axes of the slice: x: 2, y: 2, z: 4, core: 2. Of those that a mesh axis runs over, the one named last changes fastest.
Arguments:
- images: bfloat16 [2, 20, 1024, 512], P('band', 'exp', ('patch', 'sky')), parts along dimension 2, may hold values from -400 to 400
- valid_mask: int32 [2, 20, 1024, 512], P('band', 'exp', ('patch', 'sky')), parts along dimension 2, may hold values from 0 to 1, as said below
- row_kernel: float32 [2, 20, 31], P('band', 'exp'), may hold values from 0.01 to 0.06
- col_kernel: float32 [2, 20, 31], P('band', 'exp'), may hold values from 0.01 to 0.06
- exp_group: int32 [2, 20], P('band', 'exp'), may hold values from 0 to 15
- zero_point: float32 [2, 16], P('band'), may hold values from 0.5 to 2
- psf_row: float32 [2, 31], P('band'), may hold values from 0.01 to 0.06
- psf_col: float32 [2, 31], P('band'), may hold values from 0.01 to 0.06
Outputs:
- coadd_image: float32 [2, 1024, 512], P('band', ('patch', 'sky')), parts along dimension 1
- detection: float32 [1024, 512], P(('patch', 'sky'), 'band'), parts along dimension 0
There are 2 independent parts, one for each index of `patch`. A program takes and returns all parts, laid end to end along the dimension named above; an argument that names none is the same for every part. Nothing has to cross between parts.
Inputs may be any that keep to these rules, and one draw needn't show every extreme that they name: For every band and pixel at least 10 of the 20 visits have valid_mask 1; exactly that many at some pixels, all of them at others.
All inputs are finite; a program needn't handle non-finite values.
Results may differ from a plain program's by a relative error of at most 0.0006.
Values may be sent and summed in bfloat16 or wider, within the bound.
No kernel may reach another device: no remote copies, remote signals or barrier semaphores. Data moves between devices by JAX's collectives and lax.ppermute only.
A program may use at most 64 MiB of HBM per device.

v0:
```python
import jax
import jax.numpy as jnp
from jax import lax
from jax.sharding import PartitionSpec as P

HALF = 15
REJECT = 4
GROUPS = 16
TAPS = 31


SENTINEL = 1e30
EPSILON = 1e-05


def padded_2(value, sides, width):
    for axis, dim in sides:
        size, length = (lax.axis_size(axis), value.shape[dim])
        up = [(i, (i + 1) % size) for i in range(size - 1)]
        down = [(j, i) for i, j in up]
        last = lax.slice_in_dim(value, length - width, length, axis=dim)
        first = lax.slice_in_dim(value, 0, width, axis=dim)
        before = lax.ppermute(last, axis, up)
        after = lax.ppermute(first, axis, down)
        value = jnp.concatenate([before, value, after], axis=dim)
    return value


def merged_2(part, axis, combine):
    gathered = jax.tree.map(lambda a: lax.all_gather(a, axis), part)

    def take(source):
        return jax.tree.map(lambda a: lax.dynamic_index_in_dim(a, source, 0, False), gathered)

    return lax.fori_loop(
        1, lax.axis_size(axis), lambda source, state: combine(state, take(source)), take(0)
    )


def shortened(value):
    return jax.tree.map(lambda a: a.astype(jnp.bfloat16) if a.dtype == jnp.float32 else a, value)


def rows_filter(padded, kernel, height):
    result = kernel[..., 0][..., None, None] * padded[..., 0:height, :]
    for offset in range(1, TAPS):
        result = (
            result + kernel[..., offset][..., None, None] * padded[..., offset : offset + height, :]
        )
    return result


def cols_filter(grid_in, kernel):
    columns = grid_in.shape[-1]
    widths = [(0, 0)] * (grid_in.ndim - 1) + [(HALF, HALF)]
    padded = jnp.pad(grid_in, widths)
    result = kernel[..., 0][..., None, None] * padded[..., 0:columns]
    for offset in range(1, TAPS):
        result = (
            result + kernel[..., offset][..., None, None] * padded[..., offset : offset + columns]
        )
    return result


def insert_high(sorted_list, incoming):
    updated = []
    for position in range(REJECT):
        updated.append(jnp.maximum(sorted_list[position], incoming))
        incoming = jnp.minimum(sorted_list[position], incoming)
    return tuple(updated)


def insert_low(sorted_list, incoming):
    updated = []
    for position in range(REJECT):
        updated.append(jnp.minimum(sorted_list[position], incoming))
        incoming = jnp.maximum(sorted_list[position], incoming)
    return tuple(updated)


def visit_stats(visit_values, usable):
    plane = visit_values.shape[1:]
    upper_list = tuple((jnp.full(plane, -SENTINEL, jnp.float32) for position in range(REJECT)))
    lower_list = tuple((jnp.full(plane, SENTINEL, jnp.float32) for position in range(REJECT)))
    for visit_num in range(visit_values.shape[0]):
        current = visit_values[visit_num]
        is_live = usable[visit_num]
        upper_list = insert_high(upper_list, jnp.where(is_live, current, -SENTINEL))
        lower_list = insert_low(lower_list, jnp.where(is_live, current, SENTINEL))
    flux_sum = jnp.sum(jnp.where(usable, visit_values, jnp.float32(0.0)), axis=0)
    valid_count = jnp.sum(usable.astype(jnp.float32), axis=0)
    return (jnp.stack(upper_list), jnp.stack(lower_list), flux_sum, valid_count)


def combine_lists(left_side, right_side):
    upper_list = tuple((left_side[0][position] for position in range(REJECT)))
    lower_list = tuple((left_side[1][position] for position in range(REJECT)))
    for position in range(REJECT):
        upper_list = insert_high(upper_list, right_side[0][position])
        lower_list = insert_low(lower_list, right_side[1][position])
    return (
        jnp.stack(upper_list),
        jnp.stack(lower_list),
        left_side[2] + right_side[2],
        left_side[3] + right_side[3],
    )


def coadd_from(summary):
    upper_sum = jnp.sum(summary[0], axis=0)
    lower_sum = jnp.sum(summary[1], axis=0)
    return (summary[2] - upper_sum - lower_sum) / (summary[3] - 2 * REJECT)


def on_device(images, valid_mask, row_kernel, col_kernel, exp_group, zero_point, psf_row, psf_col):
    height = images.shape[2]
    padded = padded_2(images[0], (("sky", 1),), HALF)
    matches = exp_group[0][:, None] == jnp.arange(GROUPS, dtype=jnp.int32)[None, :]
    flux_scale = jnp.sum(jnp.where(matches, zero_point[0][None, :], jnp.float32(0.0)), axis=1)
    smeared = cols_filter(
        rows_filter(padded.astype(jnp.float32), row_kernel[0], height), col_kernel[0]
    )
    scaled_visits = flux_scale[:, None, None] * smeared
    usable = valid_mask[0] == 1
    summary = visit_stats(scaled_visits, usable)
    merged = merged_2(summary, "exp", combine_lists)
    coadd_image = coadd_from(merged)
    coadd_pad = padded_2(shortened(coadd_image), (("sky", 0),), HALF).astype(coadd_image.dtype)
    filtered = cols_filter(rows_filter(coadd_pad, psf_row[0], height), psf_col[0])
    energy = filtered * filtered
    energy_sum = lax.psum(jnp.sum(energy), "sky")
    variance = energy_sum / (height * lax.axis_size("sky") * energy.shape[1]) + EPSILON
    detection = lax.psum_scatter(energy / variance, "band", scatter_dimension=1, tiled=True)
    return (coadd_image[None], detection)


def solution(mesh):
    placed = (
        P("band", "exp", ("patch", "sky"), None),
        P("band", "exp", ("patch", "sky"), None),
        P("band", "exp", None),
        P("band", "exp", None),
        P("band", "exp"),
        P("band", None),
        P("band", None),
        P("band", None),
    )
    return jax.shard_map(
        on_device,
        mesh=mesh,
        in_specs=placed,
        out_specs=(P("band", ("patch", "sky"), None), P(("patch", "sky"), "band")),
        check_vma=False,
    )
```

profile of v0, /device:TPU:0, one launch (start us, length us, event | category | flops | bytes accessed | tf_op | source)
XLA Modules:
  0.0 164.6 jit_solution(17825145032995338779)
XLA Ops:
  7.2 1.0 fusion.270
  8.3 4.9 %collective-permute-start = (bf16[10,15,512]{2,1,0:T(8,128)(2,1)S(1)}, bf16[10,15,512]{2,1,0:T(8,128)(2,1)S(1)}, u32[]{:S(2)}, u32[]{:S(2)}) collective-permute-start(bf16[10,15,512]{2,1,0:T(8,128)(2,1)S(1)} %get-tuple-element.137), channel_id=1, source_target_pairs={{0,4},{4,8},{8,12},{1,5},{5,9},{9,13},{2,6},{6,10},{10,14},{3,7},{... | collective-permute-start | bytes 460808 | tf_op jit(solution)/shard_map/ppermute | solution.py:23
  13.2 1.3 collective-permute-start.1
  16.8 0.9 select_reduce_fusion.1
  18.5 2.3 %collective-permute-done.1 = bf16[10,15,512]{2,1,0:T(8,128)(2,1)S(1)} collective-permute-done((bf16[10,15,512]{2,1,0:T(8,128)(2,1)S(1)}, bf16[10,15,512]{2,1,0:T(8,128)(2,1)S(1)}, u32[]{:S(2)}, u32[]{:S(2)}) %collective-permute-start.1) | collective-permute-done | bytes 153632 | tf_op jit(solution)/shard_map/ppermute | solution.py:24
  20.8 1.8 %maximum_convert_fusion = f32[10,158,512]{2,1,0:T(8,128)S(1)} fusion(bf16[10,15,512]{2,1,0:T(8,128)(2,1)S(1)} %collective-permute-done.1, bf16[10,128,512]{2,1,0:T(8,128)(2,1)} %bitcast.349, bf16[10,15,512]{2,1,0:T(8,128)(2,1)S(1)} %collective-permute-done), kind=kLoop, calls=%fused_computation.154 | loop fusion | flops 4853760 | bytes 4853760 | tf_op jit(solution)/shard_map/convert_element_type | solution.py:121
  22.6 10.6 %fusion.61 = f32[10,128,512]{2,1,0:T(8,128)S(1)} fusion(f32[10,158,512]{2,1,0:T(8,128)S(1)} %maximum_convert_fusion, f32[10]{0:T(128)S(1)} %get-tuple-element.66, f32[10]{0:T(128)S(1)} %get-tuple-element.67, f32[10]{0:T(128)S(1)} %get-tuple-element.68, f32[10]{0:T(128)S(1)} %get-tuple-element.69, f32[10]{0:T(128)S(1)} %get-tuple-element.70, ...), kind=kLoop, calls=%fused_computation.92 | loop fusion | flops 39976960 | bytes 83887320 | tf_op jit(solution)/shard_map/add | solution.py:48
  33.2 21.9 %convert_reduce_fusion = (f32[128,512]{1,0:T(8,128)S(1)}, f32[128,512]{1,0:T(8,128)}, pred[1,10,128,512]{3,2,1,0:T(8,128)(4,1)S(1)}, f32[10,128,512]{2,1,0:T(8,128)S(1)}) fusion(s32[1,10,128,512]{3,2,1,0:T(8,128)S(1)} %copy-done, f32[10]{0:T(128)S(1)} %get-tuple-element.25, f32[10]{0:T(128)S(1)} %get-tuple-element.26, f32[10]{0:T(128)S(1)} %get-tuple-element.27, ...), kind=kLoop, calls=%fused_computation.152 | loop fusion | flops 43778048 | bytes 9045248 | tf_op jit(solution)/shard_map/reduce_sum | solution.py:91
  56.5 1.1 pad_maximum_fusion.1
  59.1 1.1 pad_maximum_fusion
  61.8 0.7 fusion.272
  62.5 2.4 %all-gather = f32[256,512]{1,0:T(8,128)S(1)} all-gather(f32[128,512]{1,0:T(8,128)S(1)} %copy-done.1), channel_id=2, replica_groups=mesh['patch'=2,'sky'=4,'exp'=2,'band'=2] {'exp'}, dimensions={0}, use_global_device_ids=true | all-gather | bytes 786432 | tf_op jit(solution)/shard_map/all_gather | solution.py:30
  64.8 2.5 %all-gather.3 = f32[256,512]{1,0:T(8,128)S(1)} all-gather(f32[128,512]{1,0:T(8,128)S(1)} %get-tuple-element.22), channel_id=5, replica_groups=mesh['patch'=2,'sky'=4,'exp'=2,'band'=2] {'exp'}, dimensions={0}, use_global_device_ids=true | all-gather | bytes 786432 | tf_op jit(solution)/shard_map/all_gather | solution.py:30
  67.3 1.4 all-gather.9.cloned.1.call-done
  68.7 13.2 %all-gather.7.cloned.1.call-done = f32[8,128,512]{2,1,0:T(8,128)} async-done(((f32[4,128,512]{2,1,0:T(8,128)}), f32[8,128,512]{2,1,0:T(8,128)}) %all-gather.7.cloned.1.call-update) | async-done | bytes 2097168 | tf_op jit(solution)/shard_map/all_gather | solution.py:30
  81.9 2.8 %fusion.206 = (bf16[128,512]{1,0:T(8,128)(2,1)S(1)}, f32[1,1,128,512]{3,2,1,0:T(8,128)S(1)}, f32[1,1,128,512]{3,2,1,0:T(8,128)S(1)}) fusion(f32[256,512]{1,0:T(8,128)S(1)} %all-gather, f32[256,512]{1,0:T(8,128)S(1)} %all-gather.3, f32[2,4,128,512]{3,2,1,0:T(8,128)} %bitcast.347, f32[2,4,128,512]{3,2,1,0:T(8,128)} %bitcast.346), kind=kLoop, calls=%fused_computation.343 | loop fusion | flops 4521984 | bytes 5898240 | tf_op jit(solution)/shard_map/convert_element_type | solution.py:41
  84.7 3.6 %collective-permute-start.2 = (bf16[15,512]{1,0:T(8,128)(2,1)S(1)}, bf16[15,512]{1,0:T(8,128)(2,1)S(1)}, u32[]{:S(2)}, u32[]{:S(2)}) collective-permute-start(bf16[15,512]{1,0:T(8,128)(2,1)S(1)} %get-tuple-element.139), channel_id=1, source_target_pairs={{0,4},{4,8},{8,12},{1,5},{5,9},{9,13},{2,6},{6,10},{10,14},{3,7},{... | collective-permute-start | bytes 46088 | tf_op jit(solution)/shard_map/ppermute | solution.py:23
  88.4 1.3 collective-permute-start.3
  90.4 3.6 %collective-permute-done.3 = bf16[15,512]{1,0:T(8,128)(2,1)S(1)} collective-permute-done((bf16[15,512]{1,0:T(8,128)(2,1)S(1)}, bf16[15,512]{1,0:T(8,128)(2,1)S(1)}, u32[]{:S(2)}, u32[]{:S(2)}) %collective-permute-start.3) | collective-permute-done | bytes 15392 | tf_op jit(solution)/shard_map/ppermute | solution.py:24
  94.0 20.1 %fusion.166 = f32[128,512]{1,0:T(8,128)S(1)} fusion(f32[158,512]{1,0:T(8,128)S(1)} %maximum_convert_fusion.1, f32[]{:T(128)} %bitcast.53, f32[]{:T(128)} %bitcast.52, f32[]{:T(128)} %bitcast.51, f32[]{:T(128)} %bitcast.50, f32[]{:T(128)} %bitcast.49, f32[]{:T(128)} %bitcast.48, f32[]{:T(128)} %bitcast.47, f32[]{:T(128)} %bitcast.46, f32[]{:T(128)} %bitcast.45, ...), kind=kLoop, calls=%fused_computation.268 | loop fusion | flops 3997696 | bytes 8388732 | tf_op jit(solution)/shard_map/add | solution.py:48
  114.2 22.0 %fusion.241 = (f32[]{:T(128)}, f32[128,512]{1,0:T(8,128)S(1)}) fusion(f32[]{:T(128)} %bitcast.83, f32[]{:T(128)} %bitcast.82, f32[]{:T(128)} %bitcast.81, f32[]{:T(128)} %bitcast.80, f32[]{:T(128)} %bitcast.79, f32[]{:T(128)} %bitcast.78, f32[]{:T(128)} %bitcast.77, f32[]{:T(128)} %bitcast.76, f32[]{:T(128)} %bitcast.75, f32[]{:T(128)} %bitcast.74, ...), kind=kLoop, calls=%fused_computation.490 | loop fusion | flops 4128767 | bytes 524416 | tf_op jit(solution)/shard_map/reduce_sum | solution.py:131
  136.2 10.5 %psum.7 = f32[]{:T(128)} all-reduce(f32[]{:T(128)} %get-tuple-element.96), channel_id=1, replica_groups=mesh['patch'=2,'sky'=4,'exp'=2,'band'=2] {'sky'}, use_global_device_ids=true, to_apply=%region_4.5 | all-reduce | flops 1 | bytes 8 | tf_op jit(solution)/shard_map/psum | solution.py:131
  148.1 0.9 bitcast_divide_fusion
  149.0 9.1 %reduce-scatter.2.cloned.1.call-done = f32[128,256]{1,0:T(8,128)} async-done(((f32[128,512]{1,0:T(8,128)}), f32[128,256]{1,0:T(8,128)}) %reduce-scatter.2.cloned.1.call-update) | async-done | bytes 131088 | tf_op jit(solution)/shard_map/reduce_scatter | solution.py:133
  (34 shorter events, 9.1 us)
Async XLA Ops:
  7.2 61.5 %all-gather.9.cloned.1.call-start = ((), (), s32[]{:S(2)}) async-start(), calls=%async_computation.3 | async-start | bytes 3145728 | tf_op jit(solution)/shard_map/all_gather | solution.py:30
  8.3 10.2 %collective-permute-start = (bf16[10,15,512]{2,1,0:T(8,128)(2,1)S(1)}, bf16[10,15,512]{2,1,0:T(8,128)(2,1)S(1)}, u32[]{:S(2)}, u32[]{:S(2)}) collective-permute-start(bf16[10,15,512]{2,1,0:T(8,128)(2,1)S(1)} %get-tuple-element.137), channel_id=1, source_target_pairs={{0,4},{4,8},{8,12},{1,5},{5,9},{9,13},{2,6},{6,10},{10,14},{3,7},{... | collective-permute-start | bytes 460808 | tf_op jit(solution)/shard_map/ppermute | solution.py:23
  13.2 7.6 %collective-permute-start.1 = (bf16[10,15,512]{2,1,0:T(8,128)(2,1)S(1)}, bf16[10,15,512]{2,1,0:T(8,128)(2,1)S(1)}, u32[]{:S(2)}, u32[]{:S(2)}) collective-permute-start(bf16[10,15,512]{2,1,0:T(8,128)(2,1)S(1)} %get-tuple-element.138), channel_id=1, source_target_pairs={{4,0},{8,4},{12,8},{5,1},{9,5},{13,9},{6,2},{10,6},{14,10},{7,3},{... | collective-permute-start | bytes 460808 | tf_op jit(solution)/shard_map/ppermute | solution.py:24
  22.6 10.6 %copy-start = (s32[1,10,128,512]{3,2,1,0:T(8,128)S(1)}, s32[1,10,128,512]{3,2,1,0:T(8,128)}, u32[]{:S(2)}) copy-start(s32[1,10,128,512]{3,2,1,0:T(8,128)} %param.9) | copy-start | bytes 7864324
  57.6 24.3 %all-gather.7.cloned.1.call-start = ((), (), s32[]{:S(2)}) async-start(), calls=%async_computation.2 | async-start | bytes 3145728 | tf_op jit(solution)/shard_map/all_gather | solution.py:30
  58.6 1.7 %copy-start.2 = (f32[1,31]{1,0:T(1,128)S(1)}, f32[1,31]{1,0:T(1,128)}, u32[]{:S(2)}) copy-start(f32[1,31]{1,0:T(1,128)} %param.14) | copy-start | bytes 376
  58.7 3.1 %copy-start.3 = (f32[1,31]{1,0:T(1,128)S(1)}, f32[1,31]{1,0:T(1,128)}, u32[]{:S(2)}) copy-start(f32[1,31]{1,0:T(1,128)} %param.15) | copy-start | bytes 376
  59.1 3.4 %copy-start.1 = (f32[128,512]{1,0:T(8,128)S(1)}, f32[128,512]{1,0:T(8,128)}, u32[]{:S(2)}) copy-start(f32[128,512]{1,0:T(8,128)} %get-tuple-element.23) | copy-start | bytes 786436
  60.3 97.8 %reduce-scatter.2.cloned.1.call-start = ((), (), s32[]{:S(2)}) async-start(), calls=%async_computation.1 | async-start | bytes 393216 | tf_op jit(solution)/shard_map/reduce_scatter | solution.py:133
  84.7 5.7 %collective-permute-start.2 = (bf16[15,512]{1,0:T(8,128)(2,1)S(1)}, bf16[15,512]{1,0:T(8,128)(2,1)S(1)}, u32[]{:S(2)}, u32[]{:S(2)}) collective-permute-start(bf16[15,512]{1,0:T(8,128)(2,1)S(1)} %get-tuple-element.139), channel_id=1, source_target_pairs={{0,4},{4,8},{8,12},{1,5},{5,9},{9,13},{2,6},{6,10},{10,14},{3,7},{... | collective-permute-start | bytes 46088 | tf_op jit(solution)/shard_map/ppermute | solution.py:23
  88.4 5.6 %collective-permute-start.3 = (bf16[15,512]{1,0:T(8,128)(2,1)S(1)}, bf16[15,512]{1,0:T(8,128)(2,1)S(1)}, u32[]{:S(2)}, u32[]{:S(2)}) collective-permute-start(bf16[15,512]{1,0:T(8,128)(2,1)S(1)} %get-tuple-element.140), channel_id=1, source_target_pairs={{4,0},{8,4},{12,8},{5,1},{9,5},{13,9},{6,2},{10,6},{14,10},{7,3},{... | collective-permute-start | bytes 46088 | tf_op jit(solution)/shard_map/ppermute | solution.py:24
Sparse Core Ops, SparseCore 0:
  57.7 10.9 all-gather.8
  70.2 11.6 all-gather.6
  148.2 9.7 reduce-scatter.1
where the time goes:
time: 166 us; the launch traced here: 165 us
  other arithmetic  86.7 us (52%)
  waiting for transfers between devices  29.6 us (18%)
  blocking collectives  15.4 us (9%)
  between operations  14.6 us (9%)
  starting transfers between devices  11.3 us (7%)
  local copies, waits for them, and re-layouts  7.06 us (4%)
    add x2, other arithmetic, rows_filter(): result + kernel[..., offset][..., None, None] * padded[..., offset:offset...  30.7 us
    reduce_sum x1, other arithmetic, on_device(): energy_sum = lax.psum(jnp.sum(energy), 'sky')  22 us
    reduce_sum x1, other arithmetic, visit_stats(): valid_count = jnp.sum(usable.astype(jnp.float32), axis=0)  21.9 us
    all_gather x2, waiting for transfers between devices, merged_2(): gathered = jax.tree.map(lambda a: lax.all_gather(a, axis), part)  14.6 us
    psum x1, blocking collectives, on_device(): energy_sum = lax.psum(jnp.sum(energy), 'sky')  10.5 us
    reduce_scatter x1, waiting for transfers between devices, on_device(): lax.psum_scatter(energy / variance, 'band', scatter_dimension=1, tiled=True)  9.11 us
    ppermute x2, starting transfers between devices, padded_2(): before = lax.ppermute(last, axis, up)  8.59 us
    ppermute x2, waiting for transfers between devices, padded_2(): after = lax.ppermute(first, axis, down)  5.89 us
  transfers between devices with their start and end apart: 7, of which 5 were waited for; matrix products, arithmetic and copies ran while one was open for 6% of the time, Pallas kernels for 0%

commit v1 on v0

v1 whole, which is shorter than its diff:
```python
import functools

import jax
import jax.numpy as jnp
from jax import lax
from jax.experimental import pallas as pl
from jax.experimental.pallas import tpu as pltpu
from jax.sharding import PartitionSpec as P

HALF = 15
REJECT = 4
TAPS = 31
EDGE = 16
LANES = 128
SENTINEL = 1e30
EPSILON = 1e-05
F32 = jnp.float32
BF16 = jnp.bfloat16
MIB = 1024 * 1024


def split2(value):
    high = value.astype(BF16)
    return high, (value - high.astype(F32)).astype(BF16)


def band_rows(taps, rows):
    return pltpu.roll(
        jnp.broadcast_to(pltpu.roll(taps, 1, 1), (rows, LANES)), 0, 1, stride=1, stride_axis=0
    )


def square_masks():
    row = lax.broadcasted_iota(jnp.int32, (LANES, LANES), 0)
    col = lax.broadcasted_iota(jnp.int32, (LANES, LANES), 1)
    return row, col


def col_matrix(taps):
    square = band_rows(taps, LANES).T
    row, col = square_masks()
    whole = jnp.concatenate(
        [jnp.where(row > col, square, 0.0), jnp.where(row < col, square, 0.0)], axis=0
    )
    return jnp.concatenate(split2(whole), axis=1)


def row_matrix(taps):
    square = band_rows(taps, LANES)
    row, col = square_masks()
    return jnp.concatenate(
        [jnp.where(col > row, square, 0.0), jnp.where(col < row, square, 0.0)], axis=1
    )


def col_conv(value, matrix):
    rows, cols = value.shape
    tiles = cols // LANES
    turned = pltpu.roll(value, EDGE, 1)
    first = turned[:, :LANES]
    lane = lax.broadcasted_iota(jnp.int32, (rows, LANES), 1)
    wide = jnp.concatenate(
        [jnp.where(lane < EDGE, 0.0, first), turned[:, LANES:], jnp.where(lane < EDGE, first, 0.0)],
        axis=1,
    )
    parts = [
        part[:, n * LANES : (n + 2) * LANES] for part in split2(wide) for n in range(tiles)
    ]
    product = jnp.dot(jnp.concatenate(parts, axis=0), matrix, preferred_element_type=F32)

    def piece(n, side):
        return product[n * rows : (n + 1) * rows, side * LANES : (side + 1) * LANES]

    return jnp.concatenate(
        [piece(n, 0) + (piece(n, 1) + piece(tiles + n, 0)) for n in range(tiles)], axis=1
    )


def exchange(values, i, j):
    values[i], values[j] = (
        jnp.maximum(values[i], values[j]),
        jnp.minimum(values[i], values[j]),
    )


def cleaned(values):
    for i, j in ((0, 2), (1, 3), (0, 1), (2, 3)):
        exchange(values, i, j)
    return values


def top_sorted(values):
    best = None
    for start in range(0, len(values), REJECT):
        group = list(values[start : start + REJECT])
        if len(group) == 4:
            for i, j in ((0, 1), (2, 3), (0, 2), (1, 3), (1, 2)):
                exchange(group, i, j)
        elif len(group) == 3:
            for i, j in ((0, 1), (1, 2), (0, 1)):
                exchange(group, i, j)
        elif len(group) == 2:
            exchange(group, 0, 1)
        if best is None:
            best = group
        else:
            for i, value in enumerate(group):
                best[REJECT - 1 - i] = jnp.maximum(best[REJECT - 1 - i], value)
            best = cleaned(best)
    return best


def sort_visits(values, lists):
    visits, rows, cols = values.shape
    width = 2 * LANES

    def body(step, carry):
        at = pl.ds(pl.multiple_of(step * 8, 8), 8)
        for start in range(0, cols, width):
            lanes = pl.ds(start, width)
            low = [values[v, at, lanes] for v in range(visits)]
            dead = [value == SENTINEL for value in low]
            upper = top_sorted([jnp.where(d, -SENTINEL, v) for d, v in zip(dead, low)])
            total, count = 0.0, 0.0
            for d, v in zip(dead, low):
                total = total + jnp.where(d, 0.0, v)
                count = count + jnp.where(d, 0.0, 1.0)
            lower = top_sorted([-v for v in low])
            for i in range(REJECT):
                lists[i, at, lanes] = upper[i]
                lists[REJECT + i, at, lanes] = lower[i]
            lists[2 * REJECT, at, lanes] = total
            lists[2 * REJECT + 1, at, lanes] = count
        return carry

    lax.fori_loop(0, rows // 8, body, 0)


def inner_kernel(
    groups, points, images, mask, row_taps, col_taps, lists, row_out, col_out, taps, values
):
    visit = pl.program_id(0)
    visits = pl.num_programs(0)
    rows = lists.shape[1]

    @pl.when(visit == 0)
    def _():
        taps[...] = jnp.zeros_like(taps)
        taps[0, 0 : row_taps.shape[1], 0:TAPS] = row_taps[0]
        taps[1, 0 : col_taps.shape[1], 0:TAPS] = col_taps[0]

    scale = points[0, groups[0, visit]]
    row_m = jnp.concatenate(split2(band_rows(taps[0, pl.ds(visit, 1), :], rows)), axis=0)
    col_m = col_matrix(taps[1, pl.ds(visit, 1), :] * scale)
    row_out[0] = row_m
    col_out[0] = col_m
    both = jnp.dot(row_m, images[0, 0], preferred_element_type=F32)
    result = col_conv(both[:rows] + both[rows:], col_m)
    usable = mask[0, 0, pl.ds(EDGE, rows), :] == 1
    values[visit] = jnp.where(usable, result, SENTINEL)

    @pl.when(visit == visits - 1)
    def _():
        sort_visits(values, lists)


def edge_kernel(
    above, below, first, last, first_mask, last_mask, row_m, col_m, lists, values
):
    visits = values.shape[0]
    inner = row_m.shape[1] // 2
    cols = values.shape[2]
    reach = 3 * EDGE
    for visit in range(visits):
        pieces = []
        for start in (0, inner):
            pieces += [row_m[visit, start : start + EDGE], row_m[visit, start + reach : start + reach + EDGE]]
        window = jnp.concatenate(
            [
                above[visit],
                first[0, visit],
                last[0, visit],
                below[visit],
                jnp.zeros((LANES - 2 * reach, cols), BF16),
            ],
            axis=0,
        )
        both = jnp.dot(jnp.concatenate(pieces, axis=0), window, preferred_element_type=F32)
        result = col_conv(both[: 2 * EDGE] + both[2 * EDGE :], col_m[visit])
        usable = jnp.concatenate([first_mask[0, visit], last_mask[0, visit]], axis=0) == 1
        values[visit] = jnp.where(usable, result, SENTINEL)
    sort_visits(values, lists)


def merge_kernel(mine, other, coadd):
    def body(step, carry):
        at = pl.ds(pl.multiple_of(step * 8, 8), 8)
        upper, lower = 0.0, 0.0
        for i in range(REJECT):
            j = REJECT - 1 - i
            upper = upper + jnp.maximum(mine[i, at, :], other[j, at, :])
            lower = lower + jnp.maximum(mine[REJECT + i, at, :], other[REJECT + j, at, :])
        total = mine[2 * REJECT, at, :] + other[2 * REJECT, at, :]
        count = mine[2 * REJECT + 1, at, :] + other[2 * REJECT + 1, at, :]
        coadd[at, :] = (total - upper + lower) / (count - 2 * REJECT)
        return carry

    lax.fori_loop(0, coadd.shape[0] // 8, body, 0)


def psf_kernel(place, above, below, edges, inner, row_taps, col_taps, coadd, pieces, taps):
    height, cols = coadd.shape[1:]
    bands, _, width = pieces.shape
    coadd[0, 0:EDGE] = edges[0:EDGE]
    coadd[0, EDGE : height - EDGE] = inner[...]
    coadd[0, height - EDGE : height] = edges[EDGE : 2 * EDGE]
    taps[...] = jnp.zeros_like(taps)
    taps[0:1, 0:TAPS] = row_taps[...]
    taps[8:9, 0:TAPS] = col_taps[...]
    row_h, row_l = split2(row_matrix(taps[0:1, :]))
    col_m = col_matrix(taps[8:9, :])
    mid_h, mid_l = split2(coadd[0])
    rest = jnp.zeros((2 * LANES - height - 2 * EDGE, cols), BF16)
    empty = jnp.zeros((EDGE, cols), BF16)
    high = jnp.concatenate([above[...], mid_h, below[...], rest], axis=0)
    low = jnp.concatenate([empty, mid_l, empty, rest], axis=0)
    both = jnp.dot(jnp.concatenate([row_h, row_l], axis=0), high, preferred_element_type=F32)
    both_low = jnp.dot(row_h, low, preferred_element_type=F32)
    filtered = col_conv(both[:height] + (both[height:] + both_low), col_m)
    energy = filtered * filtered
    part = jnp.sum(energy.reshape(height // 8, 8, cols), axis=0)
    part = sum(part[:, n * LANES : (n + 1) * LANES] for n in range(cols // LANES))
    own = place[0]
    for band in range(bands):
        slot = lax.rem(band - own + bands, bands)
        pieces[slot, 0:height, :] = energy[:, band * width : (band + 1) * width]
    for slot in range(bands):
        pieces[slot, height : height + 8, :] = jnp.concatenate([part] * (width // LANES), axis=1)


def final_kernel(pixels, pieces, sums, detection):
    height = detection.shape[0]
    total = 0.0
    for i in range(len(pieces)):
        variance = jnp.sum(sums[i, :, :]) / pixels + EPSILON
        total = total + pieces[i][...] / variance
    detection[...] = total


def vmem(shape, dtype=F32):
    return jax.ShapeDtypeStruct(shape, dtype)


VMEM = pl.BlockSpec(memory_space=pltpu.VMEM)
SMEM = pl.BlockSpec(memory_space=pltpu.SMEM)
PARAMS = pltpu.CompilerParams(vmem_limit_bytes=40 * MIB)


def shifted(value, axis, step):
    size = lax.axis_size(axis)
    pairs = [(i, i + step) for i in range(size) if 0 <= i + step < size]
    return lax.ppermute(value, axis, pairs)


def turned(value, axis, step):
    size = lax.axis_size(axis)
    return lax.ppermute(value, axis, [(i, (i + step) % size) for i in range(size)])


def on_device(images, valid_mask, row_kernel, col_kernel, exp_group, zero_point, psf_row, psf_col):
    _, visits, height, cols = images.shape
    inner = height - 2 * EDGE
    bands = lax.axis_size("band")
    strips = lax.axis_size("sky")
    above = shifted(images[0, :, height - EDGE :, :], "sky", 1)
    below = shifted(images[0, :, :EDGE, :], "sky", -1)

    inner_lists, row_m, col_m = pl.pallas_call(
        inner_kernel,
        grid=(visits,),
        in_specs=[
            SMEM,
            SMEM,
            pl.BlockSpec((1, 1, height, cols), lambda v: (0, v, 0, 0)),
            pl.BlockSpec((1, 1, height, cols), lambda v: (0, v, 0, 0)),
            pl.BlockSpec((1, visits, TAPS), lambda v: (0, 0, 0)),
            pl.BlockSpec((1, visits, TAPS), lambda v: (0, 0, 0)),
        ],
        out_specs=[
            pl.BlockSpec((2 * REJECT + 2, inner, cols), lambda v: (0, 0, 0)),
            pl.BlockSpec((1, 2 * inner, LANES), lambda v: (v, 0, 0)),
            pl.BlockSpec((1, 2 * LANES, 2 * LANES), lambda v: (v, 0, 0)),
        ],
        out_shape=[
            vmem((2 * REJECT + 2, inner, cols)),
            vmem((visits, 2 * inner, LANES), BF16),
            vmem((visits, 2 * LANES, 2 * LANES), BF16),
        ],
        scratch_shapes=[
            pltpu.VMEM((2, -(-visits // 8) * 8, LANES), F32),
            pltpu.VMEM((visits, inner, cols), F32),
        ],
        compiler_params=PARAMS,
        name="inner_visits",
    )(exp_group, zero_point, images, valid_mask, row_kernel, col_kernel)
    swap = [(0, 1), (1, 0)]
    inner_other = lax.ppermute(inner_lists, "exp", swap)

    last_block = height // (2 * EDGE) - 1
    last_mask_block = height // EDGE - 1
    edge_lists = pl.pallas_call(
        edge_kernel,
        grid=(1,),
        in_specs=[
            pl.BlockSpec((visits, EDGE, cols), lambda i: (0, 0, 0)),
            pl.BlockSpec((visits, EDGE, cols), lambda i: (0, 0, 0)),
            pl.BlockSpec((1, visits, 2 * EDGE, cols), lambda i: (0, 0, 0, 0)),
            pl.BlockSpec((1, visits, 2 * EDGE, cols), lambda i: (0, 0, last_block, 0)),
            pl.BlockSpec((1, visits, EDGE, cols), lambda i: (0, 0, 0, 0)),
            pl.BlockSpec((1, visits, EDGE, cols), lambda i: (0, 0, last_mask_block, 0)),
            pl.BlockSpec((visits, 2 * inner, LANES), lambda i: (0, 0, 0)),
            pl.BlockSpec((visits, 2 * LANES, 2 * LANES), lambda i: (0, 0, 0)),
        ],
        out_specs=pl.BlockSpec((2 * REJECT + 2, 2 * EDGE, cols), lambda i: (0, 0, 0)),
        out_shape=vmem((2 * REJECT + 2, 2 * EDGE, cols)),
        scratch_shapes=[pltpu.VMEM((visits, 2 * EDGE, cols), F32)],
        compiler_params=PARAMS,
        name="edge_visits",
    )(above, below, images, images, valid_mask, valid_mask, row_m, col_m)
    edge_other = lax.ppermute(edge_lists, "exp", swap)

    def merged(mine, other):
        rows = mine.shape[1]
        return pl.pallas_call(
            merge_kernel,
            in_specs=[VMEM, VMEM],
            out_specs=VMEM,
            out_shape=vmem((rows, cols)),
            compiler_params=PARAMS,
            name="merge",
        )(mine, other)

    edges = merged(edge_lists, edge_other)
    coadd_above = shifted(edges[EDGE:].astype(BF16), "sky", 1)
    coadd_below = shifted(edges[:EDGE].astype(BF16), "sky", -1)
    inner_coadd = merged(inner_lists, inner_other)

    width = cols // bands
    place = lax.axis_index("band").astype(jnp.int32)[None]
    coadd_image, pieces = pl.pallas_call(
        psf_kernel,
        in_specs=[SMEM] + [VMEM] * 6,
        out_specs=[VMEM, VMEM],
        out_shape=[vmem((1, height, cols)), vmem((bands, height + 8, width))],
        scratch_shapes=[pltpu.VMEM((16, LANES), F32)],
        compiler_params=PARAMS,
        name="psf",
    )(place, coadd_above, coadd_below, edges, inner_coadd, psf_row, psf_col)

    parts = [pieces[0]] + [turned(pieces[k], "band", k) for k in range(1, bands)]
    sums = jnp.stack([part[height:, :LANES] for part in parts])
    if strips <= 4:
        sums = sum((turned(sums, "sky", k) for k in range(1, strips)), sums)
    else:
        sums = lax.psum(sums, "sky")
    pixels = height * strips * cols
    detection = pl.pallas_call(
        lambda *refs: final_kernel(pixels, refs[:bands], refs[bands], refs[bands + 1]),
        in_specs=[VMEM] * (bands + 1),
        out_specs=VMEM,
        out_shape=vmem((height, width)),
        compiler_params=PARAMS,
        name="detection",
    )(*[part[:height] for part in parts], sums)
    return coadd_image, detection


def solution(mesh):
    placed = (
        P("band", "exp", ("patch", "sky"), None),
        P("band", "exp", ("patch", "sky"), None),
        P("band", "exp", None),
        P("band", "exp", None),
        P("band", "exp"),
        P("band", None),
        P("band", None),
        P("band", None),
    )
    return jax.shard_map(
        on_device,
        mesh=mesh,
        in_specs=placed,
        out_specs=(P("band", ("patch", "sky"), None), P(("patch", "sky"), "band")),
        check_vma=False,
    )
```

time: 166 us -> 54.8 us (0.33)
  other arithmetic: 86.7 us -> 0.02 us
  blocking collectives: 15.4 us -> 0 us
  Pallas kernels: 0 us -> 14 us
  between operations: 14.6 us -> 0.79 us
  waiting for transfers between devices: 29.6 us -> 16.7 us
  starting transfers between devices: 11.3 us -> 17 us
    reduce_sum x3 -> x0, other arithmetic: 44.7 us -> none  [the longest x1 22 us: on_device(): energy_sum = lax.psum(jnp.sum(energy), 'sky')]
    add x2 -> x1, other arithmetic: 30.7 us -> 0.01 us  [on_device(): sums = sum((turned(sums, 'sky', k) for k in range(1, strips)), sums)]
    all_gather x2 -> x0, waiting for transfers between devices: 14.6 us -> none  [merged_2(): gathered = jax.tree.map(lambda a: lax.all_gather(a, axis), part)]
    pallas_call x0 -> x6, Pallas kernels: none -> 14 us  [the longest x1 8.32 us: on_device(): pl.pallas_call(inner_kernel, grid=(visits,), in_specs=[SMEM, SMEM, pl.Blo...]
    ppermute x4 -> x10, waiting for transfers between devices: 5.9 us -> 16.7 us  [the longest x4 9.3 us: shifted(): return lax.ppermute(value, axis, pairs)]
    psum x1 -> x0, blocking collectives: 10.5 us -> none  [on_device(): energy_sum = lax.psum(jnp.sum(energy), 'sky')]
    reduce_scatter x1 -> x0, waiting for transfers between devices: 9.11 us -> none  [on_device(): lax.psum_scatter(energy / variance, 'band', scatter_dimension=1, tiled=True)]
    ppermute x4 -> x10, starting transfers between devices: 11.2 us -> 17 us  [the longest x4 10.6 us: shifted(): return lax.ppermute(value, axis, pairs)]
  transfers between devices with their start and end apart: 7 -> 10, of which waited for: 5 -> 7; matrix products, arithmetic and copies ran while one was open for 6% -> 0% of each run, Pallas kernels for 0% -> 7%
where the time goes in v1:
time: 54.8 us; the launch traced here: 54.4 us
  starting transfers between devices  17 us (31%)
  waiting for transfers between devices  16.7 us (30%)
  Pallas kernels  14 us (26%)
  local copies, waits for them, and re-layouts  5.83 us (11%)
  between operations  0.79 us (1%)
    ppermute x4, starting transfers between devices, shifted(): return lax.ppermute(value, axis, pairs)  10.6 us
    ppermute x4, waiting for transfers between devices, shifted(): return lax.ppermute(value, axis, pairs)  9.3 us
    pallas_call x1, Pallas kernels, on_device(): pl.pallas_call(inner_kernel, grid=(visits,), in_specs=[SMEM, SMEM, pl.Blo...  8.32 us
    ppermute x4, starting transfers between devices, turned(): lax.ppermute(value, axis, [(i, (i + step) % size) for i in range(size)])  5.87 us
    unnamed x16, local copies, waits for them, and re-layouts  5.76 us
    ppermute x4, waiting for transfers between devices, turned(): lax.ppermute(value, axis, [(i, (i + step) % size) for i in range(size)])  5.34 us
    ppermute x1, waiting for transfers between devices, on_device(): edge_other = lax.ppermute(edge_lists, 'exp', swap)  2.08 us
    pallas_call x2, Pallas kernels, merged(): pl.pallas_call(merge_kernel, in_specs=[VMEM, VMEM], out_specs=VMEM, out_s...  2 us
  transfers between devices with their start and end apart: 10, of which 7 were waited for; matrix products, arithmetic and copies ran while one was open for 0% of the time, Pallas kernels for 7%

profile of v1, /device:TPU:0, one launch (start us, length us, event | category | flops | bytes accessed | tf_op | source)
XLA Modules:
  0.0 54.4 jit_solution(15891617936976326585)
XLA Ops:
  0.6 0.7 %copy.10.row_taps = f32[1,10,31]{2,1,0:T(8,128)S(1)} copy(f32[1,10,31]{2,0,1:T(1,128)} %param.10) | data formatting | bytes 2480 | tf_op args[2]
  1.3 0.7 %copy.11.col_taps = f32[1,10,31]{2,1,0:T(8,128)S(1)} copy(f32[1,10,31]{2,0,1:T(1,128)} %param.11) | data formatting | bytes 2480 | tf_op args[3]
  2.0 1.7 %copy-done = s32[1,10,128,512]{3,2,1,0:T(8,128)S(1)} copy-done((s32[1,10,128,512]{3,2,1,0:T(8,128)S(1)}, s32[1,10,128,512]{3,2,1,0:T(8,128)}, u32[]{:S(2)}) %copy-start) | copy-done | bytes 2621464
  3.8 1.3 %copy-done.2 = bf16[1,10,128,512]{3,2,1,0:T(8,128)(2,1)S(1)} copy-done((bf16[1,10,128,512]{3,2,1,0:T(8,128)(2,1)S(1)}, bf16[1,10,128,512]{3,2,1,0:T(8,128)(2,1)}, u32[]{:S(2)}) %copy-start.2) | copy-done | bytes 1310744
  5.1 0.7 %copy-done.3 = s32[1,10]{1,0:T(1,128)S(1)} copy-done((s32[1,10]{1,0:T(1,128)S(1)}, s32[1,10]{1,0:T(1,128)}, u32[]{:S(2)}) %copy-start.3) | copy-done | bytes 64
  6.4 8.3 %inner_visits.1 = (f32[10,96,512]{2,1,0:T(8,128)S(1)}, bf16[10,192,128]{2,1,0:T(8,128)(2,1)S(1)}, bf16[10,256,256]{2,1,0:T(8,128)(2,1)S(1)}) custom-call(s32[1,10]{1,0:T(1,128)S(1)} %copy-done.3, f32[1,16]{1,0:T(1,128)S(1)} %copy-done.4, bf16[1,10,128,512]{3,2,1,0:T(8,128)(2,1)S(1)} %copy-done.2, s32[1,10,128,512]{3,2,1,0:T(8,128)S(1)} %copy-done, ...), custom_call_target="tpu_custom_call" | custom-call | tf_op jit(solution)/shard_map/inner_visits/pallas_call | solution.py:278
  15.3 4.5 %collective-permute-start = (bf16[10,16,512]{2,1,0:T(8,128)(2,1)S(1)}, bf16[10,16,512]{2,1,0:T(8,128)(2,1)S(1)}, u32[]{:S(2)}, u32[]{:S(2)}) collective-permute-start(bf16[10,16,512]{2,1,0:T(8,128)(2,1)S(1)} %get-tuple-element.13), channel_id=1, source_target_pairs={{0,4},{4,8},{8,12},{1,5},{5,9},{9,13},{2,6},{6,10},{10,14},{3,7},{... | collective-permute-start | bytes 491528 | tf_op jit(solution)/shard_map/ppermute | solution.py:262
  19.8 1.3 %collective-permute-start.1 = (bf16[10,16,512]{2,1,0:T(8,128)(2,1)S(1)}, bf16[10,16,512]{2,1,0:T(8,128)(2,1)S(1)}, u32[]{:S(2)}, u32[]{:S(2)}) collective-permute-start(bf16[10,16,512]{2,1,0:T(8,128)(2,1)S(1)} %get-tuple-element.12), channel_id=1, source_target_pairs={{4,0},{8,4},{12,8},{5,1},{9,5},{13,9},{6,2},{10,6},{14,10},{7,3},{... | collective-permute-start | bytes 491528 | tf_op jit(solution)/shard_map/ppermute | solution.py:262
  21.1 2.8 %collective-permute-done.above = bf16[10,16,512]{2,1,0:T(8,128)(2,1)S(1)} collective-permute-done((bf16[10,16,512]{2,1,0:T(8,128)(2,1)S(1)}, bf16[10,16,512]{2,1,0:T(8,128)(2,1)S(1)}, u32[]{:S(2)}, u32[]{:S(2)}) %collective-permute-start) | collective-permute-done | bytes 163872 | tf_op jit(solution)/shard_map/ppermute | solution.py:262
  23.9 4.1 %collective-permute-done.1.below = bf16[10,16,512]{2,1,0:T(8,128)(2,1)S(1)} collective-permute-done((bf16[10,16,512]{2,1,0:T(8,128)(2,1)S(1)}, bf16[10,16,512]{2,1,0:T(8,128)(2,1)S(1)}, u32[]{:S(2)}, u32[]{:S(2)}) %collective-permute-start.1) | collective-permute-done | bytes 163872 | tf_op jit(solution)/shard_map/ppermute | solution.py:262
  28.0 2.0 %edge_visits.1.mine = f32[10,32,512]{2,1,0:T(8,128)S(1)} custom-call(bf16[10,16,512]{2,1,0:T(8,128)(2,1)S(1)} %collective-permute-done.above, bf16[10,16,512]{2,1,0:T(8,128)(2,1)S(1)} %collective-permute-done.1.below, bf16[1,10,128,512]{3,2,1,0:T(8,128)(2,1)S(1)} %copy-done.2, bf16[1,10,128,512]{3,2,1,0:T(8,128)(2,1)S(1)} %copy-done.2, ...), custom_call_target="tpu_custom_call" | custom-call | tf_op jit(solution)/shard_map/edge_visits/pallas_call | solution.py:311
  30.0 2.1 %collective-permute-done.2.other = f32[10,32,512]{2,1,0:T(8,128)S(1)} collective-permute-done((f32[10,32,512]{2,1,0:T(8,128)S(1)}, f32[10,32,512]{2,1,0:T(8,128)S(1)}, u32[]{:S(2)}, u32[]{:S(2)}) %collective-permute-start.2) | collective-permute-done | bytes 655392 | tf_op jit(solution)/shard_map/ppermute | solution.py:330
  32.3 3.5 %collective-permute-start.3 = (bf16[16,512]{1,0:T(8,128)(2,1)S(1)}, bf16[16,512]{1,0:T(8,128)(2,1)S(1)}, u32[]{:S(2)}, u32[]{:S(2)}) collective-permute-start(bf16[16,512]{1,0:T(8,128)(2,1)S(1)} %get-tuple-element.17), channel_id=1, source_target_pairs={{0,4},{4,8},{8,12},{1,5},{5,9},{9,13},{2,6},{6,10},{10,14},{3,7},{... | collective-permute-start | bytes 49160 | tf_op jit(solution)/shard_map/ppermute | solution.py:262
  35.8 1.3 %collective-permute-start.4 = (bf16[16,512]{1,0:T(8,128)(2,1)S(1)}, bf16[16,512]{1,0:T(8,128)(2,1)S(1)}, u32[]{:S(2)}, u32[]{:S(2)}) collective-permute-start(bf16[16,512]{1,0:T(8,128)(2,1)S(1)} %get-tuple-element.16), channel_id=1, source_target_pairs={{4,0},{8,4},{12,8},{5,1},{9,5},{13,9},{6,2},{10,6},{14,10},{7,3},{... | collective-permute-start | bytes 49160 | tf_op jit(solution)/shard_map/ppermute | solution.py:262
  37.1 1.9 %merge.3.inner = f32[96,512]{1,0:T(8,128)S(1)} custom-call(f32[10,96,512]{2,1,0:T(8,128)S(1)} %get-tuple-element.9.mine, f32[10,96,512]{2,1,0:T(8,128)} %collective-permute-done.5.other), custom_call_target="tpu_custom_call" | custom-call | tf_op jit(solution)/shard_map/merge/pallas_call | solution.py:334
  39.0 2.4 %collective-permute-done.4.below = bf16[16,512]{1,0:T(8,128)(2,1)S(1)} collective-permute-done((bf16[16,512]{1,0:T(8,128)(2,1)S(1)}, bf16[16,512]{1,0:T(8,128)(2,1)S(1)}, u32[]{:S(2)}, u32[]{:S(2)}) %collective-permute-start.4) | collective-permute-done | bytes 16416 | tf_op jit(solution)/shard_map/ppermute | solution.py:262
  41.4 0.9 %psf.1 = (f32[1,128,512]{2,1,0:T(8,128)}, f32[2,136,256]{2,1,0:T(8,128)S(1)}) custom-call(s32[1]{0:T(128)} %bitcast.place, bf16[16,512]{1,0:T(8,128)(2,1)S(1)} %collective-permute-done.3.above, bf16[16,512]{1,0:T(8,128)(2,1)S(1)} %collective-permute-done.4.below, f32[32,512]{1,0:T(8,128)S(1)} %merge.2.edges, f32[96,512]{1,0:T(8,128)S(1)} %merge.3.inner, ...), custom_call_target="tpu_custom_call" | custom-call | tf_op jit(solution)/shard_map/psf/pallas_call | solution.py:350
  42.3 1.6 %collective-permute-start.6 = (f32[136,256]{1,0:T(8,128)S(1)}, f32[136,256]{1,0:T(8,128)S(1)}, u32[]{:S(2)}, u32[]{:S(2)}) collective-permute-start(f32[136,256]{1,0:T(8,128)S(1)} %get-tuple-element.15), channel_id=1, source_target_pairs={{0,1},{1,0},{2,3},{3,2},{4,5},{5,4},{6,7},{7,6},{8,9},{9,8},{10,11... | collective-permute-start | bytes 417800 | tf_op jit(solution)/shard_map/ppermute | solution.py:267
  43.9 3.6 %collective-permute-done.6 = f32[136,256]{1,0:T(8,128)S(1)} collective-permute-done((f32[136,256]{1,0:T(8,128)S(1)}, f32[136,256]{1,0:T(8,128)S(1)}, u32[]{:S(2)}, u32[]{:S(2)}) %collective-permute-start.6) | collective-permute-done | bytes 139296 | tf_op jit(solution)/shard_map/ppermute | solution.py:267
  47.4 1.6 %collective-permute-start.7 = (f32[2,8,128]{2,1,0:T(8,128)S(1)}, f32[2,8,128]{2,1,0:T(8,128)S(1)}, u32[]{:S(2)}, u32[]{:S(2)}) collective-permute-start(f32[2,8,128]{2,1,0:T(8,128)S(1)} %pad_maximum_fusion), channel_id=1, source_target_pairs={{0,4},{4,8},{8,12},{12,0},{1,5},{5,9},{9,13},{13,1},{2,6},{6,10},{... | collective-permute-start | bytes 24584 | tf_op jit(solution)/shard_map/ppermute | solution.py:267
  49.1 2.6 %collective-permute-start.9 = (f32[2,8,128]{2,1,0:T(8,128)S(1)}, f32[2,8,128]{2,1,0:T(8,128)S(1)}, u32[]{:S(2)}, u32[]{:S(2)}) collective-permute-start(f32[2,8,128]{2,1,0:T(8,128)S(1)} %pad_maximum_fusion), channel_id=1, source_target_pairs={{0,12},{4,0},{8,4},{12,8},{1,13},{5,1},{9,5},{13,9},{2,14},{6,2},{... | collective-permute-start | bytes 24584 | tf_op jit(solution)/shard_map/ppermute | solution.py:267
  51.8 1.1 %collective-permute-done.7 = f32[2,8,128]{2,1,0:T(8,128)S(1)} collective-permute-done((f32[2,8,128]{2,1,0:T(8,128)S(1)}, f32[2,8,128]{2,1,0:T(8,128)S(1)}, u32[]{:S(2)}, u32[]{:S(2)}) %collective-permute-start.7) | collective-permute-done | bytes 8224 | tf_op jit(solution)/shard_map/ppermute | solution.py:267
  52.9 0.7 %collective-permute-done.8 = f32[2,8,128]{2,1,0:T(8,128)S(1)} collective-permute-done((f32[2,8,128]{2,1,0:T(8,128)S(1)}, f32[2,8,128]{2,1,0:T(8,128)S(1)}, u32[]{:S(2)}, u32[]{:S(2)}) %collective-permute-start.8) | collective-permute-done | bytes 8224 | tf_op jit(solution)/shard_map/ppermute | solution.py:267
  53.6 0.8 %detection.1 = f32[128,256]{1,0:T(8,128)} custom-call(f32[128,256]{1,0:T(8,128)S(1)} %slice_bitcast_fusion.4.refs_0_, f32[128,256]{1,0:T(8,128)S(1)} %slice.49.refs_1_, f32[2,8,128]{2,1,0:T(8,128)S(1)} %add_add_fusion.refs_2_), custom_call_target="tpu_custom_call" | custom-call | tf_op jit(solution)/shard_map/detection/pallas_call | solution.py:367
  (28 shorter events, 1.6 us)
Async XLA Ops:
  2.0 1.7 %copy-start = (s32[1,10,128,512]{3,2,1,0:T(8,128)S(1)}, s32[1,10,128,512]{3,2,1,0:T(8,128)}, u32[]{:S(2)}) copy-start(s32[1,10,128,512]{3,2,1,0:T(8,128)} %last_mask.1) | copy-start | bytes 7864324
  3.8 1.3 %copy-start.2 = (bf16[1,10,128,512]{3,2,1,0:T(8,128)(2,1)S(1)}, bf16[1,10,128,512]{3,2,1,0:T(8,128)(2,1)}, u32[]{:S(2)}) copy-start(bf16[1,10,128,512]{3,2,1,0:T(8,128)(2,1)} %last.1) | copy-start | bytes 3932164
  5.1 0.7 %copy-start.3 = (s32[1,10]{1,0:T(1,128)S(1)}, s32[1,10]{1,0:T(1,128)}, u32[]{:S(2)}) copy-start(s32[1,10]{1,0:T(1,128)} %groups.1) | copy-start | bytes 124
  5.7 0.7 %copy-start.4 = (f32[1,16]{1,0:T(1,128)S(1)}, f32[1,16]{1,0:T(1,128)}, u32[]{:S(2)}) copy-start(f32[1,16]{1,0:T(1,128)} %points.1) | copy-start | bytes 196
  6.4 21.6 %copy-start.1 = (s32[1,10,128,512]{3,2,1,0:T(8,128)S(1)}, s32[1,10,128,512]{3,2,1,0:T(8,128)}, u32[]{:S(2)}) copy-start(s32[1,10,128,512]{3,2,1,0:T(8,128)} %last_mask.1) | copy-start | bytes 7864324
  14.7 22.4 %collective-permute-start.5 = (f32[10,96,512]{2,1,0:T(8,128)S(1)}, f32[10,96,512]{2,1,0:T(8,128)}, u32[]{:S(2)}, u32[]{:S(2)}) collective-permute-start(f32[10,96,512]{2,1,0:T(8,128)S(1)} %get-tuple-element.9.mine), channel_id=1, source_target_pairs={{0,2},{2,0},{1,3},{3,1},{4,6},{6,4},{5,7},{7,5},{8,10},{10,8},{9,1... | collective-permute-start | bytes 5898248 | tf_op jit(solution)/shard_map/ppermute | solution.py:307
  15.3 8.6 %collective-permute-start = (bf16[10,16,512]{2,1,0:T(8,128)(2,1)S(1)}, bf16[10,16,512]{2,1,0:T(8,128)(2,1)S(1)}, u32[]{:S(2)}, u32[]{:S(2)}) collective-permute-start(bf16[10,16,512]{2,1,0:T(8,128)(2,1)S(1)} %get-tuple-element.13), channel_id=1, source_target_pairs={{0,4},{4,8},{8,12},{1,5},{5,9},{9,13},{2,6},{6,10},{10,14},{3,7},{... | collective-permute-start | bytes 491528 | tf_op jit(solution)/shard_map/ppermute | solution.py:262
  19.8 8.2 %collective-permute-start.1 = (bf16[10,16,512]{2,1,0:T(8,128)(2,1)S(1)}, bf16[10,16,512]{2,1,0:T(8,128)(2,1)S(1)}, u32[]{:S(2)}, u32[]{:S(2)}) collective-permute-start(bf16[10,16,512]{2,1,0:T(8,128)(2,1)S(1)} %get-tuple-element.12), channel_id=1, source_target_pairs={{4,0},{8,4},{12,8},{5,1},{9,5},{13,9},{6,2},{10,6},{14,10},{7,3},{... | collective-permute-start | bytes 491528 | tf_op jit(solution)/shard_map/ppermute | solution.py:262
  30.0 2.2 %collective-permute-start.2 = (f32[10,32,512]{2,1,0:T(8,128)S(1)}, f32[10,32,512]{2,1,0:T(8,128)S(1)}, u32[]{:S(2)}, u32[]{:S(2)}) collective-permute-start(f32[10,32,512]{2,1,0:T(8,128)S(1)} %edge_visits.1.mine), channel_id=1, source_target_pairs={{0,2},{2,0},{1,3},{3,1},{4,6},{6,4},{5,7},{7,5},{8,10},{10,8},{9,1... | collective-permute-start | bytes 1966088 | tf_op jit(solution)/shard_map/ppermute | solution.py:330
  32.3 6.7 %collective-permute-start.3 = (bf16[16,512]{1,0:T(8,128)(2,1)S(1)}, bf16[16,512]{1,0:T(8,128)(2,1)S(1)}, u32[]{:S(2)}, u32[]{:S(2)}) collective-permute-start(bf16[16,512]{1,0:T(8,128)(2,1)S(1)} %get-tuple-element.17), channel_id=1, source_target_pairs={{0,4},{4,8},{8,12},{1,5},{5,9},{9,13},{2,6},{6,10},{10,14},{3,7},{... | collective-permute-start | bytes 49160 | tf_op jit(solution)/shard_map/ppermute | solution.py:262
  35.8 5.6 %collective-permute-start.4 = (bf16[16,512]{1,0:T(8,128)(2,1)S(1)}, bf16[16,512]{1,0:T(8,128)(2,1)S(1)}, u32[]{:S(2)}, u32[]{:S(2)}) collective-permute-start(bf16[16,512]{1,0:T(8,128)(2,1)S(1)} %get-tuple-element.16), channel_id=1, source_target_pairs={{4,0},{8,4},{12,8},{5,1},{9,5},{13,9},{6,2},{10,6},{14,10},{7,3},{... | collective-permute-start | bytes 49160 | tf_op jit(solution)/shard_map/ppermute | solution.py:262
  37.1 4.3 %copy-start.5 = (f32[1,31]{1,0:T(1,128)S(1)}, f32[1,31]{1,0:T(1,128)}, u32[]{:S(2)}) copy-start(f32[1,31]{1,0:T(1,128)} %row_taps.2) | copy-start | bytes 376
  37.1 4.3 %copy-start.6 = (f32[1,31]{1,0:T(1,128)S(1)}, f32[1,31]{1,0:T(1,128)}, u32[]{:S(2)}) copy-start(f32[1,31]{1,0:T(1,128)} %col_taps.2) | copy-start | bytes 376
  42.3 5.1 %collective-permute-start.6 = (f32[136,256]{1,0:T(8,128)S(1)}, f32[136,256]{1,0:T(8,128)S(1)}, u32[]{:S(2)}, u32[]{:S(2)}) collective-permute-start(f32[136,256]{1,0:T(8,128)S(1)} %get-tuple-element.15), channel_id=1, source_target_pairs={{0,1},{1,0},{2,3},{3,2},{4,5},{5,4},{6,7},{7,6},{8,9},{9,8},{10,11... | collective-permute-start | bytes 417800 | tf_op jit(solution)/shard_map/ppermute | solution.py:267
  47.4 5.4 %collective-permute-start.7 = (f32[2,8,128]{2,1,0:T(8,128)S(1)}, f32[2,8,128]{2,1,0:T(8,128)S(1)}, u32[]{:S(2)}, u32[]{:S(2)}) collective-permute-start(f32[2,8,128]{2,1,0:T(8,128)S(1)} %pad_maximum_fusion), channel_id=1, source_target_pairs={{0,4},{4,8},{8,12},{12,0},{1,5},{5,9},{9,13},{13,1},{2,6},{6,10},{... | collective-permute-start | bytes 24584 | tf_op jit(solution)/shard_map/ppermute | solution.py:267
  49.0 4.5 %collective-permute-start.8 = (f32[2,8,128]{2,1,0:T(8,128)S(1)}, f32[2,8,128]{2,1,0:T(8,128)S(1)}, u32[]{:S(2)}, u32[]{:S(2)}) collective-permute-start(f32[2,8,128]{2,1,0:T(8,128)S(1)} %pad_maximum_fusion), channel_id=1, source_target_pairs={{0,8},{4,12},{8,0},{12,4},{1,9},{5,13},{9,1},{13,5},{2,10},{6,14},... | collective-permute-start | bytes 24584 | tf_op jit(solution)/shard_map/ppermute | solution.py:267
  49.1 4.4 %collective-permute-start.9 = (f32[2,8,128]{2,1,0:T(8,128)S(1)}, f32[2,8,128]{2,1,0:T(8,128)S(1)}, u32[]{:S(2)}, u32[]{:S(2)}) collective-permute-start(f32[2,8,128]{2,1,0:T(8,128)S(1)} %pad_maximum_fusion), channel_id=1, source_target_pairs={{0,12},{4,0},{8,4},{12,8},{1,13},{5,1},{9,5},{13,9},{2,14},{6,2},{... | collective-permute-start | bytes 24584 | tf_op jit(solution)/shard_map/ppermute | solution.py:267

commit v2 on v1

--- a/solution.py
+++ b/solution.py
@@ -17,6 +17,7 @@
 F32 = jnp.float32
 BF16 = jnp.bfloat16
 MIB = 1024 * 1024
+UNROLL = 2
 
 
 def split2(value):
@@ -28,6 +29,11 @@
     return pltpu.roll(
         jnp.broadcast_to(pltpu.roll(taps, 1, 1), (rows, LANES)), 0, 1, stride=1, stride_axis=0
     )
+
+
+def around_matrix(taps):
+    base = pltpu.roll(taps, LANES - HALF, 1)
+    return pltpu.roll(jnp.broadcast_to(base, (LANES, LANES)), 0, 1, stride=1, stride_axis=0)
 
 
 def square_masks():
@@ -136,59 +142,113 @@
     lax.fori_loop(0, rows // 8, body, 0)
 
 
+def at_ends(above, below):
+    strip = lax.axis_index("sky")
+    top, bottom = strip == 0, strip == lax.axis_size("sky") - 1
+    return (
+        jnp.where(top, jnp.zeros_like(above), above),
+        jnp.where(bottom, jnp.zeros_like(below), below),
+    )
+
+
 def inner_kernel(
-    groups, points, images, mask, row_taps, col_taps, lists, row_out, col_out, taps, values
+    groups_h,
+    points_h,
+    images_h,
+    mask_h,
+    row_taps_h,
+    col_taps_h,
+    lists,
+    part,
+    edge_m,
+    col_m,
+    edge_mask,
+    groups,
+    points,
+    row_taps,
+    col_taps,
+    images,
+    mask,
+    taps,
+    row_m,
+    values,
+    small_sems,
+    image_sems,
+    mask_sems,
 ):
-    visit = pl.program_id(0)
-    visits = pl.num_programs(0)
-    rows = lists.shape[1]
-
-    @pl.when(visit == 0)
-    def _():
-        taps[...] = jnp.zeros_like(taps)
-        taps[0, 0 : row_taps.shape[1], 0:TAPS] = row_taps[0]
-        taps[1, 0 : col_taps.shape[1], 0:TAPS] = col_taps[0]
-
-    scale = points[0, groups[0, visit]]
-    row_m = jnp.concatenate(split2(band_rows(taps[0, pl.ds(visit, 1), :], rows)), axis=0)
-    col_m = col_matrix(taps[1, pl.ds(visit, 1), :] * scale)
-    row_out[0] = row_m
-    col_out[0] = col_m
-    both = jnp.dot(row_m, images[0, 0], preferred_element_type=F32)
-    result = col_conv(both[:rows] + both[rows:], col_m)
-    usable = mask[0, 0, pl.ds(EDGE, rows), :] == 1
-    values[visit] = jnp.where(usable, result, SENTINEL)
-
-    @pl.when(visit == visits - 1)
-    def _():
-        sort_visits(values, lists)
-
-
-def edge_kernel(
-    above, below, first, last, first_mask, last_mask, row_m, col_m, lists, values
-):
-    visits = values.shape[0]
-    inner = row_m.shape[1] // 2
-    cols = values.shape[2]
-    reach = 3 * EDGE
+    visits, height, _ = images.shape
+    small = [
+        pltpu.make_async_copy(source, target, small_sems.at[i])
+        for i, (source, target) in enumerate(
+            ((groups_h, groups), (points_h, points), (row_taps_h, row_taps), (col_taps_h, col_taps))
+        )
+    ]
+
+    def image_copy(v):
+        return pltpu.make_async_copy(images_h.at[0, v], images.at[v], image_sems.at[v])
+
+    def mask_copy(v):
+        return pltpu.make_async_copy(mask_h.at[0, v], mask.at[v], mask_sems.at[v])
+
+    for copy in small:
+        copy.start()
+    for v in range(visits):
+        image_copy(v).start()
+        mask_copy(v).start()
+    taps[...] = jnp.zeros_like(taps)
+    row, col = square_masks()
+    near = jnp.abs(row - col) <= HALF
+    for copy in small:
+        copy.wait()
+    def build(v, slot):
+        taps[slot : slot + 1, 0:TAPS] = row_taps[v]
+        taps[slot + 8 : slot + 9, 0:TAPS] = col_taps[v]
+        scale = points[0, groups[0, v]]
+        square = around_matrix(taps[slot : slot + 1, :])
+        row_m[v] = jnp.concatenate(split2(jnp.where(near, square, 0.0)), axis=0)
+        far = jnp.where(near, 0.0, square)
+        far = jnp.concatenate([far[:EDGE], far[height - EDGE :]], axis=0)
+        edge_m[v] = jnp.concatenate(split2(far), axis=0)
+        col_m[v] = col_matrix(taps[slot + 8 : slot + 9, :] * scale)
+
+    def convolve(v, slot):
+        both = jnp.dot(row_m[v], images[v], preferred_element_type=F32)
+        smeared = both[:height] + both[height:]
+        part[v, 0:EDGE] = smeared[:EDGE]
+        part[v, EDGE : 2 * EDGE] = smeared[height - EDGE :]
+        result = col_conv(smeared[EDGE : height - EDGE], col_m[v])
+        values[v] = jnp.where(mask[v, EDGE : height - EDGE] == 1, result, SENTINEL)
+        edge_mask[v, 0:EDGE] = mask[v, 0:EDGE]
+        edge_mask[v, EDGE : 2 * EDGE] = mask[v, height - EDGE :]
+
+    def each(step_of, at_once):
+        at_once = at_once if visits % at_once == 0 else 1
+
+        def body(step, carry):
+            for i in range(at_once):
+                step_of(step * at_once + i, 16 * i)
+            return carry
+
+        lax.fori_loop(0, visits // at_once, body, 0)
+
+    each(build, UNROLL)
+    for v in range(visits):
+        image_copy(v).wait()
+        mask_copy(v).wait()
+    each(convolve, UNROLL)
+    sort_visits(values, lists)
+
+
+def edge_kernel(above, below, part, edge_m, col_m, edge_mask, lists, values):
+    visits, _, cols = values.shape
     for visit in range(visits):
-        pieces = []
-        for start in (0, inner):
-            pieces += [row_m[visit, start : start + EDGE], row_m[visit, start + reach : start + reach + EDGE]]
+        before, after = at_ends(above[visit], below[visit])
         window = jnp.concatenate(
-            [
-                above[visit],
-                first[0, visit],
-                last[0, visit],
-                below[visit],
-                jnp.zeros((LANES - 2 * reach, cols), BF16),
-            ],
-            axis=0,
+            [after, jnp.zeros((LANES - 2 * EDGE, cols), BF16), before], axis=0
         )
-        both = jnp.dot(jnp.concatenate(pieces, axis=0), window, preferred_element_type=F32)
-        result = col_conv(both[: 2 * EDGE] + both[2 * EDGE :], col_m[visit])
-        usable = jnp.concatenate([first_mask[0, visit], last_mask[0, visit]], axis=0) == 1
-        values[visit] = jnp.where(usable, result, SENTINEL)
+        both = jnp.dot(edge_m[visit], window, preferred_element_type=F32)
+        result = col_conv(part[visit] + (both[: 2 * EDGE] + both[2 * EDGE :]), col_m[visit])
+        values[visit] = jnp.where(edge_mask[visit] == 1, result, SENTINEL)
     sort_visits(values, lists)
 
 
@@ -208,7 +268,7 @@
     lax.fori_loop(0, coadd.shape[0] // 8, body, 0)
 
 
-def psf_kernel(place, above, below, edges, inner, row_taps, col_taps, coadd, pieces, taps):
+def psf_kernel(above, below, edges, inner, row_taps, col_taps, coadd, pieces, taps):
     height, cols = coadd.shape[1:]
     bands, _, width = pieces.shape
     coadd[0, 0:EDGE] = edges[0:EDGE]
@@ -222,7 +282,8 @@
     mid_h, mid_l = split2(coadd[0])
     rest = jnp.zeros((2 * LANES - height - 2 * EDGE, cols), BF16)
     empty = jnp.zeros((EDGE, cols), BF16)
-    high = jnp.concatenate([above[...], mid_h, below[...], rest], axis=0)
+    before, after = at_ends(above[...], below[...])
+    high = jnp.concatenate([before, mid_h, after, rest], axis=0)
     low = jnp.concatenate([empty, mid_l, empty, rest], axis=0)
     both = jnp.dot(jnp.concatenate([row_h, row_l], axis=0), high, preferred_element_type=F32)
     both_low = jnp.dot(row_h, low, preferred_element_type=F32)
@@ -230,7 +291,7 @@
     energy = filtered * filtered
     part = jnp.sum(energy.reshape(height // 8, 8, cols), axis=0)
     part = sum(part[:, n * LANES : (n + 1) * LANES] for n in range(cols // LANES))
-    own = place[0]
+    own = lax.axis_index("band")
     for band in range(bands):
         slot = lax.rem(band - own + bands, bands)
         pieces[slot, 0:height, :] = energy[:, band * width : (band + 1) * width]
@@ -253,13 +314,8 @@
 
 VMEM = pl.BlockSpec(memory_space=pltpu.VMEM)
 SMEM = pl.BlockSpec(memory_space=pltpu.SMEM)
-PARAMS = pltpu.CompilerParams(vmem_limit_bytes=40 * MIB)
-
-
-def shifted(value, axis, step):
-    size = lax.axis_size(axis)
-    pairs = [(i, i + step) for i in range(size) if 0 <= i + step < size]
-    return lax.ppermute(value, axis, pairs)
+HBM = pl.BlockSpec(memory_space=pltpu.HBM)
+PARAMS = pltpu.CompilerParams(vmem_limit_bytes=20 * MIB)
 
 
 def turned(value, axis, step):
@@ -272,61 +328,68 @@
     inner = height - 2 * EDGE
     bands = lax.axis_size("band")
     strips = lax.axis_size("sky")
-    above = shifted(images[0, :, height - EDGE :, :], "sky", 1)
-    below = shifted(images[0, :, :EDGE, :], "sky", -1)
-
-    inner_lists, row_m, col_m = pl.pallas_call(
+    above = turned(images[0, :, height - EDGE :, :], "sky", 1)
+    below = turned(images[0, :, :EDGE, :], "sky", -1)
+
+    lists = 2 * REJECT + 2
+    inner_lists, part, edge_m, col_m, edge_mask = pl.pallas_call(
         inner_kernel,
-        grid=(visits,),
-        in_specs=[
-            SMEM,
-            SMEM,
-            pl.BlockSpec((1, 1, height, cols), lambda v: (0, v, 0, 0)),
-            pl.BlockSpec((1, 1, height, cols), lambda v: (0, v, 0, 0)),
-            pl.BlockSpec((1, visits, TAPS), lambda v: (0, 0, 0)),
-            pl.BlockSpec((1, visits, TAPS), lambda v: (0, 0, 0)),
-        ],
-        out_specs=[
-            pl.BlockSpec((2 * REJECT + 2, inner, cols), lambda v: (0, 0, 0)),
-            pl.BlockSpec((1, 2 * inner, LANES), lambda v: (v, 0, 0)),
-            pl.BlockSpec((1, 2 * LANES, 2 * LANES), lambda v: (v, 0, 0)),
-        ],
+        in_specs=[HBM] * 6,
+        out_specs=[VMEM] * 5,
         out_shape=[
-            vmem((2 * REJECT + 2, inner, cols)),
-            vmem((visits, 2 * inner, LANES), BF16),
+            vmem((lists, inner, cols)),
+            vmem((visits, 2 * EDGE, cols)),
+            vmem((visits, 4 * EDGE, LANES), BF16),
             vmem((visits, 2 * LANES, 2 * LANES), BF16),
+            vmem((visits, 2 * EDGE, cols), jnp.int32),
         ],
         scratch_shapes=[
-            pltpu.VMEM((2, -(-visits // 8) * 8, LANES), F32),
+            pltpu.SMEM((1, visits), jnp.int32),
+            pltpu.SMEM(zero_point.shape, F32),
+            pltpu.VMEM((visits, 1, TAPS), F32),
+            pltpu.VMEM((visits, 1, TAPS), F32),
+            pltpu.VMEM((visits, height, cols), BF16),
+            pltpu.VMEM((visits, height, cols), jnp.int32),
+            pltpu.VMEM((16 * UNROLL, LANES), F32),
+            pltpu.VMEM((visits, 2 * LANES, LANES), BF16),
             pltpu.VMEM((visits, inner, cols), F32),
+            pltpu.SemaphoreType.DMA((4,)),
+            pltpu.SemaphoreType.DMA((visits,)),
+            pltpu.SemaphoreType.DMA((visits,)),
         ],
         compiler_params=PARAMS,
+        cost_estimate=pl.CostEstimate(
+            flops=visits * height * cols * 4096,
+            bytes_accessed=visits * height * cols * 6,
+            transcendentals=0,
+        ),
         name="inner_visits",
-    )(exp_group, zero_point, images, valid_mask, row_kernel, col_kernel)
+    )(
+        *(
+            pltpu.with_memory_space_constraint(value, pltpu.HBM)
+            for value in (
+                exp_group,
+                zero_point,
+                images,
+                valid_mask,
+                row_kernel.transpose(1, 0, 2),
+                col_kernel.transpose(1, 0, 2),
+            )
+        )
+    )
     swap = [(0, 1), (1, 0)]
-    inner_other = lax.ppermute(inner_lists, "exp", swap)
-
-    last_block = height // (2 * EDGE) - 1
-    last_mask_block = height // EDGE - 1
+    held, _, _ = lax.optimization_barrier((inner_lists, above, below))
+    inner_other = lax.ppermute(held, "exp", swap)
+
     edge_lists = pl.pallas_call(
         edge_kernel,
-        grid=(1,),
-        in_specs=[
-            pl.BlockSpec((visits, EDGE, cols), lambda i: (0, 0, 0)),
-            pl.BlockSpec((visits, EDGE, cols), lambda i: (0, 0, 0)),
-            pl.BlockSpec((1, visits, 2 * EDGE, cols), lambda i: (0, 0, 0, 0)),
-            pl.BlockSpec((1, visits, 2 * EDGE, cols), lambda i: (0, 0, last_block, 0)),
-            pl.BlockSpec((1, visits, EDGE, cols), lambda i: (0, 0, 0, 0)),
-            pl.BlockSpec((1, visits, EDGE, cols), lambda i: (0, 0, last_mask_block, 0)),
-            pl.BlockSpec((visits, 2 * inner, LANES), lambda i: (0, 0, 0)),
-            pl.BlockSpec((visits, 2 * LANES, 2 * LANES), lambda i: (0, 0, 0)),
-        ],
-        out_specs=pl.BlockSpec((2 * REJECT + 2, 2 * EDGE, cols), lambda i: (0, 0, 0)),
-        out_shape=vmem((2 * REJECT + 2, 2 * EDGE, cols)),
+        in_specs=[VMEM] * 6,
+        out_specs=VMEM,
+        out_shape=vmem((lists, 2 * EDGE, cols)),
         scratch_shapes=[pltpu.VMEM((visits, 2 * EDGE, cols), F32)],
         compiler_params=PARAMS,
         name="edge_visits",
-    )(above, below, images, images, valid_mask, valid_mask, row_m, col_m)
+    )(above, below, part, edge_m, col_m, edge_mask)
     edge_other = lax.ppermute(edge_lists, "exp", swap)
 
     def merged(mine, other):
@@ -341,21 +404,20 @@
         )(mine, other)
 
     edges = merged(edge_lists, edge_other)
-    coadd_above = shifted(edges[EDGE:].astype(BF16), "sky", 1)
-    coadd_below = shifted(edges[:EDGE].astype(BF16), "sky", -1)
+    coadd_above = turned(edges[EDGE:].astype(BF16), "sky", 1)
+    coadd_below = turned(edges[:EDGE].astype(BF16), "sky", -1)
     inner_coadd = merged(inner_lists, inner_other)
 
     width = cols // bands
-    place = lax.axis_index("band").astype(jnp.int32)[None]
     coadd_image, pieces = pl.pallas_call(
         psf_kernel,
-        in_specs=[SMEM] + [VMEM] * 6,
+        in_specs=[VMEM] * 6,
         out_specs=[VMEM, VMEM],
         out_shape=[vmem((1, height, cols)), vmem((bands, height + 8, width))],
         scratch_shapes=[pltpu.VMEM((16, LANES), F32)],
         compiler_params=PARAMS,
         name="psf",
-    )(place, coadd_above, coadd_below, edges, inner_coadd, psf_row, psf_col)
+    )(coadd_above, coadd_below, edges, inner_coadd, psf_row, psf_col)
 
     parts = [pieces[0]] + [turned(pieces[k], "band", k) for k in range(1, bands)]
     sums = jnp.stack([part[height:, :LANES] for part in parts])

time: 54.8 us -> 42.6 us (0.78)
  local copies, waits for them, and re-layouts: 5.83 us -> 1.08 us
  starting transfers between devices: 17 us -> 13.2 us
  Pallas kernels: 14 us -> 12.2 us
  waiting for transfers between devices: 16.7 us -> 15.2 us
    ppermute x5 -> x1, starting transfers between devices: 11.1 us -> 0.07 us  [on_device(): inner_other = lax.ppermute(held, 'exp', swap)]
    ppermute x5 -> x1, waiting for transfers between devices: 9.3 us -> 0.01 us  [on_device(): inner_other = lax.ppermute(held, 'exp', swap)]
    ppermute x4 -> x8, waiting for transfers between devices: 5.34 us -> 12.8 us  [turned(): lax.ppermute(value, axis, [(i, (i + step) % size) for i in range(size)])]
    ppermute x4 -> x8, starting transfers between devices: 5.87 us -> 12.6 us  [turned(): lax.ppermute(value, axis, [(i, (i + step) % size) for i in range(size)])]
    unnamed x16 -> x4, local copies, waits for them, and re-layouts: 5.76 us -> 0.01 us
    pallas_call x2, Pallas kernels: 2 us -> 0.46 us  [merged(): pl.pallas_call(merge_kernel, in_specs=[VMEM, VMEM], out_specs=VMEM, out_s...]
    squeeze x1, local copies, waits for them, and re-layouts: 0.02 us -> 1.03 us  [on_device(): below = turned(images[0, :, :EDGE, :], 'sky', -1)]
  transfers between devices with their start and end apart: 10 -> 10, of which waited for: 7 -> 6; matrix products, arithmetic and copies ran while one was open for 0% -> 0% of each run, Pallas kernels for 7% -> 25%
where the time goes in v2:
time: 42.6 us; the launch traced here: 42.4 us
  waiting for transfers between devices  15.2 us (36%)
  starting transfers between devices  13.2 us (31%)
  Pallas kernels  12.2 us (29%)
  local copies, waits for them, and re-layouts  1.08 us (3%)
  between operations  0.73 us (2%)
    ppermute x8, waiting for transfers between devices, turned(): lax.ppermute(value, axis, [(i, (i + step) % size) for i in range(size)])  12.8 us
    ppermute x8, starting transfers between devices, turned(): lax.ppermute(value, axis, [(i, (i + step) % size) for i in range(size)])  12.6 us
    pallas_call x1, Pallas kernels, on_device(): pl.pallas_call(inner_kernel, in_specs=[HBM] * 6, out_specs=[VMEM] * 5, ou...  8.04 us
    ppermute x1, waiting for transfers between devices, on_device(): edge_other = lax.ppermute(edge_lists, 'exp', swap)  2.35 us
    pallas_call x1, Pallas kernels, on_device(): pl.pallas_call(edge_kernel, in_specs=[VMEM] * 6, out_specs=VMEM, out_shap...  1.99 us
    squeeze x1, local copies, waits for them, and re-layouts, on_device(): below = turned(images[0, :, :EDGE, :], 'sky', -1)  1.03 us
    pallas_call x1, Pallas kernels, on_device(): pl.pallas_call(psf_kernel, in_specs=[VMEM] * 6, out_specs=[VMEM, VMEM], o...  0.89 us
  transfers between devices with their start and end apart: 10, of which 6 were waited for; matrix products, arithmetic and copies ran while one was open for 0% of the time, Pallas kernels for 25%

profile of v2, /device:TPU:0, one launch (start us, length us, event | category | flops | bytes accessed | tf_op | source)
XLA Modules:
  0.0 42.4 jit_solution(9934458568521676942)
XLA Ops:
  0.6 1.0 %slice_bitcast_fusion = (bf16[10,16,512]{2,1,0:T(8,128)(2,1)S(1)}, bf16[10,16,512]{2,1,0:T(8,128)(2,1)S(1)}) fusion(bf16[1,10,128,512]{3,2,1,0:T(8,128)(2,1)} %images_h.1), kind=kLoop, calls=%fused_computation | loop fusion | bytes 655360 | tf_op jit(solution)/shard_map/squeeze | solution.py:332
  1.7 5.1 %collective-permute-start.1 = (bf16[10,16,512]{2,1,0:T(8,128)(2,1)S(1)}, bf16[10,16,512]{2,1,0:T(8,128)(2,1)S(1)}, u32[]{:S(2)}, u32[]{:S(2)}) collective-permute-start(bf16[10,16,512]{2,1,0:T(8,128)(2,1)S(1)} %get-tuple-element.18), channel_id=1, source_target_pairs={{0,12},{4,0},{8,4},{12,8},{1,13},{5,1},{9,5},{13,9},{2,14},{6,2},{... | collective-permute-start | bytes 491528 | tf_op jit(solution)/shard_map/ppermute | solution.py:323
  6.8 0.0 collective-permute-start
  6.8 8.0 %inner_visits.1 = (f32[10,96,512]{2,1,0:T(8,128)S(1)}, f32[10,32,512]{2,1,0:T(8,128)S(1)}, bf16[10,64,128]{2,1,0:T(8,128)(2,1)S(1)}, bf16[10,256,256]{2,1,0:T(8,128)(2,1)S(1)}, s32[10,32,512]{2,1,0:T(8,128)S(1)}) custom-call(s32[1,10]{1,0:T(1,128)} %groups_h.1, f32[1,16]{1,0:T(1,128)} %points_h.1, bf16[1,10,128,512]{3,2,1,0:T(8,128)(2,1)} %images_h.1, ...), custom_call_target="tpu_custom_call" | custom-call | flops 2684354560 | bytes 3932160 | tf_op jit(solution)/shard_map/inner_visits/pallas_call | solution.py:335
  14.8 0.0 collective-permute-done.1.below
  14.8 0.0 collective-permute-done.above
  14.8 0.1 collective-permute-start.5
  14.9 2.0 %edge_visits.1.mine = f32[10,32,512]{2,1,0:T(8,128)S(1)} custom-call(bf16[10,16,512]{2,1,0:T(8,128)(2,1)S(1)} %collective-permute-done.above, bf16[10,16,512]{2,1,0:T(8,128)(2,1)S(1)} %collective-permute-done.1.below, f32[10,32,512]{2,1,0:T(8,128)S(1)} %get-tuple-element.10.part, bf16[10,64,128]{2,1,0:T(8,128)(2,1)S(1)} %get-tuple-element.11.edge_m, ...), custom_call_target="tpu_custom_call" | custom-call | tf_op jit(solution)/shard_map/edge_visits/pallas_call | solution.py:384
  16.9 0.6 %collective-permute-start.2 = (f32[10,32,512]{2,1,0:T(8,128)S(1)}, f32[10,32,512]{2,1,0:T(8,128)S(1)}, u32[]{:S(2)}, u32[]{:S(2)}) collective-permute-start(f32[10,32,512]{2,1,0:T(8,128)S(1)} %edge_visits.1.mine), channel_id=1, source_target_pairs={{0,2},{2,0},{1,3},{3,1},{4,6},{6,4},{5,7},{7,5},{8,10},{10,8},{9,1... | collective-permute-start | bytes 1966088 | tf_op jit(solution)/shard_map/ppermute | solution.py:393
  17.5 2.3 %collective-permute-done.2.other = f32[10,32,512]{2,1,0:T(8,128)S(1)} collective-permute-done((f32[10,32,512]{2,1,0:T(8,128)S(1)}, f32[10,32,512]{2,1,0:T(8,128)S(1)}, u32[]{:S(2)}, u32[]{:S(2)}) %collective-permute-start.2) | collective-permute-done | bytes 655392 | tf_op jit(solution)/shard_map/ppermute | solution.py:393
  19.8 0.1 merge.2.edges
  19.9 3.9 %collective-permute-start.4 = (bf16[16,512]{1,0:T(8,128)(2,1)S(1)}, bf16[16,512]{1,0:T(8,128)(2,1)S(1)}, u32[]{:S(2)}, u32[]{:S(2)}) collective-permute-start(bf16[16,512]{1,0:T(8,128)(2,1)S(1)} %get-tuple-element.22), channel_id=1, source_target_pairs={{0,12},{4,0},{8,4},{12,8},{1,13},{5,1},{9,5},{13,9},{2,14},{6,2},{... | collective-permute-start | bytes 49160 | tf_op jit(solution)/shard_map/ppermute | solution.py:323
  23.8 0.3 merge.3.inner
  24.2 1.1 %collective-permute-done.4.below = bf16[16,512]{1,0:T(8,128)(2,1)S(1)} collective-permute-done((bf16[16,512]{1,0:T(8,128)(2,1)S(1)}, bf16[16,512]{1,0:T(8,128)(2,1)S(1)}, u32[]{:S(2)}, u32[]{:S(2)}) %collective-permute-start.4) | collective-permute-done | bytes 16416 | tf_op jit(solution)/shard_map/ppermute | solution.py:323
  25.3 4.1 %collective-permute-done.3.above = bf16[16,512]{1,0:T(8,128)(2,1)S(1)} collective-permute-done((bf16[16,512]{1,0:T(8,128)(2,1)S(1)}, bf16[16,512]{1,0:T(8,128)(2,1)S(1)}, u32[]{:S(2)}, u32[]{:S(2)}) %collective-permute-start.3) | collective-permute-done | bytes 16416 | tf_op jit(solution)/shard_map/ppermute | solution.py:323
  29.4 0.9 %psf.1 = (f32[1,128,512]{2,1,0:T(8,128)}, f32[2,136,256]{2,1,0:T(8,128)S(1)}) custom-call(bf16[16,512]{1,0:T(8,128)(2,1)S(1)} %collective-permute-done.3.above, bf16[16,512]{1,0:T(8,128)(2,1)S(1)} %collective-permute-done.4.below, f32[32,512]{1,0:T(8,128)S(1)} %merge.2.edges, f32[96,512]{1,0:T(8,128)S(1)} %merge.3.inner, f32[1,31]{1,0:T(1,128)S(1)} %copy-done, ...), custom_call_target="tpu_custom_call" | custom-call | tf_op jit(solution)/shard_map/psf/pallas_call | solution.py:412
  30.3 1.6 %collective-permute-start.6 = (f32[136,256]{1,0:T(8,128)S(1)}, f32[136,256]{1,0:T(8,128)S(1)}, u32[]{:S(2)}, u32[]{:S(2)}) collective-permute-start(f32[136,256]{1,0:T(8,128)S(1)} %get-tuple-element.21), channel_id=1, source_target_pairs={{0,1},{1,0},{2,3},{3,2},{4,5},{5,4},{6,7},{7,6},{8,9},{9,8},{10,11... | collective-permute-start | bytes 417800 | tf_op jit(solution)/shard_map/ppermute | solution.py:323
  31.8 3.6 %collective-permute-done.6 = f32[136,256]{1,0:T(8,128)S(1)} collective-permute-done((f32[136,256]{1,0:T(8,128)S(1)}, f32[136,256]{1,0:T(8,128)S(1)}, u32[]{:S(2)}, u32[]{:S(2)}) %collective-permute-start.6) | collective-permute-done | bytes 139296 | tf_op jit(solution)/shard_map/ppermute | solution.py:323
  35.4 0.0 collective-permute-start.8
  35.4 0.7 %collective-permute-start.9 = (f32[2,8,128]{2,1,0:T(8,128)S(1)}, f32[2,8,128]{2,1,0:T(8,128)S(1)}, u32[]{:S(2)}, u32[]{:S(2)}) collective-permute-start(f32[2,8,128]{2,1,0:T(8,128)S(1)} %pad_maximum_fusion), channel_id=1, source_target_pairs={{0,12},{4,0},{8,4},{12,8},{1,13},{5,1},{9,5},{13,9},{2,14},{6,2},{... | collective-permute-start | bytes 24584 | tf_op jit(solution)/shard_map/ppermute | solution.py:323
  36.1 1.3 %collective-permute-start.7 = (f32[2,8,128]{2,1,0:T(8,128)S(1)}, f32[2,8,128]{2,1,0:T(8,128)S(1)}, u32[]{:S(2)}, u32[]{:S(2)}) collective-permute-start(f32[2,8,128]{2,1,0:T(8,128)S(1)} %pad_maximum_fusion), channel_id=1, source_target_pairs={{0,4},{4,8},{8,12},{12,0},{1,5},{5,9},{9,13},{13,1},{2,6},{6,10},{... | collective-permute-start | bytes 24584 | tf_op jit(solution)/shard_map/ppermute | solution.py:323
  37.5 2.4 %collective-permute-done.8 = f32[2,8,128]{2,1,0:T(8,128)S(1)} collective-permute-done((f32[2,8,128]{2,1,0:T(8,128)S(1)}, f32[2,8,128]{2,1,0:T(8,128)S(1)}, u32[]{:S(2)}, u32[]{:S(2)}) %collective-permute-start.8) | collective-permute-done | bytes 8224 | tf_op jit(solution)/shard_map/ppermute | solution.py:323
  40.0 1.6 %collective-permute-done.7 = f32[2,8,128]{2,1,0:T(8,128)S(1)} collective-permute-done((f32[2,8,128]{2,1,0:T(8,128)S(1)}, f32[2,8,128]{2,1,0:T(8,128)S(1)}, u32[]{:S(2)}, u32[]{:S(2)}) %collective-permute-start.7) | collective-permute-done | bytes 8224 | tf_op jit(solution)/shard_map/ppermute | solution.py:323
  41.6 0.8 %detection.1 = f32[128,256]{1,0:T(8,128)} custom-call(f32[128,256]{1,0:T(8,128)S(1)} %slice_bitcast_fusion.4.refs_0_, f32[128,256]{1,0:T(8,128)S(1)} %slice.49.refs_1_, f32[2,8,128]{2,1,0:T(8,128)S(1)} %add_add_fusion.refs_2_), custom_call_target="tpu_custom_call" | custom-call | tf_op jit(solution)/shard_map/detection/pallas_call | solution.py:429
  (16 shorter events, 0.1 us)
Async XLA Ops:
  1.7 13.2 %collective-permute-start.1 = (bf16[10,16,512]{2,1,0:T(8,128)(2,1)S(1)}, bf16[10,16,512]{2,1,0:T(8,128)(2,1)S(1)}, u32[]{:S(2)}, u32[]{:S(2)}) collective-permute-start(bf16[10,16,512]{2,1,0:T(8,128)(2,1)S(1)} %get-tuple-element.18), channel_id=1, source_target_pairs={{0,12},{4,0},{8,4},{12,8},{1,13},{5,1},{9,5},{13,9},{2,14},{6,2},{... | collective-permute-start | bytes 491528 | tf_op jit(solution)/shard_map/ppermute | solution.py:323
  6.8 8.1 %collective-permute-start = (bf16[10,16,512]{2,1,0:T(8,128)(2,1)S(1)}, bf16[10,16,512]{2,1,0:T(8,128)(2,1)S(1)}, u32[]{:S(2)}, u32[]{:S(2)}) collective-permute-start(bf16[10,16,512]{2,1,0:T(8,128)(2,1)S(1)} %get-tuple-element.19), channel_id=1, source_target_pairs={{0,4},{4,8},{8,12},{12,0},{1,5},{5,9},{9,13},{13,1},{2,6},{6,10},{... | collective-permute-start | bytes 491528 | tf_op jit(solution)/shard_map/ppermute | solution.py:323
  14.8 9.0 %collective-permute-start.5 = (f32[10,96,512]{2,1,0:T(8,128)S(1)}, f32[10,96,512]{2,1,0:T(8,128)S(1)}, u32[]{:S(2)}, u32[]{:S(2)}) collective-permute-start(f32[10,96,512]{2,1,0:T(8,128)S(1)} %get-tuple-element.15.mine), channel_id=1, source_target_pairs={{0,2},{2,0},{1,3},{3,1},{4,6},{6,4},{5,7},{7,5},{8,10},{10,8},{9,1... | collective-permute-start | bytes 5898248 | tf_op jit(solution)/shard_map/ppermute | solution.py:382
  16.9 2.9 %collective-permute-start.2 = (f32[10,32,512]{2,1,0:T(8,128)S(1)}, f32[10,32,512]{2,1,0:T(8,128)S(1)}, u32[]{:S(2)}, u32[]{:S(2)}) collective-permute-start(f32[10,32,512]{2,1,0:T(8,128)S(1)} %edge_visits.1.mine), channel_id=1, source_target_pairs={{0,2},{2,0},{1,3},{3,1},{4,6},{6,4},{5,7},{7,5},{8,10},{10,8},{9,1... | collective-permute-start | bytes 1966088 | tf_op jit(solution)/shard_map/ppermute | solution.py:393
  19.9 5.3 %collective-permute-start.4 = (bf16[16,512]{1,0:T(8,128)(2,1)S(1)}, bf16[16,512]{1,0:T(8,128)(2,1)S(1)}, u32[]{:S(2)}, u32[]{:S(2)}) collective-permute-start(bf16[16,512]{1,0:T(8,128)(2,1)S(1)} %get-tuple-element.22), channel_id=1, source_target_pairs={{0,12},{4,0},{8,4},{12,8},{1,13},{5,1},{9,5},{13,9},{2,14},{6,2},{... | collective-permute-start | bytes 49160 | tf_op jit(solution)/shard_map/ppermute | solution.py:323
  23.8 5.5 %copy-start = (f32[1,31]{1,0:T(1,128)S(1)}, f32[1,31]{1,0:T(1,128)}, u32[]{:S(2)}) copy-start(f32[1,31]{1,0:T(1,128)} %row_taps.1) | copy-start | bytes 376
  23.8 5.5 %copy-start.1 = (f32[1,31]{1,0:T(1,128)S(1)}, f32[1,31]{1,0:T(1,128)}, u32[]{:S(2)}) copy-start(f32[1,31]{1,0:T(1,128)} %col_taps.1) | copy-start | bytes 376
  23.8 5.5 %collective-permute-start.3 = (bf16[16,512]{1,0:T(8,128)(2,1)S(1)}, bf16[16,512]{1,0:T(8,128)(2,1)S(1)}, u32[]{:S(2)}, u32[]{:S(2)}) collective-permute-start(bf16[16,512]{1,0:T(8,128)(2,1)S(1)} %get-tuple-element.23), channel_id=1, source_target_pairs={{0,4},{4,8},{8,12},{12,0},{1,5},{5,9},{9,13},{13,1},{2,6},{6,10},{... | collective-permute-start | bytes 49160 | tf_op jit(solution)/shard_map/ppermute | solution.py:323
  30.3 5.1 %collective-permute-start.6 = (f32[136,256]{1,0:T(8,128)S(1)}, f32[136,256]{1,0:T(8,128)S(1)}, u32[]{:S(2)}, u32[]{:S(2)}) collective-permute-start(f32[136,256]{1,0:T(8,128)S(1)} %get-tuple-element.21), channel_id=1, source_target_pairs={{0,1},{1,0},{2,3},{3,2},{4,5},{5,4},{6,7},{7,6},{8,9},{9,8},{10,11... | collective-permute-start | bytes 417800 | tf_op jit(solution)/shard_map/ppermute | solution.py:323
  35.4 4.5 %collective-permute-start.8 = (f32[2,8,128]{2,1,0:T(8,128)S(1)}, f32[2,8,128]{2,1,0:T(8,128)S(1)}, u32[]{:S(2)}, u32[]{:S(2)}) collective-permute-start(f32[2,8,128]{2,1,0:T(8,128)S(1)} %pad_maximum_fusion), channel_id=1, source_target_pairs={{0,8},{4,12},{8,0},{12,4},{1,9},{5,13},{9,1},{13,5},{2,10},{6,14},... | collective-permute-start | bytes 24584 | tf_op jit(solution)/shard_map/ppermute | solution.py:323
  35.4 4.5 %collective-permute-start.9 = (f32[2,8,128]{2,1,0:T(8,128)S(1)}, f32[2,8,128]{2,1,0:T(8,128)S(1)}, u32[]{:S(2)}, u32[]{:S(2)}) collective-permute-start(f32[2,8,128]{2,1,0:T(8,128)S(1)} %pad_maximum_fusion), channel_id=1, source_target_pairs={{0,12},{4,0},{8,4},{12,8},{1,13},{5,1},{9,5},{13,9},{2,14},{6,2},{... | collective-permute-start | bytes 24584 | tf_op jit(solution)/shard_map/ppermute | solution.py:323
  36.1 5.4 %collective-permute-start.7 = (f32[2,8,128]{2,1,0:T(8,128)S(1)}, f32[2,8,128]{2,1,0:T(8,128)S(1)}, u32[]{:S(2)}, u32[]{:S(2)}) collective-permute-start(f32[2,8,128]{2,1,0:T(8,128)S(1)} %pad_maximum_fusion), channel_id=1, source_target_pairs={{0,4},{4,8},{8,12},{12,0},{1,5},{5,9},{9,13},{13,1},{2,6},{6,10},{... | collective-permute-start | bytes 24584 | tf_op jit(solution)/shard_map/ppermute | solution.py:323

commit v3 on v2

--- a/solution.py
+++ b/solution.py
@@ -43,12 +43,7 @@
 
 
 def col_matrix(taps):
-    square = band_rows(taps, LANES).T
-    row, col = square_masks()
-    whole = jnp.concatenate(
-        [jnp.where(row > col, square, 0.0), jnp.where(row < col, square, 0.0)], axis=0
-    )
-    return jnp.concatenate(split2(whole), axis=1)
+    return jnp.concatenate(split2(row_matrix(taps)), axis=0)
 
 
 def row_matrix(taps):
@@ -72,7 +67,12 @@
     parts = [
         part[:, n * LANES : (n + 2) * LANES] for part in split2(wide) for n in range(tiles)
     ]
-    product = jnp.dot(jnp.concatenate(parts, axis=0), matrix, preferred_element_type=F32)
+    product = lax.dot_general(
+        jnp.concatenate(parts, axis=0),
+        matrix,
+        (((1,), (1,)), ((), ())),
+        preferred_element_type=F32,
+    )
 
     def piece(n, side):
         return product[n * rows : (n + 1) * rows, side * LANES : (side + 1) * LANES]
@@ -142,9 +142,11 @@
     lax.fori_loop(0, rows // 8, body, 0)
 
 
-def at_ends(above, below):
+def at_ends(first, second):
     strip = lax.axis_index("sky")
+    even = lax.rem(strip, 2) == 0
     top, bottom = strip == 0, strip == lax.axis_size("sky") - 1
+    above, below = jnp.where(even, second, first), jnp.where(even, first, second)
     return (
         jnp.where(top, jnp.zeros_like(above), above),
         jnp.where(bottom, jnp.zeros_like(below), below),
@@ -184,17 +186,21 @@
         )
     ]
 
-    def image_copy(v):
-        return pltpu.make_async_copy(images_h.at[0, v], images.at[v], image_sems.at[v])
-
-    def mask_copy(v):
-        return pltpu.make_async_copy(mask_h.at[0, v], mask.at[v], mask_sems.at[v])
+    middle = visits // 2 // UNROLL * UNROLL if visits % UNROLL == 0 else visits // 2
+
+    def image_copy(i):
+        at = pl.ds(0, middle) if i == 0 else pl.ds(middle, visits - middle)
+        return pltpu.make_async_copy(images_h.at[0, at], images.at[at], image_sems.at[i])
+
+    def mask_copy(i):
+        at = pl.ds(0, middle) if i == 0 else pl.ds(middle, visits - middle)
+        return pltpu.make_async_copy(mask_h.at[0, at], mask.at[at], mask_sems.at[i])
 
     for copy in small:
         copy.start()
-    for v in range(visits):
-        image_copy(v).start()
-        mask_copy(v).start()
+    for i in range(2):
+        image_copy(i).start()
+        mask_copy(i).start()
     taps[...] = jnp.zeros_like(taps)
     row, col = square_masks()
     near = jnp.abs(row - col) <= HALF
@@ -205,15 +211,17 @@
         taps[slot + 8 : slot + 9, 0:TAPS] = col_taps[v]
         scale = points[0, groups[0, v]]
         square = around_matrix(taps[slot : slot + 1, :])
-        row_m[v] = jnp.concatenate(split2(jnp.where(near, square, 0.0)), axis=0)
+        row_m[v] = jnp.concatenate(split2(jnp.where(near, square, 0.0)), axis=1)
         far = jnp.where(near, 0.0, square)
         far = jnp.concatenate([far[:EDGE], far[height - EDGE :]], axis=0)
         edge_m[v] = jnp.concatenate(split2(far), axis=0)
         col_m[v] = col_matrix(taps[slot + 8 : slot + 9, :] * scale)
 
     def convolve(v, slot):
-        both = jnp.dot(row_m[v], images[v], preferred_element_type=F32)
-        smeared = both[:height] + both[height:]
+        image = images[v]
+        smeared = jnp.dot(
+            row_m[v], jnp.concatenate([image, image], axis=0), preferred_element_type=F32
+        )
         part[v, 0:EDGE] = smeared[:EDGE]
         part[v, EDGE : 2 * EDGE] = smeared[height - EDGE :]
         result = col_conv(smeared[EDGE : height - EDGE], col_m[v])
@@ -221,28 +229,30 @@
         edge_mask[v, 0:EDGE] = mask[v, 0:EDGE]
         edge_mask[v, EDGE : 2 * EDGE] = mask[v, height - EDGE :]
 
-    def each(step_of, at_once):
-        at_once = at_once if visits % at_once == 0 else 1
-
-        def body(step, carry):
-            for i in range(at_once):
-                step_of(step * at_once + i, 16 * i)
-            return carry
-
-        lax.fori_loop(0, visits // at_once, body, 0)
-
-    each(build, UNROLL)
-    for v in range(visits):
-        image_copy(v).wait()
-        mask_copy(v).wait()
-    each(convolve, UNROLL)
+    at_once = UNROLL if visits % UNROLL == 0 else 1
+    steps = visits // at_once
+
+    def body(step, carry):
+        for i in range(at_once):
+            convolve(step * at_once + i, 16 * i)
+        for i in range(at_once):
+            build(lax.rem((step + 1) * at_once + i, visits), 16 * i)
+        return carry
+
+    for i in range(at_once):
+        build(i, 16 * i)
+    turn = middle // at_once
+    for part_of, first, last in ((0, 0, turn), (1, turn, steps)):
+        image_copy(part_of).wait()
+        mask_copy(part_of).wait()
+        lax.fori_loop(first, last, body, 0)
     sort_visits(values, lists)
 
 
-def edge_kernel(above, below, part, edge_m, col_m, edge_mask, lists, values):
+def edge_kernel(first, second, part, edge_m, col_m, edge_mask, lists, values):
     visits, _, cols = values.shape
     for visit in range(visits):
-        before, after = at_ends(above[visit], below[visit])
+        before, after = at_ends(first[visit], second[visit])
         window = jnp.concatenate(
             [after, jnp.zeros((LANES - 2 * EDGE, cols), BF16), before], axis=0
         )
@@ -268,9 +278,19 @@
     lax.fori_loop(0, coadd.shape[0] // 8, body, 0)
 
 
-def psf_kernel(above, below, edges, inner, row_taps, col_taps, coadd, pieces, taps):
+def edge_merge_kernel(mine, other, coadd, send_first, send_second):
+    merge_kernel(mine, other, coadd)
+    even = lax.rem(lax.axis_index("sky"), 2) == 0
+    top, bottom = coadd[0:EDGE], coadd[EDGE : 2 * EDGE]
+    send_first[...] = jnp.where(even, bottom, top).astype(BF16)
+    send_second[...] = jnp.where(even, top, bottom).astype(BF16)
+
+
+def psf_kernel(first, second, edges, inner, row_taps, col_taps, coadd, keep, send, taps, scratch):
     height, cols = coadd.shape[1:]
-    bands, _, width = pieces.shape
+    width = keep.shape[1]
+    others, half, _ = send.shape
+    half = half - 8
     coadd[0, 0:EDGE] = edges[0:EDGE]
     coadd[0, EDGE : height - EDGE] = inner[...]
     coadd[0, height - EDGE : height] = edges[EDGE : 2 * EDGE]
@@ -282,7 +302,7 @@
     mid_h, mid_l = split2(coadd[0])
     rest = jnp.zeros((2 * LANES - height - 2 * EDGE, cols), BF16)
     empty = jnp.zeros((EDGE, cols), BF16)
-    before, after = at_ends(above[...], below[...])
+    before, after = at_ends(first[...], second[...])
     high = jnp.concatenate([before, mid_h, after, rest], axis=0)
     low = jnp.concatenate([empty, mid_l, empty, rest], axis=0)
     both = jnp.dot(jnp.concatenate([row_h, row_l], axis=0), high, preferred_element_type=F32)
@@ -291,21 +311,33 @@
     energy = filtered * filtered
     part = jnp.sum(energy.reshape(height // 8, 8, cols), axis=0)
     part = sum(part[:, n * LANES : (n + 1) * LANES] for n in range(cols // LANES))
+    scratch[...] = energy
     own = lax.axis_index("band")
-    for band in range(bands):
-        slot = lax.rem(band - own + bands, bands)
-        pieces[slot, 0:height, :] = energy[:, band * width : (band + 1) * width]
-    for slot in range(bands):
-        pieces[slot, height : height + 8, :] = jnp.concatenate([part] * (width // LANES), axis=1)
-
-
-def final_kernel(pixels, pieces, sums, detection):
+    start = pl.multiple_of(lax.axis_index("exp") * half, half)
+    keep[0:height] = scratch[:, pl.ds(pl.multiple_of(own * width, width), width)]
+    for k in range(others):
+        band = lax.rem(own + k + 1, others + 1)
+        lanes = pl.ds(pl.multiple_of(band * width, width), width)
+        send[k, 0:half] = scratch[pl.ds(start, half), lanes]
+    for n in range(width // LANES):
+        keep[height : height + 8, n * LANES : (n + 1) * LANES] = part
+        for k in range(others):
+            send[k, half : half + 8, n * LANES : (n + 1) * LANES] = part
+
+
+def final_kernel(pixels, keep, *refs):
+    others = (len(refs) - 2) // 2
+    mine, theirs, sums, detection = refs[:others], refs[others : 2 * others], refs[-2], refs[-1]
     height = detection.shape[0]
-    total = 0.0
-    for i in range(len(pieces)):
-        variance = jnp.sum(sums[i, :, :]) / pixels + EPSILON
-        total = total + pieces[i][...] / variance
-    detection[...] = total
+    half = height // 2
+    scales = [1.0 / (jnp.sum(sums[i]) / pixels + EPSILON) for i in range(others + 1)]
+    core = lax.axis_index("exp")
+    for place, parts in ((core, mine), (1 - core, theirs)):
+        at = pl.ds(pl.multiple_of(place * half, half), half)
+        total = keep[at, :] * scales[0]
+        for i in range(others):
+            total = total + parts[i][0:half, :] * scales[i + 1]
+        detection[at, :] = total
 
 
 def vmem(shape, dtype=F32):
@@ -316,6 +348,23 @@
 SMEM = pl.BlockSpec(memory_space=pltpu.SMEM)
 HBM = pl.BlockSpec(memory_space=pltpu.HBM)
 PARAMS = pltpu.CompilerParams(vmem_limit_bytes=20 * MIB)
+
+
+def paired(value, start):
+    strips, cores = lax.axis_size("sky"), lax.axis_size("exp")
+    partner = {}
+    for i in range(start, strips - 1, 2):
+        partner[i], partner[i + 1] = i + 1, i
+    pairs = []
+    for strip in range(strips):
+        for core in range(cores):
+            to = (partner[strip], core) if strip in partner else (strip, cores - 1 - core)
+            pairs.append((strip * cores + core, to[0] * cores + to[1]))
+    return lax.ppermute(value, ("sky", "exp"), pairs)
+
+
+def flipped(value, axis, bits):
+    return lax.ppermute(value, axis, [(i, i ^ bits) for i in range(lax.axis_size(axis))])
 
 
 def turned(value, axis, step):
@@ -328,8 +377,10 @@
     inner = height - 2 * EDGE
     bands = lax.axis_size("band")
     strips = lax.axis_size("sky")
-    above = turned(images[0, :, height - EDGE :, :], "sky", 1)
-    below = turned(images[0, :, :EDGE, :], "sky", -1)
+    even = lax.rem(lax.axis_index("sky"), 2) == 0
+    far = jnp.where(even, height - EDGE, 0)
+    first = paired(lax.dynamic_slice_in_dim(images[0], far, EDGE, 1), 0)
+    second = paired(lax.dynamic_slice_in_dim(images[0], height - EDGE - far, EDGE, 1), 1)
 
     lists = 2 * REJECT + 2
     inner_lists, part, edge_m, col_m, edge_mask = pl.pallas_call(
@@ -351,11 +402,11 @@
             pltpu.VMEM((visits, height, cols), BF16),
             pltpu.VMEM((visits, height, cols), jnp.int32),
             pltpu.VMEM((16 * UNROLL, LANES), F32),
-            pltpu.VMEM((visits, 2 * LANES, LANES), BF16),
+            pltpu.VMEM((visits, LANES, 2 * LANES), BF16),
             pltpu.VMEM((visits, inner, cols), F32),
             pltpu.SemaphoreType.DMA((4,)),
-            pltpu.SemaphoreType.DMA((visits,)),
-            pltpu.SemaphoreType.DMA((visits,)),
+            pltpu.SemaphoreType.DMA((2,)),
+            pltpu.SemaphoreType.DMA((2,)),
         ],
         compiler_params=PARAMS,
         cost_estimate=pl.CostEstimate(
@@ -378,9 +429,6 @@
         )
     )
     swap = [(0, 1), (1, 0)]
-    held, _, _ = lax.optimization_barrier((inner_lists, above, below))
-    inner_other = lax.ppermute(held, "exp", swap)
-
     edge_lists = pl.pallas_call(
         edge_kernel,
         in_specs=[VMEM] * 6,
@@ -389,51 +437,70 @@
         scratch_shapes=[pltpu.VMEM((visits, 2 * EDGE, cols), F32)],
         compiler_params=PARAMS,
         name="edge_visits",
-    )(above, below, part, edge_m, col_m, edge_mask)
+    )(first, second, part, edge_m, col_m, edge_mask)
     edge_other = lax.ppermute(edge_lists, "exp", swap)
 
-    def merged(mine, other):
-        rows = mine.shape[1]
-        return pl.pallas_call(
-            merge_kernel,
-            in_specs=[VMEM, VMEM],
-            out_specs=VMEM,
-            out_shape=vmem((rows, cols)),
-            compiler_params=PARAMS,
-            name="merge",
-        )(mine, other)
-
-    edges = merged(edge_lists, edge_other)
-    coadd_above = turned(edges[EDGE:].astype(BF16), "sky", 1)
-    coadd_below = turned(edges[:EDGE].astype(BF16), "sky", -1)
-    inner_coadd = merged(inner_lists, inner_other)
+    held, _ = lax.optimization_barrier((inner_lists, edge_other))
+    inner_other = lax.ppermute(held, "exp", swap)
+
+    edges, send_first, send_second = pl.pallas_call(
+        edge_merge_kernel,
+        in_specs=[VMEM] * 2,
+        out_specs=[VMEM] * 3,
+        out_shape=[vmem((2 * EDGE, cols)), vmem((EDGE, cols), BF16), vmem((EDGE, cols), BF16)],
+        compiler_params=PARAMS,
+        name="edge_merge",
+    )(edge_lists, edge_other)
+    coadd_first = paired(send_first, 0)
+    coadd_second = paired(send_second, 1)
+    inner_coadd = pl.pallas_call(
+        merge_kernel,
+        in_specs=[VMEM] * 2,
+        out_specs=VMEM,
+        out_shape=vmem((inner, cols)),
+        compiler_params=PARAMS,
+        name="inner_merge",
+    )(inner_lists, inner_other)
 
     width = cols // bands
-    coadd_image, pieces = pl.pallas_call(
+    coadd_image, keep, send = pl.pallas_call(
         psf_kernel,
         in_specs=[VMEM] * 6,
-        out_specs=[VMEM, VMEM],
-        out_shape=[vmem((1, height, cols)), vmem((bands, height + 8, width))],
-        scratch_shapes=[pltpu.VMEM((16, LANES), F32)],
+        out_specs=[VMEM] * 3,
+        out_shape=[
+            vmem((1, height, cols)),
+            vmem((height + 8, width)),
+            vmem((bands - 1, height // 2 + 8, width)),
+        ],
+        scratch_shapes=[pltpu.VMEM((16, LANES), F32), pltpu.VMEM((height, cols), F32)],
         compiler_params=PARAMS,
         name="psf",
-    )(coadd_above, coadd_below, edges, inner_coadd, psf_row, psf_col)
-
-    parts = [pieces[0]] + [turned(pieces[k], "band", k) for k in range(1, bands)]
-    sums = jnp.stack([part[height:, :LANES] for part in parts])
-    if strips <= 4:
-        sums = sum((turned(sums, "sky", k) for k in range(1, strips)), sums)
+    )(coadd_first, coadd_second, edges, inner_coadd, psf_row, psf_col)
+
+    if strips == 4 and bands == 2:
+        power = keep[height:, :LANES]
+        got = turned(send[0], "band", 1)
+        mine, theirs = [got], [lax.ppermute(got, "exp", swap)]
+        beside = flipped(power, "sky", 1)
+        across = lax.ppermute(
+            power, ("sky", "band"), [(2 * i + j, 2 * (i ^ 1) + 1 - j) for i in range(4) for j in (0, 1)]
+        )
+        sums = jnp.stack([power + beside, got[height // 2 :, :LANES] + across])
+        sums = sums + flipped(sums, "sky", 2)
     else:
+        mine = [turned(send[k - 1], "band", k) for k in range(1, bands)]
+        theirs = [lax.ppermute(part, "exp", swap) for part in mine]
+        sums = jnp.stack([keep[height:, :LANES]] + [part[height // 2 :, :LANES] for part in mine])
         sums = lax.psum(sums, "sky")
     pixels = height * strips * cols
     detection = pl.pallas_call(
-        lambda *refs: final_kernel(pixels, refs[:bands], refs[bands], refs[bands + 1]),
-        in_specs=[VMEM] * (bands + 1),
+        functools.partial(final_kernel, pixels),
+        in_specs=[VMEM] * (2 * bands),
         out_specs=VMEM,
         out_shape=vmem((height, width)),
         compiler_params=PARAMS,
         name="detection",
-    )(*[part[:height] for part in parts], sums)
+    )(keep, *mine, *theirs, sums)
     return coadd_image, detection
 
 

time: 42.6 us -> 34.5 us (0.81)
  waiting for transfers between devices: 15.2 us -> 12 us
  starting transfers between devices: 13.2 us -> 10.5 us
  Pallas kernels: 12.2 us -> 10 us
    ppermute x8 -> x1, starting transfers between devices: 12.6 us -> 0.54 us  [turned(): lax.ppermute(value, axis, [(i, (i + step) % size) for i in range(size)])]
    ppermute x8 -> x1, waiting for transfers between devices: 12.8 us -> 1.04 us  [turned(): lax.ppermute(value, axis, [(i, (i + step) % size) for i in range(size)])]
    ppermute x0 -> x8, starting transfers between devices: none -> 9.78 us  [the longest x4 5.19 us: paired(): return lax.ppermute(value, ('sky', 'exp'), pairs)]
    ppermute x0 -> x8, waiting for transfers between devices: none -> 5.69 us  [the longest x2 3.02 us: flipped(): lax.ppermute(value, axis, [(i, i ^ bits) for i in range(lax.axis_size(axi...]
    ppermute x1, waiting for transfers between devices: 0.01 us -> 3.16 us  [on_device(): inner_other = lax.ppermute(held, 'exp', swap)]
    pallas_call x1, Pallas kernels: 8.04 us -> 5.89 us  [on_device(): pl.pallas_call(inner_kernel, in_specs=[HBM] * 6, out_specs=[VMEM] * 5, ou...]
    squeeze x2 -> x0, local copies, waits for them, and re-layouts: 1.04 us -> none  [the longest x1 1.03 us: on_device(): below = turned(images[0, :, :EDGE, :], 'sky', -1)]
    dynamic_slice x0 -> x1, local copies, waits for them, and re-layouts: none -> 1.03 us  [on_device(): lax.dynamic_slice_in_dim(images[0], height - EDGE - far, EDGE, 1)]
  transfers between devices with their start and end apart: 10 -> 11, of which waited for: 6 -> 6; matrix products, arithmetic and copies ran while one was open for 0% -> 0% of each run, Pallas kernels for 25% -> 19%
where the time goes in v3:
time: 34.5 us; the launch traced here: 34.3 us
  waiting for transfers between devices  12 us (35%)
  starting transfers between devices  10.5 us (30%)
  Pallas kernels  10 us (29%)
  local copies, waits for them, and re-layouts  1.04 us (3%)
  between operations  0.76 us (2%)
    pallas_call x1, Pallas kernels, on_device(): pl.pallas_call(inner_kernel, in_specs=[HBM] * 6, out_specs=[VMEM] * 5, ou...  5.89 us
    ppermute x4, starting transfers between devices, paired(): return lax.ppermute(value, ('sky', 'exp'), pairs)  5.19 us
    ppermute x2, starting transfers between devices, flipped(): lax.ppermute(value, axis, [(i, i ^ bits) for i in range(lax.axis_size(axi...  3.4 us
    ppermute x1, waiting for transfers between devices, on_device(): inner_other = lax.ppermute(held, 'exp', swap)  3.16 us
    ppermute x2, waiting for transfers between devices, flipped(): lax.ppermute(value, axis, [(i, i ^ bits) for i in range(lax.axis_size(axi...  3.02 us
    ppermute x1, waiting for transfers between devices, on_device(): lax.ppermute(power, ('sky', 'band'), [(2 * i + j, 2 * (i ^ 1) + 1 - j) fo...  2.65 us
    ppermute x1, waiting for transfers between devices, on_device(): edge_other = lax.ppermute(edge_lists, 'exp', swap)  2.08 us
    pallas_call x1, Pallas kernels, on_device(): pl.pallas_call(edge_kernel, in_specs=[VMEM] * 6, out_specs=VMEM, out_shap...  1.93 us
  transfers between devices with their start and end apart: 11, of which 6 were waited for; matrix products, arithmetic and copies ran while one was open for 0% of the time, Pallas kernels for 19%

profile of v3, /device:TPU:0, one launch (start us, length us, event | category | flops | bytes accessed | tf_op | source)
XLA Modules:
  0.0 34.3 jit_solution(1159642217775686593)
XLA Ops:
  0.6 1.0 %dynamic-slice_bitcast_fusion = (bf16[10,16,512]{2,1,0:T(8,128)(2,1)S(1)}, bf16[10,16,512]{2,1,0:T(8,128)(2,1)S(1)}) fusion(bf16[1,10,128,512]{3,2,1,0:T(8,128)(2,1)} %images_h.1, s32[]{:T(128)S(6)} %select_n.9, s32[]{:T(128)S(6)} %select_n.8), kind=kLoop, calls=%fused_computation | loop fusion | bytes 655368 | tf_op jit(solution)/shard_map/dynamic_slice | solution.py:383
  1.7 0.5 %collective-permute-start.1 = (bf16[10,16,512]{2,1,0:T(8,128)(2,1)S(1)}, bf16[10,16,512]{2,1,0:T(8,128)(2,1)S(1)}, u32[]{:S(2)}, u32[]{:S(2)}) collective-permute-start(bf16[10,16,512]{2,1,0:T(8,128)(2,1)S(1)} %get-tuple-element.26), channel_id=1, source_target_pairs={{0,2},{2,0},{4,8},{6,10},{8,4},{10,6},{12,14},{14,12},{1,3},{3,1},... | collective-permute-start | bytes 491528 | tf_op jit(solution)/shard_map/ppermute | solution.py:363
  2.2 4.1 %collective-permute-start = (bf16[10,16,512]{2,1,0:T(8,128)(2,1)S(1)}, bf16[10,16,512]{2,1,0:T(8,128)(2,1)S(1)}, u32[]{:S(2)}, u32[]{:S(2)}) collective-permute-start(bf16[10,16,512]{2,1,0:T(8,128)(2,1)S(1)} %get-tuple-element.27), channel_id=1, source_target_pairs={{0,4},{2,6},{4,0},{6,2},{8,12},{10,14},{12,8},{14,10},{1,5},{3,7},... | collective-permute-start | bytes 491528 | tf_op jit(solution)/shard_map/ppermute | solution.py:363
  6.3 5.9 %inner_visits.1 = (f32[10,96,512]{2,1,0:T(8,128)S(1)}, f32[10,32,512]{2,1,0:T(8,128)S(1)}, bf16[10,64,128]{2,1,0:T(8,128)(2,1)S(1)}, bf16[10,256,256]{2,1,0:T(8,128)(2,1)S(1)}, s32[10,32,512]{2,1,0:T(8,128)S(1)}) custom-call(s32[1,10]{1,0:T(1,128)} %groups_h.1, f32[1,16]{1,0:T(1,128)} %points_h.1, bf16[1,10,128,512]{3,2,1,0:T(8,128)(2,1)} %images_h.1, ...), custom_call_target="tpu_custom_call" | custom-call | flops 2684354560 | bytes 3932160 | tf_op jit(solution)/shard_map/inner_visits/pallas_call | solution.py:386
  12.3 1.9 %edge_visits.1.mine = f32[10,32,512]{2,1,0:T(8,128)S(1)} custom-call(bf16[10,16,512]{2,1,0:T(8,128)(2,1)S(1)} %collective-permute-done.first, bf16[10,16,512]{2,1,0:T(8,128)(2,1)S(1)} %collective-permute-done.1.second, f32[10,32,512]{2,1,0:T(8,128)S(1)} %get-tuple-element.14.part, bf16[10,64,128]{2,1,0:T(8,128)(2,1)S(1)} %get-tuple-element.15.edge_m, ...), custom_call_target="tpu_custom_call" | custom-call | tf_op jit(solution)/shard_map/edge_visits/pallas_call | solution.py:432
  14.2 0.1 collective-permute-start.2
  14.3 2.1 %collective-permute-done.2.other = f32[10,32,512]{2,1,0:T(8,128)S(1)} collective-permute-done((f32[10,32,512]{2,1,0:T(8,128)S(1)}, f32[10,32,512]{2,1,0:T(8,128)S(1)}, u32[]{:S(2)}, u32[]{:S(2)}) %collective-permute-start.2) | collective-permute-done | bytes 655392 | tf_op jit(solution)/shard_map/ppermute | solution.py:441
  16.4 0.1 collective-permute-start.5
  16.5 0.1 edge_merge.1
  16.6 0.1 collective-permute-start.3
  16.7 0.0 copy-start.1
  16.7 0.4 %collective-permute-start.4 = (bf16[16,512]{1,0:T(8,128)(2,1)S(1)}, bf16[16,512]{1,0:T(8,128)(2,1)S(1)}, u32[]{:S(2)}, u32[]{:S(2)}) collective-permute-start(bf16[16,512]{1,0:T(8,128)(2,1)S(1)} %get-tuple-element.19), channel_id=1, source_target_pairs={{0,2},{2,0},{4,8},{6,10},{8,4},{10,6},{12,14},{14,12},{1,3},{3,1},... | collective-permute-start | bytes 49160 | tf_op jit(solution)/shard_map/ppermute | solution.py:363
  17.2 3.2 %collective-permute-done.5.other = f32[10,96,512]{2,1,0:T(8,128)S(1)} collective-permute-done((f32[10,96,512]{2,1,0:T(8,128)S(1)}, f32[10,96,512]{2,1,0:T(8,128)S(1)}, u32[]{:S(2)}, u32[]{:S(2)}) %collective-permute-start.5) | collective-permute-done | bytes 1966112 | tf_op jit(solution)/shard_map/ppermute | solution.py:444
  20.3 0.3 inner_merge.1.inner
  20.7 0.9 %psf.1 = (f32[1,128,512]{2,1,0:T(8,128)}, f32[136,256]{1,0:T(8,128)S(1)}, f32[1,72,256]{2,1,0:T(8,128)S(1)}) custom-call(bf16[16,512]{1,0:T(8,128)(2,1)S(1)} %collective-permute-done.3.first, bf16[16,512]{1,0:T(8,128)(2,1)S(1)} %collective-permute-done.4.second, f32[32,512]{1,0:T(8,128)S(1)} %get-tuple-element.20.edges, f32[96,512]{1,0:T(8,128)S(1)} %inner_merge.1.inner, ...), custom_call_target="tpu_custom_call" | custom-call | tf_op jit(solution)/shard_map/psf/pallas_call | solution.py:466
  21.6 1.8 %collective-permute-start.8 = (f32[8,128]{1,0:T(8,128)S(1)}, f32[8,128]{1,0:T(8,128)S(1)}, u32[]{:S(2)}, u32[]{:S(2)}) collective-permute-start(f32[8,128]{1,0:T(8,128)S(1)} %slice.6), channel_id=1, source_target_pairs={{0,4},{4,0},{8,12},{12,8},{1,5},{5,1},{9,13},{13,9},{2,6},{6,2},{1... | collective-permute-start | bytes 12296 | tf_op jit(solution)/shard_map/ppermute | solution.py:367
  23.4 1.2 %collective-permute-start.9 = (f32[8,128]{1,0:T(8,128)S(1)}, f32[8,128]{1,0:T(8,128)S(1)}, u32[]{:S(2)}, u32[]{:S(2)}) collective-permute-start(f32[8,128]{1,0:T(8,128)S(1)} %slice.6), channel_id=1, source_target_pairs={{0,5},{1,4},{4,1},{5,0},{8,13},{9,12},{12,9},{13,8},{2,7},{3,6},{6... | collective-permute-start | bytes 12296 | tf_op jit(solution)/shard_map/ppermute | solution.py:485
  24.6 0.5 %collective-permute-start.6 = (f32[72,256]{1,0:T(8,128)S(1)}, f32[72,256]{1,0:T(8,128)S(1)}, u32[]{:S(2)}, u32[]{:S(2)}) collective-permute-start(f32[72,256]{1,0:T(8,128)S(1)} %bitcast.11), channel_id=1, source_target_pairs={{0,1},{1,0},{2,3},{3,2},{4,5},{5,4},{6,7},{7,6},{8,9},{9,8},{10,11... | collective-permute-start | bytes 221192 | tf_op jit(solution)/shard_map/ppermute | solution.py:372
  25.1 0.1 collective-permute-done.8
  25.2 2.7 %collective-permute-done.9 = f32[8,128]{1,0:T(8,128)S(1)} collective-permute-done((f32[8,128]{1,0:T(8,128)S(1)}, f32[8,128]{1,0:T(8,128)S(1)}, u32[]{:S(2)}, u32[]{:S(2)}) %collective-permute-start.9) | collective-permute-done | bytes 4128 | tf_op jit(solution)/shard_map/ppermute | solution.py:485
  27.9 1.0 %collective-permute-done.6.refs_0_ = f32[72,256]{1,0:T(8,128)S(1)} collective-permute-done((f32[72,256]{1,0:T(8,128)S(1)}, f32[72,256]{1,0:T(8,128)S(1)}, u32[]{:S(2)}, u32[]{:S(2)}) %collective-permute-start.6) | collective-permute-done | bytes 73760 | tf_op jit(solution)/shard_map/ppermute | solution.py:372
  28.9 1.6 %collective-permute-start.10 = (f32[2,8,128]{2,1,0:T(8,128)S(1)}, f32[2,8,128]{2,1,0:T(8,128)S(1)}, u32[]{:S(2)}, u32[]{:S(2)}) collective-permute-start(f32[2,8,128]{2,1,0:T(8,128)S(1)} %pad_maximum_fusion), channel_id=1, source_target_pairs={{0,8},{4,12},{8,0},{12,4},{1,9},{5,13},{9,1},{13,5},{2,10},{6,14},... | collective-permute-start | bytes 24584 | tf_op jit(solution)/shard_map/ppermute | solution.py:367
  30.6 2.9 %collective-permute-done.10 = f32[2,8,128]{2,1,0:T(8,128)S(1)} collective-permute-done((f32[2,8,128]{2,1,0:T(8,128)S(1)}, f32[2,8,128]{2,1,0:T(8,128)S(1)}, u32[]{:S(2)}, u32[]{:S(2)}) %collective-permute-start.10) | collective-permute-done | bytes 8224 | tf_op jit(solution)/shard_map/ppermute | solution.py:367
  33.5 0.9 %detection.1 = f32[128,256]{1,0:T(8,128)} custom-call(f32[136,256]{1,0:T(8,128)S(1)} %get-tuple-element.24.keep, f32[72,256]{1,0:T(8,128)S(1)} %collective-permute-done.6.refs_0_, f32[72,256]{1,0:T(8,128)S(1)} %collective-permute-done.7.refs_1_, f32[2,8,128]{2,1,0:T(8,128)S(1)} %fusion.1.refs_2_), custom_call_target="tpu_custom_call" | custom-call | tf_op jit(solution)/shard_map/detection/pallas_call | solution.py:496
  (14 shorter events, 0.0 us)
Async XLA Ops:
  1.7 10.6 %collective-permute-start.1 = (bf16[10,16,512]{2,1,0:T(8,128)(2,1)S(1)}, bf16[10,16,512]{2,1,0:T(8,128)(2,1)S(1)}, u32[]{:S(2)}, u32[]{:S(2)}) collective-permute-start(bf16[10,16,512]{2,1,0:T(8,128)(2,1)S(1)} %get-tuple-element.26), channel_id=1, source_target_pairs={{0,2},{2,0},{4,8},{6,10},{8,4},{10,6},{12,14},{14,12},{1,3},{3,1},... | collective-permute-start | bytes 491528 | tf_op jit(solution)/shard_map/ppermute | solution.py:363
  2.2 10.1 %collective-permute-start = (bf16[10,16,512]{2,1,0:T(8,128)(2,1)S(1)}, bf16[10,16,512]{2,1,0:T(8,128)(2,1)S(1)}, u32[]{:S(2)}, u32[]{:S(2)}) collective-permute-start(bf16[10,16,512]{2,1,0:T(8,128)(2,1)S(1)} %get-tuple-element.27), channel_id=1, source_target_pairs={{0,4},{2,6},{4,0},{6,2},{8,12},{10,14},{12,8},{14,10},{1,5},{3,7},... | collective-permute-start | bytes 491528 | tf_op jit(solution)/shard_map/ppermute | solution.py:363
  14.2 2.2 %collective-permute-start.2 = (f32[10,32,512]{2,1,0:T(8,128)S(1)}, f32[10,32,512]{2,1,0:T(8,128)S(1)}, u32[]{:S(2)}, u32[]{:S(2)}) collective-permute-start(f32[10,32,512]{2,1,0:T(8,128)S(1)} %edge_visits.1.mine), channel_id=1, source_target_pairs={{0,2},{2,0},{1,3},{3,1},{4,6},{6,4},{5,7},{7,5},{8,10},{10,8},{9,1... | collective-permute-start | bytes 1966088 | tf_op jit(solution)/shard_map/ppermute | solution.py:441
  16.4 4.0 %collective-permute-start.5 = (f32[10,96,512]{2,1,0:T(8,128)S(1)}, f32[10,96,512]{2,1,0:T(8,128)S(1)}, u32[]{:S(2)}, u32[]{:S(2)}) collective-permute-start(f32[10,96,512]{2,1,0:T(8,128)S(1)} %get-tuple-element.22.mine), channel_id=1, source_target_pairs={{0,2},{2,0},{1,3},{3,1},{4,6},{6,4},{5,7},{7,5},{8,10},{10,8},{9,1... | collective-permute-start | bytes 5898248 | tf_op jit(solution)/shard_map/ppermute | solution.py:444
  16.6 4.1 %collective-permute-start.3 = (bf16[16,512]{1,0:T(8,128)(2,1)S(1)}, bf16[16,512]{1,0:T(8,128)(2,1)S(1)}, u32[]{:S(2)}, u32[]{:S(2)}) collective-permute-start(bf16[16,512]{1,0:T(8,128)(2,1)S(1)} %get-tuple-element.18), channel_id=1, source_target_pairs={{0,4},{2,6},{4,0},{6,2},{8,12},{10,14},{12,8},{14,10},{1,5},{3,7},... | collective-permute-start | bytes 49160 | tf_op jit(solution)/shard_map/ppermute | solution.py:363
  16.7 4.0 %copy-start = (f32[1,31]{1,0:T(1,128)S(1)}, f32[1,31]{1,0:T(1,128)}, u32[]{:S(2)}) copy-start(f32[1,31]{1,0:T(1,128)} %row_taps.1) | copy-start | bytes 376
  16.7 4.0 %copy-start.1 = (f32[1,31]{1,0:T(1,128)S(1)}, f32[1,31]{1,0:T(1,128)}, u32[]{:S(2)}) copy-start(f32[1,31]{1,0:T(1,128)} %col_taps.1) | copy-start | bytes 376
  16.7 4.0 %collective-permute-start.4 = (bf16[16,512]{1,0:T(8,128)(2,1)S(1)}, bf16[16,512]{1,0:T(8,128)(2,1)S(1)}, u32[]{:S(2)}, u32[]{:S(2)}) collective-permute-start(bf16[16,512]{1,0:T(8,128)(2,1)S(1)} %get-tuple-element.19), channel_id=1, source_target_pairs={{0,2},{2,0},{4,8},{6,10},{8,4},{10,6},{12,14},{14,12},{1,3},{3,1},... | collective-permute-start | bytes 49160 | tf_op jit(solution)/shard_map/ppermute | solution.py:363
  21.6 3.6 %collective-permute-start.8 = (f32[8,128]{1,0:T(8,128)S(1)}, f32[8,128]{1,0:T(8,128)S(1)}, u32[]{:S(2)}, u32[]{:S(2)}) collective-permute-start(f32[8,128]{1,0:T(8,128)S(1)} %slice.6), channel_id=1, source_target_pairs={{0,4},{4,0},{8,12},{12,8},{1,5},{5,1},{9,13},{13,9},{2,6},{6,2},{1... | collective-permute-start | bytes 12296 | tf_op jit(solution)/shard_map/ppermute | solution.py:367
  23.4 4.5 %collective-permute-start.9 = (f32[8,128]{1,0:T(8,128)S(1)}, f32[8,128]{1,0:T(8,128)S(1)}, u32[]{:S(2)}, u32[]{:S(2)}) collective-permute-start(f32[8,128]{1,0:T(8,128)S(1)} %slice.6), channel_id=1, source_target_pairs={{0,5},{1,4},{4,1},{5,0},{8,13},{9,12},{12,9},{13,8},{2,7},{3,6},{6... | collective-permute-start | bytes 12296 | tf_op jit(solution)/shard_map/ppermute | solution.py:485
  24.6 4.4 %collective-permute-start.6 = (f32[72,256]{1,0:T(8,128)S(1)}, f32[72,256]{1,0:T(8,128)S(1)}, u32[]{:S(2)}, u32[]{:S(2)}) collective-permute-start(f32[72,256]{1,0:T(8,128)S(1)} %bitcast.11), channel_id=1, source_target_pairs={{0,1},{1,0},{2,3},{3,2},{4,5},{5,4},{6,7},{7,6},{8,9},{9,8},{10,11... | collective-permute-start | bytes 221192 | tf_op jit(solution)/shard_map/ppermute | solution.py:372
  28.9 4.5 %collective-permute-start.10 = (f32[2,8,128]{2,1,0:T(8,128)S(1)}, f32[2,8,128]{2,1,0:T(8,128)S(1)}, u32[]{:S(2)}, u32[]{:S(2)}) collective-permute-start(f32[2,8,128]{2,1,0:T(8,128)S(1)} %pad_maximum_fusion), channel_id=1, source_target_pairs={{0,8},{4,12},{8,0},{12,4},{1,9},{5,13},{9,1},{13,5},{2,10},{6,14},... | collective-permute-start | bytes 24584 | tf_op jit(solution)/shard_map/ppermute | solution.py:367
  30.6 2.9 %collective-permute-start.7 = (f32[72,256]{1,0:T(8,128)S(1)}, f32[72,256]{1,0:T(8,128)S(1)}, u32[]{:S(2)}, u32[]{:S(2)}) collective-permute-start(f32[72,256]{1,0:T(8,128)S(1)} %collective-permute-done.6.refs_0_), channel_id=1, source_target_pairs={{0,2},{2,0},{1,3},{3,1},{4,6},{6,4},{5,7},{7,5},{8,10},{10,8},{9,1... | collective-permute-start | bytes 221192 | tf_op jit(solution)/shard_map/ppermute | solution.py:483

commit v4 on v3

--- a/solution.py
+++ b/solution.py
@@ -213,18 +213,21 @@
         square = around_matrix(taps[slot : slot + 1, :])
         row_m[v] = jnp.concatenate(split2(jnp.where(near, square, 0.0)), axis=1)
         far = jnp.where(near, 0.0, square)
-        far = jnp.concatenate([far[:EDGE], far[height - EDGE :]], axis=0)
+        far = pltpu.roll(jnp.concatenate([far[:EDGE], far[height - EDGE :]], axis=0), EDGE, 1)
         edge_m[v] = jnp.concatenate(split2(far), axis=0)
         col_m[v] = col_matrix(taps[slot + 8 : slot + 9, :] * scale)
 
-    def convolve(v, slot):
+    def smear(v):
         image = images[v]
         smeared = jnp.dot(
             row_m[v], jnp.concatenate([image, image], axis=0), preferred_element_type=F32
         )
+        values[v] = smeared[EDGE : height - EDGE]
         part[v, 0:EDGE] = smeared[:EDGE]
         part[v, EDGE : 2 * EDGE] = smeared[height - EDGE :]
-        result = col_conv(smeared[EDGE : height - EDGE], col_m[v])
+
+    def convolve(v):
+        result = col_conv(values[v], col_m[v])
         values[v] = jnp.where(mask[v, EDGE : height - EDGE] == 1, result, SENTINEL)
         edge_mask[v, 0:EDGE] = mask[v, 0:EDGE]
         edge_mask[v, EDGE : 2 * EDGE] = mask[v, height - EDGE :]
@@ -232,20 +235,35 @@
     at_once = UNROLL if visits % UNROLL == 0 else 1
     steps = visits // at_once
 
+    def work(step, most=None):
+        for i in range(at_once):
+            convolve(step * at_once + i)
+        for i in range(at_once):
+            if most is None or most >= 1:
+                smear((step + 1) * at_once + i)
+        for i in range(at_once):
+            if most is None or most >= 2:
+                build((step + 2) * at_once + i, 16 * i)
+
+    for step in range(min(2, steps)):
+        for i in range(at_once):
+            build(step * at_once + i, 16 * i)
+    image_copy(0).wait()
+    mask_copy(0).wait()
+    for i in range(at_once):
+        smear(i)
+    early = max(min(middle // at_once - 1, steps - 2), 0)
+
     def body(step, carry):
-        for i in range(at_once):
-            convolve(step * at_once + i, 16 * i)
-        for i in range(at_once):
-            build(lax.rem((step + 1) * at_once + i, visits), 16 * i)
+        work(step)
         return carry
 
-    for i in range(at_once):
-        build(i, 16 * i)
-    turn = middle // at_once
-    for part_of, first, last in ((0, 0, turn), (1, turn, steps)):
-        image_copy(part_of).wait()
-        mask_copy(part_of).wait()
-        lax.fori_loop(first, last, body, 0)
+    lax.fori_loop(0, early, body, 0)
+    image_copy(1).wait()
+    mask_copy(1).wait()
+    lax.fori_loop(early, steps - 2, body, 0)
+    for step in range(max(steps - 2, 0), steps):
+        work(step, steps - 1 - step)
     sort_visits(values, lists)
 
 
@@ -253,11 +271,11 @@
     visits, _, cols = values.shape
     for visit in range(visits):
         before, after = at_ends(first[visit], second[visit])
-        window = jnp.concatenate(
-            [after, jnp.zeros((LANES - 2 * EDGE, cols), BF16), before], axis=0
-        )
-        both = jnp.dot(edge_m[visit], window, preferred_element_type=F32)
-        result = col_conv(part[visit] + (both[: 2 * EDGE] + both[2 * EDGE :]), col_m[visit])
+        window = jnp.concatenate([before, after], axis=0)
+        both = jnp.dot(edge_m[visit, :, 0 : 2 * EDGE], window, preferred_element_type=F32)
+        values[visit] = part[visit] + (both[: 2 * EDGE] + both[2 * EDGE :])
+    for visit in range(visits):
+        result = col_conv(values[visit], col_m[visit])
         values[visit] = jnp.where(edge_mask[visit] == 1, result, SENTINEL)
     sort_visits(values, lists)
 
@@ -286,11 +304,8 @@
     send_second[...] = jnp.where(even, top, bottom).astype(BF16)
 
 
-def psf_kernel(first, second, edges, inner, row_taps, col_taps, coadd, keep, send, taps, scratch):
+def psf_kernel(first, second, edges, inner, row_taps, col_taps, coadd, energy, power, taps):
     height, cols = coadd.shape[1:]
-    width = keep.shape[1]
-    others, half, _ = send.shape
-    half = half - 8
     coadd[0, 0:EDGE] = edges[0:EDGE]
     coadd[0, EDGE : height - EDGE] = inner[...]
     coadd[0, height - EDGE : height] = edges[EDGE : 2 * EDGE]
@@ -308,33 +323,36 @@
     both = jnp.dot(jnp.concatenate([row_h, row_l], axis=0), high, preferred_element_type=F32)
     both_low = jnp.dot(row_h, low, preferred_element_type=F32)
     filtered = col_conv(both[:height] + (both[height:] + both_low), col_m)
-    energy = filtered * filtered
-    part = jnp.sum(energy.reshape(height // 8, 8, cols), axis=0)
-    part = sum(part[:, n * LANES : (n + 1) * LANES] for n in range(cols // LANES))
-    scratch[...] = energy
+    squares = filtered * filtered
+    energy[...] = squares
+    part = jnp.sum(squares.reshape(height // 8, 8, cols), axis=0)
+    power[...] = sum(part[:, n * LANES : (n + 1) * LANES] for n in range(cols // LANES))
+
+
+def pack_kernel(energy, power, send):
+    others, half, width = send.shape
+    half = half - 8
     own = lax.axis_index("band")
     start = pl.multiple_of(lax.axis_index("exp") * half, half)
-    keep[0:height] = scratch[:, pl.ds(pl.multiple_of(own * width, width), width)]
     for k in range(others):
         band = lax.rem(own + k + 1, others + 1)
         lanes = pl.ds(pl.multiple_of(band * width, width), width)
-        send[k, 0:half] = scratch[pl.ds(start, half), lanes]
-    for n in range(width // LANES):
-        keep[height : height + 8, n * LANES : (n + 1) * LANES] = part
-        for k in range(others):
-            send[k, half : half + 8, n * LANES : (n + 1) * LANES] = part
-
-
-def final_kernel(pixels, keep, *refs):
+        send[k, 0:half] = energy[pl.ds(start, half), lanes]
+        for n in range(width // LANES):
+            send[k, half : half + 8, n * LANES : (n + 1) * LANES] = power[...]
+
+
+def final_kernel(pixels, energy, *refs):
     others = (len(refs) - 2) // 2
     mine, theirs, sums, detection = refs[:others], refs[others : 2 * others], refs[-2], refs[-1]
-    height = detection.shape[0]
+    height, width = detection.shape
     half = height // 2
+    lanes = pl.ds(pl.multiple_of(lax.axis_index("band") * width, width), width)
     scales = [1.0 / (jnp.sum(sums[i]) / pixels + EPSILON) for i in range(others + 1)]
     core = lax.axis_index("exp")
     for place, parts in ((core, mine), (1 - core, theirs)):
         at = pl.ds(pl.multiple_of(place * half, half), half)
-        total = keep[at, :] * scales[0]
+        total = energy[at, lanes] * scales[0]
         for i in range(others):
             total = total + parts[i][0:half, :] * scales[i + 1]
         detection[at, :] = total
@@ -463,34 +481,47 @@
     )(inner_lists, inner_other)
 
     width = cols // bands
-    coadd_image, keep, send = pl.pallas_call(
+    coadd_image, energy, power = pl.pallas_call(
         psf_kernel,
         in_specs=[VMEM] * 6,
         out_specs=[VMEM] * 3,
         out_shape=[
             vmem((1, height, cols)),
-            vmem((height + 8, width)),
-            vmem((bands - 1, height // 2 + 8, width)),
+            vmem((height, cols)),
+            vmem((8, LANES)),
         ],
-        scratch_shapes=[pltpu.VMEM((16, LANES), F32), pltpu.VMEM((height, cols), F32)],
+        scratch_shapes=[pltpu.VMEM((16, LANES), F32)],
         compiler_params=PARAMS,
         name="psf",
     )(coadd_first, coadd_second, edges, inner_coadd, psf_row, psf_col)
-
-    if strips == 4 and bands == 2:
-        power = keep[height:, :LANES]
+    send = pl.pallas_call(
+        pack_kernel,
+        in_specs=[VMEM] * 2,
+        out_specs=VMEM,
+        out_shape=vmem((bands - 1, height // 2 + 8, width)),
+        compiler_params=PARAMS,
+        name="pack",
+    )(energy, power)
+
+    if strips == 4 and bands == 2 and lax.axis_size("exp") == 2:
+        pairs = []
+        for strip in range(strips):
+            for core in range(2):
+                for band in range(2):
+                    to = (strip ^ 1, core, band ^ core)
+                    pairs.append((4 * strip + 2 * core + band, 4 * to[0] + 2 * to[1] + to[2]))
+        one = lax.ppermute(power, ("sky", "exp", "band"), pairs)
+        two = lax.ppermute(one, "exp", swap)
+        first_core = lax.axis_index("exp") == 0
+        beside, across = jnp.where(first_core, one, two), jnp.where(first_core, two, one)
         got = turned(send[0], "band", 1)
         mine, theirs = [got], [lax.ppermute(got, "exp", swap)]
-        beside = flipped(power, "sky", 1)
-        across = lax.ppermute(
-            power, ("sky", "band"), [(2 * i + j, 2 * (i ^ 1) + 1 - j) for i in range(4) for j in (0, 1)]
-        )
         sums = jnp.stack([power + beside, got[height // 2 :, :LANES] + across])
         sums = sums + flipped(sums, "sky", 2)
     else:
         mine = [turned(send[k - 1], "band", k) for k in range(1, bands)]
         theirs = [lax.ppermute(part, "exp", swap) for part in mine]
-        sums = jnp.stack([keep[height:, :LANES]] + [part[height // 2 :, :LANES] for part in mine])
+        sums = jnp.stack([power] + [part[height // 2 :, :LANES] for part in mine])
         sums = lax.psum(sums, "sky")
     pixels = height * strips * cols
     detection = pl.pallas_call(
@@ -500,7 +531,7 @@
         out_shape=vmem((height, width)),
         compiler_params=PARAMS,
         name="detection",
-    )(keep, *mine, *theirs, sums)
+    )(energy, *mine, *theirs, sums)
     return coadd_image, detection
 
 

time: 34.5 us -> 32.3 us (0.936)
  Pallas kernels: 10 us -> 8.77 us
  waiting for transfers between devices: 12 us -> 10.9 us
    ppermute x2 -> x1, starting transfers between devices: 3.4 us -> 1.98 us  [flipped(): lax.ppermute(value, axis, [(i, i ^ bits) for i in range(lax.axis_size(axi...]
    ppermute x1, waiting for transfers between devices: 1.04 us -> 0.01 us  [turned(): lax.ppermute(value, axis, [(i, (i + step) % size) for i in range(size)])]
    ppermute x1, starting transfers between devices: 0.54 us -> 1.49 us  [turned(): lax.ppermute(value, axis, [(i, (i + step) % size) for i in range(size)])]
    pallas_call x1, Pallas kernels: 1.93 us -> 1.13 us  [on_device(): pl.pallas_call(edge_kernel, in_specs=[VMEM] * 6, out_specs=VMEM, out_shap...]
    ppermute x1 -> x2, starting transfers between devices: 1.19 us -> 1.76 us  [the longest x1 1.76 us: on_device(): one = lax.ppermute(power, ('sky', 'exp', 'band'), pairs)]
    pallas_call x1, Pallas kernels: 5.89 us -> 5.42 us  [on_device(): pl.pallas_call(inner_kernel, in_specs=[HBM] * 6, out_specs=[VMEM] * 5, ou...]
    ppermute x2 -> x1, waiting for transfers between devices: 3.02 us -> 2.63 us  [flipped(): lax.ppermute(value, axis, [(i, i ^ bits) for i in range(lax.axis_size(axi...]
    ppermute x1 -> x2, waiting for transfers between devices: 2.65 us -> 3.01 us  [the longest x1 1.85 us: on_device(): one = lax.ppermute(power, ('sky', 'exp', 'band'), pairs)]
  transfers between devices with their start and end apart: 11 -> 11, of which waited for: 6 -> 5; matrix products, arithmetic and copies ran while one was open for 0% -> 0% of each run, Pallas kernels for 19% -> 18%
where the time goes in v4:
time: 32.3 us; the launch traced here: 32.1 us
  waiting for transfers between devices  10.9 us (34%)
  starting transfers between devices  10.6 us (33%)
  Pallas kernels  8.77 us (27%)
  local copies, waits for them, and re-layouts  1.04 us (3%)
  between operations  0.75 us (2%)
    pallas_call x1, Pallas kernels, on_device(): pl.pallas_call(inner_kernel, in_specs=[HBM] * 6, out_specs=[VMEM] * 5, ou...  5.42 us
    ppermute x4, starting transfers between devices, paired(): return lax.ppermute(value, ('sky', 'exp'), pairs)  5.2 us
    ppermute x1, waiting for transfers between devices, on_device(): inner_other = lax.ppermute(held, 'exp', swap)  3.16 us
    ppermute x1, waiting for transfers between devices, flipped(): lax.ppermute(value, axis, [(i, i ^ bits) for i in range(lax.axis_size(axi...  2.63 us
    ppermute x1, waiting for transfers between devices, on_device(): edge_other = lax.ppermute(edge_lists, 'exp', swap)  2.08 us
    ppermute x1, starting transfers between devices, flipped(): lax.ppermute(value, axis, [(i, i ^ bits) for i in range(lax.axis_size(axi...  1.98 us
    ppermute x1, waiting for transfers between devices, on_device(): one = lax.ppermute(power, ('sky', 'exp', 'band'), pairs)  1.85 us
    ppermute x1, starting transfers between devices, on_device(): one = lax.ppermute(power, ('sky', 'exp', 'band'), pairs)  1.76 us
  transfers between devices with their start and end apart: 11, of which 5 were waited for; matrix products, arithmetic and copies ran while one was open for 0% of the time, Pallas kernels for 18%

profile of v4, /device:TPU:0, one launch (start us, length us, event | category | flops | bytes accessed | tf_op | source)
XLA Modules:
  0.0 32.1 jit_solution(1404555568439324524)
XLA Ops:
  0.6 1.0 %dynamic-slice_bitcast_fusion = (bf16[10,16,512]{2,1,0:T(8,128)(2,1)S(1)}, bf16[10,16,512]{2,1,0:T(8,128)(2,1)S(1)}) fusion(bf16[1,10,128,512]{3,2,1,0:T(8,128)(2,1)} %images_h.1, s32[]{:T(128)S(6)} %select_n.21, s32[]{:T(128)S(6)} %select_n.20), kind=kLoop, calls=%fused_computation | loop fusion | bytes 655368 | tf_op jit(solution)/shard_map/dynamic_slice | solution.py:401
  1.7 0.5 %collective-permute-start.1 = (bf16[10,16,512]{2,1,0:T(8,128)(2,1)S(1)}, bf16[10,16,512]{2,1,0:T(8,128)(2,1)S(1)}, u32[]{:S(2)}, u32[]{:S(2)}) collective-permute-start(bf16[10,16,512]{2,1,0:T(8,128)(2,1)S(1)} %get-tuple-element.26), channel_id=1, source_target_pairs={{0,2},{2,0},{4,8},{6,10},{8,4},{10,6},{12,14},{14,12},{1,3},{3,1},... | collective-permute-start | bytes 491528 | tf_op jit(solution)/shard_map/ppermute | solution.py:381
  2.2 4.1 %collective-permute-start = (bf16[10,16,512]{2,1,0:T(8,128)(2,1)S(1)}, bf16[10,16,512]{2,1,0:T(8,128)(2,1)S(1)}, u32[]{:S(2)}, u32[]{:S(2)}) collective-permute-start(bf16[10,16,512]{2,1,0:T(8,128)(2,1)S(1)} %get-tuple-element.27), channel_id=1, source_target_pairs={{0,4},{2,6},{4,0},{6,2},{8,12},{10,14},{12,8},{14,10},{1,5},{3,7},... | collective-permute-start | bytes 491528 | tf_op jit(solution)/shard_map/ppermute | solution.py:381
  6.3 5.4 %inner_visits.1 = (f32[10,96,512]{2,1,0:T(8,128)S(1)}, f32[10,32,512]{2,1,0:T(8,128)S(1)}, bf16[10,64,128]{2,1,0:T(8,128)(2,1)S(1)}, bf16[10,256,256]{2,1,0:T(8,128)(2,1)S(1)}, s32[10,32,512]{2,1,0:T(8,128)S(1)}) custom-call(s32[1,10]{1,0:T(1,128)} %groups_h.1, f32[1,16]{1,0:T(1,128)} %points_h.1, bf16[1,10,128,512]{3,2,1,0:T(8,128)(2,1)} %images_h.1, ...), custom_call_target="tpu_custom_call" | custom-call | flops 2684354560 | bytes 3932160 | tf_op jit(solution)/shard_map/inner_visits/pallas_call | solution.py:404
  11.8 0.0 collective-permute-done.1.second
  11.8 1.1 %edge_visits.1.mine = f32[10,32,512]{2,1,0:T(8,128)S(1)} custom-call(bf16[10,16,512]{2,1,0:T(8,128)(2,1)S(1)} %collective-permute-done.first, bf16[10,16,512]{2,1,0:T(8,128)(2,1)S(1)} %collective-permute-done.1.second, f32[10,32,512]{2,1,0:T(8,128)S(1)} %get-tuple-element.14.part, bf16[10,64,128]{2,1,0:T(8,128)(2,1)S(1)} %get-tuple-element.15.edge_m, ...), custom_call_target="tpu_custom_call" | custom-call | tf_op jit(solution)/shard_map/edge_visits/pallas_call | solution.py:450
  12.9 0.1 collective-permute-start.2
  13.0 2.1 %collective-permute-done.2.other = f32[10,32,512]{2,1,0:T(8,128)S(1)} collective-permute-done((f32[10,32,512]{2,1,0:T(8,128)S(1)}, f32[10,32,512]{2,1,0:T(8,128)S(1)}, u32[]{:S(2)}, u32[]{:S(2)}) %collective-permute-start.2) | collective-permute-done | bytes 655392 | tf_op jit(solution)/shard_map/ppermute | solution.py:459
  15.1 0.1 collective-permute-start.5
  15.2 0.1 edge_merge.1
  15.4 0.3 collective-permute-start.3
  15.6 0.3 collective-permute-start.4
  15.9 3.2 %collective-permute-done.5.other = f32[10,96,512]{2,1,0:T(8,128)S(1)} collective-permute-done((f32[10,96,512]{2,1,0:T(8,128)S(1)}, f32[10,96,512]{2,1,0:T(8,128)S(1)}, u32[]{:S(2)}, u32[]{:S(2)}) %collective-permute-start.5) | collective-permute-done | bytes 1966112 | tf_op jit(solution)/shard_map/ppermute | solution.py:462
  19.1 0.3 %inner_merge.1.inner = f32[96,512]{1,0:T(8,128)S(1)} custom-call(f32[10,96,512]{2,1,0:T(8,128)S(1)} %get-tuple-element.22.mine, f32[10,96,512]{2,1,0:T(8,128)S(1)} %collective-permute-done.5.other), custom_call_target="tpu_custom_call" | custom-call | tf_op jit(solution)/shard_map/inner_merge/pallas_call | solution.py:474
  19.4 0.9 %psf.1 = (f32[1,128,512]{2,1,0:T(8,128)}, f32[128,512]{1,0:T(8,128)S(1)}, f32[8,128]{1,0:T(8,128)S(1)}) custom-call(bf16[16,512]{1,0:T(8,128)(2,1)S(1)} %collective-permute-done.3.first, bf16[16,512]{1,0:T(8,128)(2,1)S(1)} %collective-permute-done.4.second, f32[32,512]{1,0:T(8,128)S(1)} %get-tuple-element.20.edges, f32[96,512]{1,0:T(8,128)S(1)} %inner_merge.1.inner, ...), custom_call_target="tpu_custom_call" | custom-call | tf_op jit(solution)/shard_map/psf/pallas_call | solution.py:484
  20.3 1.5 %collective-permute-start.6 = (f32[72,256]{1,0:T(8,128)S(1)}, f32[72,256]{1,0:T(8,128)S(1)}, u32[]{:S(2)}, u32[]{:S(2)}) collective-permute-start(f32[72,256]{1,0:T(8,128)S(1)} %bitcast.11), channel_id=1, source_target_pairs={{0,1},{1,0},{2,3},{3,2},{4,5},{5,4},{6,7},{7,6},{8,9},{9,8},{10,11... | collective-permute-start | bytes 221192 | tf_op jit(solution)/shard_map/ppermute | solution.py:390
  21.8 1.8 %collective-permute-start.8 = (f32[8,128]{1,0:T(8,128)S(1)}, f32[8,128]{1,0:T(8,128)S(1)}, u32[]{:S(2)}, u32[]{:S(2)}) collective-permute-start(f32[8,128]{1,0:T(8,128)S(1)} %get-tuple-element.25.power), channel_id=1, source_target_pairs={{0,4},{1,5},{2,7},{3,6},{4,0},{5,1},{6,3},{7,2},{8,12},{9,13},{10,... | collective-permute-start | bytes 12296 | tf_op jit(solution)/shard_map/ppermute | solution.py:513
  23.6 1.8 %collective-permute-done.8 = f32[8,128]{1,0:T(8,128)S(1)} collective-permute-done((f32[8,128]{1,0:T(8,128)S(1)}, f32[8,128]{1,0:T(8,128)S(1)}, u32[]{:S(2)}, u32[]{:S(2)}) %collective-permute-start.8) | collective-permute-done | bytes 4128 | tf_op jit(solution)/shard_map/ppermute | solution.py:513
  25.4 0.0 collective-permute-start.9
  25.4 1.2 %collective-permute-done.9 = f32[8,128]{1,0:T(8,128)S(1)} collective-permute-done((f32[8,128]{1,0:T(8,128)S(1)}, f32[8,128]{1,0:T(8,128)S(1)}, u32[]{:S(2)}, u32[]{:S(2)}) %collective-permute-start.9) | collective-permute-done | bytes 4128 | tf_op jit(solution)/shard_map/ppermute | solution.py:514
  26.6 0.0 collective-permute-done.6.refs_0_
  26.6 2.0 %collective-permute-start.10 = (f32[2,8,128]{2,1,0:T(8,128)S(1)}, f32[2,8,128]{2,1,0:T(8,128)S(1)}, u32[]{:S(2)}, u32[]{:S(2)}) collective-permute-start(f32[2,8,128]{2,1,0:T(8,128)S(1)} %pad_maximum_fusion), channel_id=1, source_target_pairs={{0,8},{4,12},{8,0},{12,4},{1,9},{5,13},{9,1},{13,5},{2,10},{6,14},... | collective-permute-start | bytes 24584 | tf_op jit(solution)/shard_map/ppermute | solution.py:385
  28.6 2.6 %collective-permute-done.10 = f32[2,8,128]{2,1,0:T(8,128)S(1)} collective-permute-done((f32[2,8,128]{2,1,0:T(8,128)S(1)}, f32[2,8,128]{2,1,0:T(8,128)S(1)}, u32[]{:S(2)}, u32[]{:S(2)}) %collective-permute-start.10) | collective-permute-done | bytes 8224 | tf_op jit(solution)/shard_map/ppermute | solution.py:385
  31.2 0.9 %detection.1 = f32[128,256]{1,0:T(8,128)} custom-call(f32[128,512]{1,0:T(8,128)S(1)} %get-tuple-element.24.energy, f32[72,256]{1,0:T(8,128)S(1)} %collective-permute-done.6.refs_0_, f32[72,256]{1,0:T(8,128)S(1)} %collective-permute-done.7.refs_1_, f32[2,8,128]{2,1,0:T(8,128)S(1)} %fusion.1.refs_2_), custom_call_target="tpu_custom_call" | custom-call | tf_op jit(solution)/shard_map/detection/pallas_call | solution.py:527
  (13 shorter events, 0.0 us)
Async XLA Ops:
  1.7 10.1 %collective-permute-start.1 = (bf16[10,16,512]{2,1,0:T(8,128)(2,1)S(1)}, bf16[10,16,512]{2,1,0:T(8,128)(2,1)S(1)}, u32[]{:S(2)}, u32[]{:S(2)}) collective-permute-start(bf16[10,16,512]{2,1,0:T(8,128)(2,1)S(1)} %get-tuple-element.26), channel_id=1, source_target_pairs={{0,2},{2,0},{4,8},{6,10},{8,4},{10,6},{12,14},{14,12},{1,3},{3,1},... | collective-permute-start | bytes 491528 | tf_op jit(solution)/shard_map/ppermute | solution.py:381
  2.2 9.6 %collective-permute-start = (bf16[10,16,512]{2,1,0:T(8,128)(2,1)S(1)}, bf16[10,16,512]{2,1,0:T(8,128)(2,1)S(1)}, u32[]{:S(2)}, u32[]{:S(2)}) collective-permute-start(bf16[10,16,512]{2,1,0:T(8,128)(2,1)S(1)} %get-tuple-element.27), channel_id=1, source_target_pairs={{0,4},{2,6},{4,0},{6,2},{8,12},{10,14},{12,8},{14,10},{1,5},{3,7},... | collective-permute-start | bytes 491528 | tf_op jit(solution)/shard_map/ppermute | solution.py:381
  12.9 2.2 %collective-permute-start.2 = (f32[10,32,512]{2,1,0:T(8,128)S(1)}, f32[10,32,512]{2,1,0:T(8,128)S(1)}, u32[]{:S(2)}, u32[]{:S(2)}) collective-permute-start(f32[10,32,512]{2,1,0:T(8,128)S(1)} %edge_visits.1.mine), channel_id=1, source_target_pairs={{0,2},{2,0},{1,3},{3,1},{4,6},{6,4},{5,7},{7,5},{8,10},{10,8},{9,1... | collective-permute-start | bytes 1966088 | tf_op jit(solution)/shard_map/ppermute | solution.py:459
  15.1 4.0 %collective-permute-start.5 = (f32[10,96,512]{2,1,0:T(8,128)S(1)}, f32[10,96,512]{2,1,0:T(8,128)S(1)}, u32[]{:S(2)}, u32[]{:S(2)}) collective-permute-start(f32[10,96,512]{2,1,0:T(8,128)S(1)} %get-tuple-element.22.mine), channel_id=1, source_target_pairs={{0,2},{2,0},{1,3},{3,1},{4,6},{6,4},{5,7},{7,5},{8,10},{10,8},{9,1... | collective-permute-start | bytes 5898248 | tf_op jit(solution)/shard_map/ppermute | solution.py:462
  15.4 4.1 %collective-permute-start.3 = (bf16[16,512]{1,0:T(8,128)(2,1)S(1)}, bf16[16,512]{1,0:T(8,128)(2,1)S(1)}, u32[]{:S(2)}, u32[]{:S(2)}) collective-permute-start(bf16[16,512]{1,0:T(8,128)(2,1)S(1)} %get-tuple-element.18), channel_id=1, source_target_pairs={{0,4},{2,6},{4,0},{6,2},{8,12},{10,14},{12,8},{14,10},{1,5},{3,7},... | collective-permute-start | bytes 49160 | tf_op jit(solution)/shard_map/ppermute | solution.py:381
  15.6 3.8 %copy-start = (f32[1,31]{1,0:T(1,128)S(1)}, f32[1,31]{1,0:T(1,128)}, u32[]{:S(2)}) copy-start(f32[1,31]{1,0:T(1,128)} %row_taps.1) | copy-start | bytes 376
  15.6 3.8 %copy-start.1 = (f32[1,31]{1,0:T(1,128)S(1)}, f32[1,31]{1,0:T(1,128)}, u32[]{:S(2)}) copy-start(f32[1,31]{1,0:T(1,128)} %col_taps.1) | copy-start | bytes 376
  15.6 3.8 %collective-permute-start.4 = (bf16[16,512]{1,0:T(8,128)(2,1)S(1)}, bf16[16,512]{1,0:T(8,128)(2,1)S(1)}, u32[]{:S(2)}, u32[]{:S(2)}) collective-permute-start(bf16[16,512]{1,0:T(8,128)(2,1)S(1)} %get-tuple-element.19), channel_id=1, source_target_pairs={{0,2},{2,0},{4,8},{6,10},{8,4},{10,6},{12,14},{14,12},{1,3},{3,1},... | collective-permute-start | bytes 49160 | tf_op jit(solution)/shard_map/ppermute | solution.py:381
  20.3 6.3 %collective-permute-start.6 = (f32[72,256]{1,0:T(8,128)S(1)}, f32[72,256]{1,0:T(8,128)S(1)}, u32[]{:S(2)}, u32[]{:S(2)}) collective-permute-start(f32[72,256]{1,0:T(8,128)S(1)} %bitcast.11), channel_id=1, source_target_pairs={{0,1},{1,0},{2,3},{3,2},{4,5},{5,4},{6,7},{7,6},{8,9},{9,8},{10,11... | collective-permute-start | bytes 221192 | tf_op jit(solution)/shard_map/ppermute | solution.py:390
  21.8 3.6 %collective-permute-start.8 = (f32[8,128]{1,0:T(8,128)S(1)}, f32[8,128]{1,0:T(8,128)S(1)}, u32[]{:S(2)}, u32[]{:S(2)}) collective-permute-start(f32[8,128]{1,0:T(8,128)S(1)} %get-tuple-element.25.power), channel_id=1, source_target_pairs={{0,4},{1,5},{2,7},{3,6},{4,0},{5,1},{6,3},{7,2},{8,12},{9,13},{10,... | collective-permute-start | bytes 12296 | tf_op jit(solution)/shard_map/ppermute | solution.py:513
  25.4 1.2 %collective-permute-start.9 = (f32[8,128]{1,0:T(8,128)S(1)}, f32[8,128]{1,0:T(8,128)S(1)}, u32[]{:S(2)}, u32[]{:S(2)}) collective-permute-start(f32[8,128]{1,0:T(8,128)S(1)} %collective-permute-done.8), channel_id=1, source_target_pairs={{0,2},{2,0},{1,3},{3,1},{4,6},{6,4},{5,7},{7,5},{8,10},{10,8},{9,1... | collective-permute-start | bytes 12296 | tf_op jit(solution)/shard_map/ppermute | solution.py:514
  26.6 4.6 %collective-permute-start.10 = (f32[2,8,128]{2,1,0:T(8,128)S(1)}, f32[2,8,128]{2,1,0:T(8,128)S(1)}, u32[]{:S(2)}, u32[]{:S(2)}) collective-permute-start(f32[2,8,128]{2,1,0:T(8,128)S(1)} %pad_maximum_fusion), channel_id=1, source_target_pairs={{0,8},{4,12},{8,0},{12,4},{1,9},{5,13},{9,1},{13,5},{2,10},{6,14},... | collective-permute-start | bytes 24584 | tf_op jit(solution)/shard_map/ppermute | solution.py:385
  28.6 2.6 %collective-permute-start.7 = (f32[72,256]{1,0:T(8,128)S(1)}, f32[72,256]{1,0:T(8,128)S(1)}, u32[]{:S(2)}, u32[]{:S(2)}) collective-permute-start(f32[72,256]{1,0:T(8,128)S(1)} %collective-permute-done.6.refs_0_), channel_id=1, source_target_pairs={{0,2},{2,0},{1,3},{3,1},{4,6},{6,4},{5,7},{7,5},{8,10},{10,8},{9,1... | collective-permute-start | bytes 221192 | tf_op jit(solution)/shard_map/ppermute | solution.py:518

commit v5 on v4

v5 whole, which is shorter than its diff:
```python
import functools

import jax
import jax.numpy as jnp
from jax import lax
from jax.experimental import pallas as pl
from jax.experimental.pallas import tpu as pltpu
from jax.sharding import PartitionSpec as P

HALF = 15
REJECT = 4
TAPS = 31
EDGE = 16
LANES = 128
SENTINEL = 1e30
EPSILON = 1e-05
F32 = jnp.float32
BF16 = jnp.bfloat16
MIB = 1024 * 1024
UNROLL = 2


def split2(value):
    high = value.astype(BF16)
    return high, (value - high.astype(F32)).astype(BF16)


def band_rows(taps, rows):
    return pltpu.roll(
        jnp.broadcast_to(pltpu.roll(taps, 1, 1), (rows, LANES)), 0, 1, stride=1, stride_axis=0
    )


def around_matrix(taps):
    base = pltpu.roll(taps, LANES - HALF, 1)
    return pltpu.roll(jnp.broadcast_to(base, (LANES, LANES)), 0, 1, stride=1, stride_axis=0)


def square_masks():
    row = lax.broadcasted_iota(jnp.int32, (LANES, LANES), 0)
    col = lax.broadcasted_iota(jnp.int32, (LANES, LANES), 1)
    return row, col


def col_matrix(taps):
    return jnp.concatenate(split2(row_matrix(taps)), axis=0)


def row_matrix(taps):
    square = band_rows(taps, LANES)
    row, col = square_masks()
    return jnp.concatenate(
        [jnp.where(col > row, square, 0.0), jnp.where(col < row, square, 0.0)], axis=1
    )


def col_conv(value, matrix):
    rows, cols = value.shape
    tiles = cols // LANES
    turned = pltpu.roll(value, EDGE, 1)
    first = turned[:, :LANES]
    lane = lax.broadcasted_iota(jnp.int32, (rows, LANES), 1)
    wide = jnp.concatenate(
        [jnp.where(lane < EDGE, 0.0, first), turned[:, LANES:], jnp.where(lane < EDGE, first, 0.0)],
        axis=1,
    )
    parts = [
        part[:, n * LANES : (n + 2) * LANES] for part in split2(wide) for n in range(tiles)
    ]
    product = lax.dot_general(
        jnp.concatenate(parts, axis=0),
        matrix,
        (((1,), (1,)), ((), ())),
        preferred_element_type=F32,
    )

    def piece(n, side):
        return product[n * rows : (n + 1) * rows, side * LANES : (side + 1) * LANES]

    return jnp.concatenate(
        [piece(n, 0) + (piece(n, 1) + piece(tiles + n, 0)) for n in range(tiles)], axis=1
    )


def ordered(values, pairs, first, second):
    values = list(values)
    for i, j in pairs:
        values[i], values[j] = first(values[i], values[j]), second(values[i], values[j])
    return values


def foremost(groups, first, second):
    best = None
    while groups:
        group, groups = groups[0], groups[1:]
        if len(group) == 2 and groups and len(groups[0]) == 2:
            group, groups = [*group, *groups[0]], groups[1:]
            group = ordered(group, ((0, 2), (1, 3), (1, 2)), first, second)
        if best is None:
            best = group
        elif len(best) < REJECT:
            best = best + group
            pairs = [(j, j + 1) for i in range(len(best)) for j in range(len(best) - 1 - i)]
            best = ordered(best, pairs, first, second)[:REJECT]
        else:
            best = list(best)
            for i, value in enumerate(group):
                best[REJECT - 1 - i] = first(best[REJECT - 1 - i], value)
            best = ordered(best, ((0, 2), (1, 3), (0, 1), (2, 3)), first, second)
    return best


def hold(visit, results, masks, upper, lower, totals, counts):
    masks = [mask for mask in masks]
    usable = [mask == 1 for mask in masks]
    tops = [jnp.where(use, value, -SENTINEL) for use, value in zip(usable, results)]
    ends = [jnp.where(use, value, SENTINEL) for use, value in zip(usable, results)]
    if len(results) == 2:
        tops = ordered(tops, ((0, 1),), jnp.maximum, jnp.minimum)
        ends = ordered(ends, ((0, 1),), jnp.minimum, jnp.maximum)
    for i in range(len(results)):
        upper[visit + i] = tops[i]
        lower[visit + i] = ends[i]
    totals[...] += sum(jnp.where(use, value, 0.0) for use, value in zip(usable, results))
    counts[...] += sum(masks)


def sort_visits(at_once, upper, lower, totals, counts, start, lists):
    visits, _, cols = upper.shape
    rows = lists.shape[1]
    width = 2 * LANES

    def body(step, carry):
        at = pl.ds(pl.multiple_of(step * 8, 8), 8)
        source = pl.ds(pl.multiple_of(step * 8 + start, 8), 8)
        for left in range(0, cols, width):
            lanes = pl.ds(left, width)
            for place, values, first, second in (
                (0, upper, jnp.maximum, jnp.minimum),
                (REJECT, lower, jnp.minimum, jnp.maximum),
            ):
                groups = [
                    [values[v + i, source, lanes] for i in range(at_once)]
                    for v in range(0, visits, at_once)
                ]
                for i, value in enumerate(foremost(groups, first, second)):
                    lists[place + i, at, lanes] = value
            lists[2 * REJECT, at, lanes] = totals[source, lanes]
            lists[2 * REJECT + 1, at, lanes] = counts[source, lanes].astype(F32)
        return carry

    lax.fori_loop(0, rows // 8, body, 0)


def inner_kernel(
    groups_h,
    points_h,
    images_h,
    mask_h,
    row_taps_h,
    col_taps_h,
    early_lists,
    late_lists,
    part,
    edge_m,
    col_m,
    edge_mask,
    groups,
    points,
    row_taps,
    col_taps,
    images,
    mask,
    taps,
    row_m,
    values,
    upper,
    lower,
    totals,
    counts,
    small_sems,
    image_sems,
    mask_sems,
):
    visits, height, _ = images.shape
    small = [
        pltpu.make_async_copy(source, target, small_sems.at[i])
        for i, (source, target) in enumerate(
            ((groups_h, groups), (points_h, points), (row_taps_h, row_taps), (col_taps_h, col_taps))
        )
    ]

    middle = visits // 2 // UNROLL * UNROLL if visits % UNROLL == 0 else visits // 2

    def image_copy(i):
        at = pl.ds(0, middle) if i == 0 else pl.ds(middle, visits - middle)
        return pltpu.make_async_copy(images_h.at[0, at], images.at[at], image_sems.at[i])

    def mask_copy(i):
        at = pl.ds(0, middle) if i == 0 else pl.ds(middle, visits - middle)
        return pltpu.make_async_copy(mask_h.at[0, at], mask.at[at], mask_sems.at[i])

    for copy in small:
        copy.start()
    for i in range(2):
        image_copy(i).start()
        mask_copy(i).start()
    taps[...] = jnp.zeros_like(taps)
    totals[...] = jnp.zeros_like(totals)
    counts[...] = jnp.zeros_like(counts)
    row, col = square_masks()
    near = jnp.abs(row - col) <= HALF
    for copy in small:
        copy.wait()
    def build(v, slot):
        taps[slot : slot + 1, 0:TAPS] = row_taps[v]
        taps[slot + 8 : slot + 9, 0:TAPS] = col_taps[v]
        scale = points[0, groups[0, v]]
        square = around_matrix(taps[slot : slot + 1, :])
        row_m[v] = jnp.concatenate(split2(jnp.where(near, square, 0.0)), axis=1)
        far = jnp.where(near, 0.0, square)
        far = pltpu.roll(jnp.concatenate([far[:EDGE], far[height - EDGE :]], axis=0), EDGE, 1)
        edge_m[v] = jnp.concatenate(split2(far), axis=0)
        col_m[v] = col_matrix(taps[slot + 8 : slot + 9, :] * scale)

    def smear(v):
        image = images[v]
        smeared = jnp.dot(
            row_m[v], jnp.concatenate([image, image], axis=0), preferred_element_type=F32
        )
        values[v] = smeared[EDGE : height - EDGE]
        part[v, 0:EDGE] = smeared[:EDGE]
        part[v, EDGE : 2 * EDGE] = smeared[height - EDGE :]

    def convolve(v, number):
        results = [col_conv(values[v + i], col_m[v + i]) for i in range(number)]
        masks = [mask[v + i, EDGE : height - EDGE] for i in range(number)]
        hold(v, results, masks, upper, lower, totals, counts)
        for i in range(number):
            edge_mask[v + i, 0:EDGE] = mask[v + i, 0:EDGE]
            edge_mask[v + i, EDGE : 2 * EDGE] = mask[v + i, height - EDGE :]

    at_once = UNROLL if visits % UNROLL == 0 else 1
    steps = visits // at_once

    def work(step, most=None):
        convolve(step * at_once, at_once)
        for i in range(at_once):
            if most is None or most >= 1:
                smear((step + 1) * at_once + i)
        for i in range(at_once):
            if most is None or most >= 2:
                build((step + 2) * at_once + i, 16 * i)

    for step in range(min(2, steps)):
        for i in range(at_once):
            build(step * at_once + i, 16 * i)
    image_copy(0).wait()
    mask_copy(0).wait()
    for i in range(at_once):
        smear(i)
    ready = max(min(middle // at_once - 1, steps - 2), 0)

    def body(step, carry):
        work(step)
        return carry

    lax.fori_loop(0, ready, body, 0)
    image_copy(1).wait()
    mask_copy(1).wait()
    lax.fori_loop(ready, steps - 2, body, 0)
    for step in range(max(steps - 2, 0), steps):
        work(step, steps - 1 - step)
    held = (at_once, upper, lower, totals, counts)
    sort_visits(*held, 0, early_lists)
    sort_visits(*held, early_lists.shape[1], late_lists)


def at_ends(first, second):
    strip = lax.axis_index("sky")
    even = lax.rem(strip, 2) == 0
    top, bottom = strip == 0, strip == lax.axis_size("sky") - 1
    above, below = jnp.where(even, second, first), jnp.where(even, first, second)
    return (
        jnp.where(top, jnp.zeros_like(above), above),
        jnp.where(bottom, jnp.zeros_like(below), below),
    )


def edge_kernel(
    first, second, part, edge_m, col_m, edge_mask, lists, values, upper, lower, totals, counts
):
    visits, _, cols = values.shape
    for visit in range(visits):
        before, after = at_ends(first[visit], second[visit])
        window = jnp.concatenate([before, after], axis=0)
        both = jnp.dot(edge_m[visit, :, 0 : 2 * EDGE], window, preferred_element_type=F32)
        values[visit] = part[visit] + (both[: 2 * EDGE] + both[2 * EDGE :])
    at_once = UNROLL if visits % UNROLL == 0 else 1
    totals[...] = jnp.zeros_like(totals)
    counts[...] = jnp.zeros_like(counts)
    for visit in range(0, visits, at_once):
        results = [col_conv(values[visit + i], col_m[visit + i]) for i in range(at_once)]
        masks = [edge_mask[visit + i] for i in range(at_once)]
        hold(visit, results, masks, upper, lower, totals, counts)
    sort_visits(at_once, upper, lower, totals, counts, 0, lists)


def merge(mine, other, coadd, start):
    def body(step, carry):
        at = pl.ds(pl.multiple_of(step * 8, 8), 8)
        upper, lower = 0.0, 0.0
        for i in range(REJECT):
            j = REJECT - 1 - i
            upper = upper + jnp.maximum(mine[i, at, :], other[j, at, :])
            lower = lower + jnp.minimum(mine[REJECT + i, at, :], other[REJECT + j, at, :])
        total = mine[2 * REJECT, at, :] + other[2 * REJECT, at, :]
        count = mine[2 * REJECT + 1, at, :] + other[2 * REJECT + 1, at, :]
        coadd[pl.ds(pl.multiple_of(step * 8 + start, 8), 8), :] = (total - upper - lower) / (
            count - 2 * REJECT
        )
        return carry

    lax.fori_loop(0, mine.shape[1] // 8, body, 0)


def edge_merge_kernel(mine, other, coadd, send_first, send_second):
    merge(mine, other, coadd, 0)
    even = lax.rem(lax.axis_index("sky"), 2) == 0
    top, bottom = coadd[0:EDGE], coadd[EDGE : 2 * EDGE]
    send_first[...] = jnp.where(even, bottom, top).astype(BF16)
    send_second[...] = jnp.where(even, top, bottom).astype(BF16)


def lane_sums(squares):
    rows, cols = squares.shape
    part = jnp.sum(squares.reshape(rows // 8, 8, cols), axis=0)
    return sum(part[:, n * LANES : (n + 1) * LANES] for n in range(cols // LANES))


def inner_psf_kernel(
    early_mine,
    early_other,
    late_mine,
    late_other,
    edges,
    row_taps,
    col_taps,
    coadd,
    energy,
    power,
    part,
    edge_m,
    col_m,
    taps,
):
    height = coadd.shape[1]
    merge(early_mine, early_other, coadd.at[0], EDGE)
    merge(late_mine, late_other, coadd.at[0], EDGE + early_mine.shape[1])
    coadd[0, 0:EDGE] = edges[0:EDGE]
    coadd[0, height - EDGE : height] = edges[EDGE : 2 * EDGE]
    taps[...] = jnp.zeros_like(taps)
    taps[0:1, 0:TAPS] = row_taps[...]
    taps[8:9, 0:TAPS] = col_taps[...]
    row, col = square_masks()
    near = jnp.abs(row - col) <= HALF
    square = around_matrix(taps[0:1, :])
    row_h, row_l = split2(jnp.where(near, square, 0.0))
    far = jnp.where(near, 0.0, square)
    far = pltpu.roll(jnp.concatenate([far[:EDGE], far[height - EDGE :]], axis=0), EDGE, 1)
    edge_m[...] = jnp.concatenate(split2(far), axis=0)
    matrix = col_matrix(taps[8:9, :])
    col_m[...] = matrix
    high, low = split2(coadd[0])
    smeared = jnp.dot(
        jnp.concatenate([row_h, row_l], axis=1),
        jnp.concatenate([high, high], axis=0),
        preferred_element_type=F32,
    ) + jnp.dot(row_h, low, preferred_element_type=F32)
    part[0:EDGE] = smeared[:EDGE]
    part[EDGE : 2 * EDGE] = smeared[height - EDGE :]
    filtered = col_conv(smeared[EDGE : height - EDGE], matrix)
    squares = filtered * filtered
    energy[...] = squares
    power[...] = lane_sums(squares)


def edge_psf_kernel(first, second, part, edge_m, col_m, inner, inner_power, energy, power, send):
    before, after = at_ends(first[...], second[...])
    window = jnp.concatenate([before, after], axis=0)
    both = jnp.dot(edge_m[:, 0 : 2 * EDGE], window, preferred_element_type=F32)
    filtered = col_conv(part[...] + (both[: 2 * EDGE] + both[2 * EDGE :]), col_m[...])
    squares = filtered * filtered
    energy[...] = squares
    total = inner_power[...] + lane_sums(squares)
    power[...] = total
    others, rows, width = send.shape
    half = rows - EDGE - 8
    own, core = lax.axis_index("band"), lax.axis_index("exp")
    for k in range(others):
        band = lax.rem(own + k + 1, others + 1)
        lanes = pl.ds(pl.multiple_of(band * width, width), width)
        send[k, 0:EDGE] = energy[pl.ds(pl.multiple_of(core * EDGE, EDGE), EDGE), lanes]
        send[k, EDGE : EDGE + half] = inner[pl.ds(pl.multiple_of(core * half, half), half), lanes]
        for n in range(width // LANES):
            send[k, EDGE + half : rows, n * LANES : (n + 1) * LANES] = total


def final_kernel(pixels, edges, inner, *refs):
    others = (len(refs) - 2) // 2
    mine, theirs, sums, detection = refs[:others], refs[others : 2 * others], refs[-2], refs[-1]
    height, width = detection.shape
    half = inner.shape[0] // 2
    lanes = pl.ds(pl.multiple_of(lax.axis_index("band") * width, width), width)
    scales = [1.0 / (jnp.sum(sums[i]) / pixels + EPSILON) for i in range(others + 1)]
    core = lax.axis_index("exp")
    for place, parts in ((core, mine), (1 - core, theirs)):
        for own, rows, to, start in (
            (edges, EDGE, place * (height - EDGE), 0),
            (inner, half, EDGE + place * half, EDGE),
        ):
            total = own[pl.ds(pl.multiple_of(place * rows, rows), rows), lanes] * scales[0]
            for i in range(others):
                total = total + parts[i][start : start + rows, :] * scales[i + 1]
            detection[pl.ds(pl.multiple_of(to, EDGE), rows), :] = total


def vmem(shape, dtype=F32):
    return jax.ShapeDtypeStruct(shape, dtype)


VMEM = pl.BlockSpec(memory_space=pltpu.VMEM)
SMEM = pl.BlockSpec(memory_space=pltpu.SMEM)
HBM = pl.BlockSpec(memory_space=pltpu.HBM)
PARAMS = pltpu.CompilerParams(vmem_limit_bytes=24 * MIB)


def paired(value, start):
    strips, cores = lax.axis_size("sky"), lax.axis_size("exp")
    partner = {}
    for i in range(start, strips - 1, 2):
        partner[i], partner[i + 1] = i + 1, i
    pairs = []
    for strip in range(strips):
        for core in range(cores):
            to = (partner[strip], core) if strip in partner else (strip, cores - 1 - core)
            pairs.append((strip * cores + core, to[0] * cores + to[1]))
    return lax.ppermute(value, ("sky", "exp"), pairs)


def flipped(value, axis, bits):
    return lax.ppermute(value, axis, [(i, i ^ bits) for i in range(lax.axis_size(axis))])


def turned(value, axis, step):
    size = lax.axis_size(axis)
    return lax.ppermute(value, axis, [(i, (i + step) % size) for i in range(size)])


def on_device(images, valid_mask, row_kernel, col_kernel, exp_group, zero_point, psf_row, psf_col):
    _, visits, height, cols = images.shape
    inner = height - 2 * EDGE
    bands = lax.axis_size("band")
    strips = lax.axis_size("sky")
    even = lax.rem(lax.axis_index("sky"), 2) == 0
    far = jnp.where(even, height - EDGE, 0)
    first = paired(lax.dynamic_slice_in_dim(images[0], far, EDGE, 1), 0)
    second = paired(lax.dynamic_slice_in_dim(images[0], height - EDGE - far, EDGE, 1), 1)

    lists = 2 * REJECT + 2
    early = inner // 16 * 8
    early_lists, late_lists, part, edge_m, col_m, edge_mask = pl.pallas_call(
        inner_kernel,
        in_specs=[HBM] * 6,
        out_specs=[VMEM] * 6,
        out_shape=[
            vmem((lists, early, cols)),
            vmem((lists, inner - early, cols)),
            vmem((visits, 2 * EDGE, cols)),
            vmem((visits, 4 * EDGE, LANES), BF16),
            vmem((visits, 2 * LANES, 2 * LANES), BF16),
            vmem((visits, 2 * EDGE, cols), jnp.int32),
        ],
        scratch_shapes=[
            pltpu.SMEM((1, visits), jnp.int32),
            pltpu.SMEM(zero_point.shape, F32),
            pltpu.VMEM((visits, 1, TAPS), F32),
            pltpu.VMEM((visits, 1, TAPS), F32),
            pltpu.VMEM((visits, height, cols), BF16),
            pltpu.VMEM((visits, height, cols), jnp.int32),
            pltpu.VMEM((16 * UNROLL, LANES), F32),
            pltpu.VMEM((visits, LANES, 2 * LANES), BF16),
            pltpu.VMEM((visits, inner, cols), F32),
            pltpu.VMEM((visits, inner, cols), F32),
            pltpu.VMEM((visits, inner, cols), F32),
            pltpu.VMEM((inner, cols), F32),
            pltpu.VMEM((inner, cols), jnp.int32),
            pltpu.SemaphoreType.DMA((4,)),
            pltpu.SemaphoreType.DMA((2,)),
            pltpu.SemaphoreType.DMA((2,)),
        ],
        compiler_params=PARAMS,
        cost_estimate=pl.CostEstimate(
            flops=visits * height * cols * 4096,
            bytes_accessed=visits * height * cols * 6,
            transcendentals=0,
        ),
        name="inner_visits",
    )(
        *(
            pltpu.with_memory_space_constraint(value, pltpu.HBM)
            for value in (
                exp_group,
                zero_point,
                images,
                valid_mask,
                row_kernel.transpose(1, 0, 2),
                col_kernel.transpose(1, 0, 2),
            )
        )
    )
    swap = [(0, 1), (1, 0)]
    held, first, second = lax.optimization_barrier((early_lists, first, second))
    early_other = lax.ppermute(held, "exp", swap)
    edge_lists = pl.pallas_call(
        edge_kernel,
        in_specs=[VMEM] * 6,
        out_specs=VMEM,
        out_shape=vmem((lists, 2 * EDGE, cols)),
        scratch_shapes=[pltpu.VMEM((visits, 2 * EDGE, cols), F32)] * 3
        + [pltpu.VMEM((2 * EDGE, cols), F32), pltpu.VMEM((2 * EDGE, cols), jnp.int32)],
        compiler_params=PARAMS,
        cost_estimate=pl.CostEstimate(
            flops=visits * height * cols * 6144, bytes_accessed=visits * cols * 256, transcendentals=0
        ),
        name="edge_visits",
    )(first, second, part, edge_m, col_m, edge_mask)
    edge_other = lax.ppermute(edge_lists, "exp", swap)

    held, _ = lax.optimization_barrier((late_lists, edge_other))
    late_other = lax.ppermute(held, "exp", swap)

    edges, send_first, send_second = pl.pallas_call(
        edge_merge_kernel,
        in_specs=[VMEM] * 2,
        out_specs=[VMEM] * 3,
        out_shape=[vmem((2 * EDGE, cols)), vmem((EDGE, cols), BF16), vmem((EDGE, cols), BF16)],
        compiler_params=PARAMS,
        name="edge_merge",
    )(edge_lists, edge_other)
    coadd_first = paired(send_first, 0)
    coadd_second = paired(send_second, 1)
    coadd_image, inner_energy, inner_power, psf_part, psf_edge_m, psf_col_m = pl.pallas_call(
        inner_psf_kernel,
        in_specs=[VMEM] * 7,
        out_specs=[VMEM] * 6,
        out_shape=[
            vmem((1, height, cols)),
            vmem((inner, cols)),
            vmem((8, LANES)),
            vmem((2 * EDGE, cols)),
            vmem((4 * EDGE, LANES), BF16),
            vmem((2 * LANES, 2 * LANES), BF16),
        ],
        scratch_shapes=[pltpu.VMEM((16, LANES), F32)],
        compiler_params=PARAMS,
        name="inner_psf",
    )(early_lists, early_other, late_lists, late_other, edges, psf_row, psf_col)

    width = cols // bands
    edge_energy, power, send = pl.pallas_call(
        edge_psf_kernel,
        in_specs=[VMEM] * 7,
        out_specs=[VMEM] * 3,
        out_shape=[
            vmem((2 * EDGE, cols)),
            vmem((8, LANES)),
            vmem((bands - 1, height // 2 + 8, width)),
        ],
        compiler_params=PARAMS,
        name="edge_psf",
    )(coadd_first, coadd_second, psf_part, psf_edge_m, psf_col_m, inner_energy, inner_power)

    mine = [turned(send[k - 1], "band", k) for k in range(1, bands)]
    held = [part[height // 2 :, :LANES] for part in mine]
    if strips == 4 and bands == 2 and lax.axis_size("exp") == 2:
        first_core = lax.axis_index("exp") == 0
        total = 0.0
        for bits in range(1, strips):
            pairs = []
            for strip in range(strips):
                for core in range(2):
                    for band in range(2):
                        to = (strip ^ bits, core, band ^ core)
                        pairs.append((4 * strip + 2 * core + band, 4 * to[0] + 2 * to[1] + to[2]))
            total = total + lax.ppermute(power, ("sky", "exp", "band"), pairs)
        total = total + jnp.where(first_core, power, held[0])
        theirs = [lax.ppermute(mine[0], "exp", swap)]
        total, _ = lax.optimization_barrier((total, theirs[0]))
        other = lax.ppermute(total, "exp", swap)
        sums = jnp.where(first_core, jnp.stack([total, other]), jnp.stack([other, total]))
    else:
        theirs = [lax.ppermute(part, "exp", swap) for part in mine]
        sums = lax.psum(jnp.stack([power] + held), "sky")
    pixels = height * strips * cols
    detection = pl.pallas_call(
        functools.partial(final_kernel, pixels),
        in_specs=[VMEM] * (2 * bands + 1),
        out_specs=VMEM,
        out_shape=vmem((height, width)),
        compiler_params=PARAMS,
        name="detection",
    )(edge_energy, inner_energy, *mine, *theirs, sums)
    return coadd_image, detection


def solution(mesh):
    placed = (
        P("band", "exp", ("patch", "sky"), None),
        P("band", "exp", ("patch", "sky"), None),
        P("band", "exp", None),
        P("band", "exp", None),
        P("band", "exp"),
        P("band", None),
        P("band", None),
        P("band", None),
    )
    return jax.shard_map(
        on_device,
        mesh=mesh,
        in_specs=placed,
        out_specs=(P("band", ("patch", "sky"), None), P(("patch", "sky"), "band")),
        check_vma=False,
    )
```

time: 32.3 us -> 30.2 us (0.935)
  waiting for transfers between devices: 10.9 us -> 7.52 us
  starting transfers between devices: 10.6 us -> 11.9 us
    ppermute x5 -> x7, waiting for transfers between devices: 8.81 us -> 5.87 us  [the longest x3 2.69 us: on_device(): total = total + lax.ppermute(power, ('sky', 'exp', 'band'), pairs)]
    ppermute x5 -> x7, starting transfers between devices: 3.88 us -> 5.09 us  [the longest x3 4.39 us: on_device(): total = total + lax.ppermute(power, ('sky', 'exp', 'band'), pairs)]
    ppermute x1, waiting for transfers between devices: 2.08 us -> 1.59 us  [on_device(): edge_other = lax.ppermute(edge_lists, 'exp', swap)]
    pallas_call x4 -> x3, Pallas kernels: 6.65 us -> 6.87 us  [the longest x1 5.26 us: on_device(): pl.pallas_call(inner_kernel, in_specs=[HBM] * 6, out_specs=[VMEM] * 6, ou...]
  transfers between devices with their start and end apart: 11 -> 13, of which waited for: 5 -> 7; matrix products, arithmetic and copies ran while one was open for 0% -> 0% of each run, Pallas kernels for 18% -> 22%
where the time goes in v5:
time: 30.2 us; the launch traced here: 30.1 us
  starting transfers between devices  11.9 us (39%)
  Pallas kernels  8.89 us (29%)
  waiting for transfers between devices  7.52 us (25%)
  local copies, waits for them, and re-layouts  1.04 us (3%)
  between operations  0.74 us (2%)
    pallas_call x1, Pallas kernels, on_device(): pl.pallas_call(inner_kernel, in_specs=[HBM] * 6, out_specs=[VMEM] * 6, ou...  5.26 us
    ppermute x4, starting transfers between devices, paired(): return lax.ppermute(value, ('sky', 'exp'), pairs)  5.18 us
    ppermute x3, starting transfers between devices, on_device(): total = total + lax.ppermute(power, ('sky', 'exp', 'band'), pairs)  4.39 us
    ppermute x3, waiting for transfers between devices, on_device(): total = total + lax.ppermute(power, ('sky', 'exp', 'band'), pairs)  2.69 us
    ppermute x1, waiting for transfers between devices, on_device(): edge_other = lax.ppermute(edge_lists, 'exp', swap)  1.59 us
    ppermute x1, starting transfers between devices, turned(): lax.ppermute(value, axis, [(i, (i + step) % size) for i in range(size)])  1.56 us
    ppermute x1, waiting for transfers between devices, on_device(): late_other = lax.ppermute(held, 'exp', swap)  1.41 us
    pallas_call x1, Pallas kernels, on_device(): pl.pallas_call(inner_psf_kernel, in_specs=[VMEM] * 7, out_specs=[VMEM] *...  1.22 us
  transfers between devices with their start and end apart: 13, of which 7 were waited for; matrix products, arithmetic and copies ran while one was open for 0% of the time, Pallas kernels for 22%

profile of v5, /device:TPU:0, one launch (start us, length us, event | category | flops | bytes accessed | tf_op | source)
XLA Modules:
  0.0 30.1 jit_solution(7465622670953886070)
XLA Ops:
  0.6 1.0 %dynamic-slice_bitcast_fusion = (bf16[10,16,512]{2,1,0:T(8,128)(2,1)S(1)}, bf16[10,16,512]{2,1,0:T(8,128)(2,1)S(1)}) fusion(bf16[1,10,128,512]{3,2,1,0:T(8,128)(2,1)} %images_h.1, s32[]{:T(128)S(6)} %select_n.25, s32[]{:T(128)S(6)} %select_n.24), kind=kLoop, calls=%fused_computation | loop fusion | bytes 655368 | tf_op jit(solution)/shard_map/dynamic_slice | solution.py:468
  1.7 0.5 %collective-permute-start.1 = (bf16[10,16,512]{2,1,0:T(8,128)(2,1)S(1)}, bf16[10,16,512]{2,1,0:T(8,128)(2,1)S(1)}, u32[]{:S(2)}, u32[]{:S(2)}) collective-permute-start(bf16[10,16,512]{2,1,0:T(8,128)(2,1)S(1)} %get-tuple-element.48), channel_id=1, source_target_pairs={{0,2},{2,0},{4,8},{6,10},{8,4},{10,6},{12,14},{14,12},{1,3},{3,1},... | collective-permute-start | bytes 491528 | tf_op jit(solution)/shard_map/ppermute | solution.py:448
  2.2 4.1 %collective-permute-start = (bf16[10,16,512]{2,1,0:T(8,128)(2,1)S(1)}, bf16[10,16,512]{2,1,0:T(8,128)(2,1)S(1)}, u32[]{:S(2)}, u32[]{:S(2)}) collective-permute-start(bf16[10,16,512]{2,1,0:T(8,128)(2,1)S(1)} %get-tuple-element.49), channel_id=1, source_target_pairs={{0,4},{2,6},{4,0},{6,2},{8,12},{10,14},{12,8},{14,10},{1,5},{3,7},... | collective-permute-start | bytes 491528 | tf_op jit(solution)/shard_map/ppermute | solution.py:448
  6.3 5.3 %inner_visits.1 = (f32[10,48,512]{2,1,0:T(8,128)S(1)}, f32[10,48,512]{2,1,0:T(8,128)S(1)}, f32[10,32,512]{2,1,0:T(8,128)S(1)}, bf16[10,64,128]{2,1,0:T(8,128)(2,...) custom-call(s32[1,10]{1,0:T(1,128)} %groups_h.1, f32[1,16]{1,0:T(1,128)} %points_h.1, ...), custom_call_target="tpu_custom_call" | custom-call | flops 2684354560 | bytes 3932160 | tf_op jit(solution)/shard_map/inner_visits/pallas_call | solution.py:472
  11.6 1.0 %edge_visits.1.mine = f32[10,32,512]{2,1,0:T(8,128)S(1)} custom-call(bf16[10,16,512]{2,1,0:T(8,128)(2,1)S(1)} %collective-permute-done.first, bf16[10,16,512]{2,1,0:T(8,128)(2,1)S(1)} %collective-permute-done.1.second, f32[10,32,512]{2,1,0:T(8,128)S(1)} %get-tuple-element.30.part, bf16[10,64,128]{2,1,0:T(8,128)(2,1)S(1)} %get-tuple-element.31.edge_m, ...), custom_call_target="tpu_custom_call" | custom-call | flops 4026531840 | bytes 1310720 | tf_op jit(solution)/shard_map/edge_visits/pallas_call | solution.py:525
  12.8 0.5 %collective-permute-start.2 = (f32[10,48,512]{2,1,0:T(8,128)S(1)}, f32[10,48,512]{2,1,0:T(8,128)S(1)}, u32[]{:S(2)}, u32[]{:S(2)}) collective-permute-start(f32[10,48,512]{2,1,0:T(8,128)S(1)} %get-tuple-element.26.early_mine), channel_id=1, source_target_pairs={{0,2},{2,0},{1,3},{3,1},{4,6},{6,4},{5,7},{7,5},{8,10},{10,8},{9,1... | collective-permute-start | bytes 2949128 | tf_op jit(solution)/shard_map/ppermute | solution.py:524
  13.3 1.6 %collective-permute-done.3.other = f32[10,32,512]{2,1,0:T(8,128)S(1)} collective-permute-done((f32[10,32,512]{2,1,0:T(8,128)S(1)}, f32[10,32,512]{2,1,0:T(8,128)S(1)}, u32[]{:S(2)}, u32[]{:S(2)}) %collective-permute-start.3) | collective-permute-done | bytes 655392 | tf_op jit(solution)/shard_map/ppermute | solution.py:538
  14.8 0.1 collective-permute-start.4
  15.0 0.1 edge_merge.1
  15.1 0.4 %collective-permute-start.5 = (bf16[16,512]{1,0:T(8,128)(2,1)S(1)}, bf16[16,512]{1,0:T(8,128)(2,1)S(1)}, u32[]{:S(2)}, u32[]{:S(2)}) collective-permute-start(bf16[16,512]{1,0:T(8,128)(2,1)S(1)} %get-tuple-element.37), channel_id=1, source_target_pairs={{0,4},{2,6},{4,0},{6,2},{8,12},{10,14},{12,8},{14,10},{1,5},{3,7},... | collective-permute-start | bytes 49160 | tf_op jit(solution)/shard_map/ppermute | solution.py:448
  15.5 0.1 collective-permute-start.6
  15.6 0.6 %collective-permute-done.2.early_other = f32[10,48,512]{2,1,0:T(8,128)S(1)} collective-permute-done((f32[10,48,512]{2,1,0:T(8,128)S(1)}, f32[10,48,512]{2,1,0:T(8,128)S(1)}, u32[]{:S(2)}, u32[]{:S(2)}) %collective-permute-start.2) | collective-permute-done | bytes 983072 | tf_op jit(solution)/shard_map/ppermute | solution.py:524
  16.2 1.4 %collective-permute-done.4.late_other = f32[10,48,512]{2,1,0:T(8,128)S(1)} collective-permute-done((f32[10,48,512]{2,1,0:T(8,128)S(1)}, f32[10,48,512]{2,1,0:T(8,128)S(1)}, u32[]{:S(2)}, u32[]{:S(2)}) %collective-permute-start.4) | collective-permute-done | bytes 983072 | tf_op jit(solution)/shard_map/ppermute | solution.py:541
  17.7 1.2 %inner_psf.1 = (f32[1,128,512]{2,1,0:T(8,128)}, f32[96,512]{1,0:T(8,128)S(1)}, f32[8,128]{1,0:T(8,128)S(1)}, f32[32,512]{1,0:T(8,128)S(1)}, bf16[64,128]{1,0:T(8,128)(2,1)S(1)}, /*index=5*/bf16[256,256]{1,0:T(8,128)(2,1)S(1)}) custom-call(f32[10,48,512]{2,1,0:T(8,128)S(1)} %get-tuple-element.26.early_mine, ...), custom_call_target="tpu_custom_call" | custom-call | tf_op jit(solution)/shard_map/inner_psf/pallas_call | solution.py:553
  18.9 0.4 %edge_psf.1 = (f32[32,512]{1,0:T(8,128)S(1)}, f32[8,128]{1,0:T(8,128)S(1)}, f32[1,72,256]{2,1,0:T(8,128)S(1)}) custom-call(bf16[16,512]{1,0:T(8,128)(2,1)S(1)} %collective-permute-done.5.first, bf16[16,512]{1,0:T(8,128)(2,1)S(1)} %collective-permute-done.6.second, f32[32,512]{1,0:T(8,128)S(1)} %get-tuple-element.39.part, ...), custom_call_target="tpu_custom_call" | custom-call | tf_op jit(solution)/shard_map/edge_psf/pallas_call | solution.py:571
  19.3 1.6 %collective-permute-start.7 = (f32[72,256]{1,0:T(8,128)S(1)}, f32[72,256]{1,0:T(8,128)S(1)}, u32[]{:S(2)}, u32[]{:S(2)}) collective-permute-start(f32[72,256]{1,0:T(8,128)S(1)} %bitcast.9), channel_id=1, source_target_pairs={{0,1},{1,0},{2,3},{3,2},{4,5},{5,4},{6,7},{7,6},{8,9},{9,8},{10,11... | collective-permute-start | bytes 221192 | tf_op jit(solution)/shard_map/ppermute | solution.py:457
  20.9 1.8 %collective-permute-start.11 = (f32[8,128]{1,0:T(8,128)S(1)}, f32[8,128]{1,0:T(8,128)S(1)}, u32[]{:S(2)}, u32[]{:S(2)}) collective-permute-start(f32[8,128]{1,0:T(8,128)S(1)} %get-tuple-element.46), channel_id=1, source_target_pairs={{0,12},{1,13},{2,15},{3,14},{4,8},{5,9},{6,11},{7,10},{8,4},{9,5},... | collective-permute-start | bytes 12296 | tf_op jit(solution)/shard_map/ppermute | solution.py:596
  22.7 1.7 %collective-permute-start.10 = (f32[8,128]{1,0:T(8,128)S(1)}, f32[8,128]{1,0:T(8,128)S(1)}, u32[]{:S(2)}, u32[]{:S(2)}) collective-permute-start(f32[8,128]{1,0:T(8,128)S(1)} %get-tuple-element.46), channel_id=1, source_target_pairs={{0,8},{1,9},{2,11},{3,10},{4,12},{5,13},{6,15},{7,14},{8,0},{9,1},... | collective-permute-start | bytes 12296 | tf_op jit(solution)/shard_map/ppermute | solution.py:596
  24.4 0.9 %collective-permute-start.9 = (f32[8,128]{1,0:T(8,128)S(1)}, f32[8,128]{1,0:T(8,128)S(1)}, u32[]{:S(2)}, u32[]{:S(2)}) collective-permute-start(f32[8,128]{1,0:T(8,128)S(1)} %get-tuple-element.46), channel_id=1, source_target_pairs={{0,4},{1,5},{2,7},{3,6},{4,0},{5,1},{6,3},{7,2},{8,12},{9,13},{10,... | collective-permute-start | bytes 12296 | tf_op jit(solution)/shard_map/ppermute | solution.py:596
  25.3 1.0 %collective-permute-done.11 = f32[8,128]{1,0:T(8,128)S(1)} collective-permute-done((f32[8,128]{1,0:T(8,128)S(1)}, f32[8,128]{1,0:T(8,128)S(1)}, u32[]{:S(2)}, u32[]{:S(2)}) %collective-permute-start.11) | collective-permute-done | bytes 4128 | tf_op jit(solution)/shard_map/ppermute | solution.py:596
  26.3 0.9 %collective-permute-done.10 = f32[8,128]{1,0:T(8,128)S(1)} collective-permute-done((f32[8,128]{1,0:T(8,128)S(1)}, f32[8,128]{1,0:T(8,128)S(1)}, u32[]{:S(2)}, u32[]{:S(2)}) %collective-permute-start.10) | collective-permute-done | bytes 4128 | tf_op jit(solution)/shard_map/ppermute | solution.py:596
  27.2 0.8 %collective-permute-done.9 = f32[8,128]{1,0:T(8,128)S(1)} collective-permute-done((f32[8,128]{1,0:T(8,128)S(1)}, f32[8,128]{1,0:T(8,128)S(1)}, u32[]{:S(2)}, u32[]{:S(2)}) %collective-permute-start.9) | collective-permute-done | bytes 4128 | tf_op jit(solution)/shard_map/ppermute | solution.py:596
  28.1 1.2 %collective-permute-done.12 = f32[8,128]{1,0:T(8,128)S(1)} collective-permute-done((f32[8,128]{1,0:T(8,128)S(1)}, f32[8,128]{1,0:T(8,128)S(1)}, u32[]{:S(2)}, u32[]{:S(2)}) %collective-permute-start.12) | collective-permute-done | bytes 4128 | tf_op jit(solution)/shard_map/ppermute | solution.py:600
  29.2 0.9 %detection.1 = f32[128,256]{1,0:T(8,128)} custom-call(f32[32,512]{1,0:T(8,128)S(1)} %get-tuple-element.44.edges, f32[96,512]{1,0:T(8,128)S(1)} %get-tuple-element.42.inner, f32[72,256]{1,0:T(8,128)S(1)} %collective-permute-done.7.refs_0_, f32[72,256]{1,0:T(8,128)S(1)} %collective-permute-done.8.refs_1_, f32[2,8,128]{2,1,0:T(8,128)S(1)} %maximum_select_fusion.refs_2_), custom_call_target="tpu_custom_call" | custom-call | tf_op jit(solution)/shard_map/detection/pallas_call | solution.py:606
  (15 shorter events, 0.2 us)
Async XLA Ops:
  1.7 9.9 %collective-permute-start.1 = (bf16[10,16,512]{2,1,0:T(8,128)(2,1)S(1)}, bf16[10,16,512]{2,1,0:T(8,128)(2,1)S(1)}, u32[]{:S(2)}, u32[]{:S(2)}) collective-permute-start(bf16[10,16,512]{2,1,0:T(8,128)(2,1)S(1)} %get-tuple-element.48), channel_id=1, source_target_pairs={{0,2},{2,0},{4,8},{6,10},{8,4},{10,6},{12,14},{14,12},{1,3},{3,1},... | collective-permute-start | bytes 491528 | tf_op jit(solution)/shard_map/ppermute | solution.py:448
  2.2 9.4 %collective-permute-start = (bf16[10,16,512]{2,1,0:T(8,128)(2,1)S(1)}, bf16[10,16,512]{2,1,0:T(8,128)(2,1)S(1)}, u32[]{:S(2)}, u32[]{:S(2)}) collective-permute-start(bf16[10,16,512]{2,1,0:T(8,128)(2,1)S(1)} %get-tuple-element.49), channel_id=1, source_target_pairs={{0,4},{2,6},{4,0},{6,2},{8,12},{10,14},{12,8},{14,10},{1,5},{3,7},... | collective-permute-start | bytes 491528 | tf_op jit(solution)/shard_map/ppermute | solution.py:448
  12.7 5.0 %copy-start = (f32[1,31]{1,0:T(1,128)S(1)}, f32[1,31]{1,0:T(1,128)}, u32[]{:S(2)}) copy-start(f32[1,31]{1,0:T(1,128)} %row_taps.1) | copy-start | bytes 376
  12.7 5.0 %copy-start.1 = (f32[1,31]{1,0:T(1,128)S(1)}, f32[1,31]{1,0:T(1,128)}, u32[]{:S(2)}) copy-start(f32[1,31]{1,0:T(1,128)} %col_taps.1) | copy-start | bytes 376
  12.7 2.2 %collective-permute-start.3 = (f32[10,32,512]{2,1,0:T(8,128)S(1)}, f32[10,32,512]{2,1,0:T(8,128)S(1)}, u32[]{:S(2)}, u32[]{:S(2)}) collective-permute-start(f32[10,32,512]{2,1,0:T(8,128)S(1)} %edge_visits.1.mine), channel_id=1, source_target_pairs={{0,2},{2,0},{1,3},{3,1},{4,6},{6,4},{5,7},{7,5},{8,10},{10,8},{9,1... | collective-permute-start | bytes 1966088 | tf_op jit(solution)/shard_map/ppermute | solution.py:538
  12.8 3.5 %collective-permute-start.2 = (f32[10,48,512]{2,1,0:T(8,128)S(1)}, f32[10,48,512]{2,1,0:T(8,128)S(1)}, u32[]{:S(2)}, u32[]{:S(2)}) collective-permute-start(f32[10,48,512]{2,1,0:T(8,128)S(1)} %get-tuple-element.26.early_mine), channel_id=1, source_target_pairs={{0,2},{2,0},{1,3},{3,1},{4,6},{6,4},{5,7},{7,5},{8,10},{10,8},{9,1... | collective-permute-start | bytes 2949128 | tf_op jit(solution)/shard_map/ppermute | solution.py:524
  14.8 2.8 %collective-permute-start.4 = (f32[10,48,512]{2,1,0:T(8,128)S(1)}, f32[10,48,512]{2,1,0:T(8,128)S(1)}, u32[]{:S(2)}, u32[]{:S(2)}) collective-permute-start(f32[10,48,512]{2,1,0:T(8,128)S(1)} %get-tuple-element.34.late_mine), channel_id=1, source_target_pairs={{0,2},{2,0},{1,3},{3,1},{4,6},{6,4},{5,7},{7,5},{8,10},{10,8},{9,1... | collective-permute-start | bytes 2949128 | tf_op jit(solution)/shard_map/ppermute | solution.py:541
  15.1 3.8 %collective-permute-start.5 = (bf16[16,512]{1,0:T(8,128)(2,1)S(1)}, bf16[16,512]{1,0:T(8,128)(2,1)S(1)}, u32[]{:S(2)}, u32[]{:S(2)}) collective-permute-start(bf16[16,512]{1,0:T(8,128)(2,1)S(1)} %get-tuple-element.37), channel_id=1, source_target_pairs={{0,4},{2,6},{4,0},{6,2},{8,12},{10,14},{12,8},{14,10},{1,5},{3,7},... | collective-permute-start | bytes 49160 | tf_op jit(solution)/shard_map/ppermute | solution.py:448
  15.5 3.4 %collective-permute-start.6 = (bf16[16,512]{1,0:T(8,128)(2,1)S(1)}, bf16[16,512]{1,0:T(8,128)(2,1)S(1)}, u32[]{:S(2)}, u32[]{:S(2)}) collective-permute-start(bf16[16,512]{1,0:T(8,128)(2,1)S(1)} %get-tuple-element.38), channel_id=1, source_target_pairs={{0,2},{2,0},{4,8},{6,10},{8,4},{10,6},{12,14},{14,12},{1,3},{3,1},... | collective-permute-start | bytes 49160 | tf_op jit(solution)/shard_map/ppermute | solution.py:448
  19.3 6.0 %collective-permute-start.7 = (f32[72,256]{1,0:T(8,128)S(1)}, f32[72,256]{1,0:T(8,128)S(1)}, u32[]{:S(2)}, u32[]{:S(2)}) collective-permute-start(f32[72,256]{1,0:T(8,128)S(1)} %bitcast.9), channel_id=1, source_target_pairs={{0,1},{1,0},{2,3},{3,2},{4,5},{5,4},{6,7},{7,6},{8,9},{9,8},{10,11... | collective-permute-start | bytes 221192 | tf_op jit(solution)/shard_map/ppermute | solution.py:457
  20.9 5.4 %collective-permute-start.11 = (f32[8,128]{1,0:T(8,128)S(1)}, f32[8,128]{1,0:T(8,128)S(1)}, u32[]{:S(2)}, u32[]{:S(2)}) collective-permute-start(f32[8,128]{1,0:T(8,128)S(1)} %get-tuple-element.46), channel_id=1, source_target_pairs={{0,12},{1,13},{2,15},{3,14},{4,8},{5,9},{6,11},{7,10},{8,4},{9,5},... | collective-permute-start | bytes 12296 | tf_op jit(solution)/shard_map/ppermute | solution.py:596
  22.7 4.5 %collective-permute-start.10 = (f32[8,128]{1,0:T(8,128)S(1)}, f32[8,128]{1,0:T(8,128)S(1)}, u32[]{:S(2)}, u32[]{:S(2)}) collective-permute-start(f32[8,128]{1,0:T(8,128)S(1)} %get-tuple-element.46), channel_id=1, source_target_pairs={{0,8},{1,9},{2,11},{3,10},{4,12},{5,13},{6,15},{7,14},{8,0},{9,1},... | collective-permute-start | bytes 12296 | tf_op jit(solution)/shard_map/ppermute | solution.py:596
  24.4 3.6 %collective-permute-start.9 = (f32[8,128]{1,0:T(8,128)S(1)}, f32[8,128]{1,0:T(8,128)S(1)}, u32[]{:S(2)}, u32[]{:S(2)}) collective-permute-start(f32[8,128]{1,0:T(8,128)S(1)} %get-tuple-element.46), channel_id=1, source_target_pairs={{0,4},{1,5},{2,7},{3,6},{4,0},{5,1},{6,3},{7,2},{8,12},{9,13},{10,... | collective-permute-start | bytes 12296 | tf_op jit(solution)/shard_map/ppermute | solution.py:596
  25.3 2.7 %collective-permute-start.8 = (f32[72,256]{1,0:T(8,128)S(1)}, f32[72,256]{1,0:T(8,128)S(1)}, u32[]{:S(2)}, u32[]{:S(2)}) collective-permute-start(f32[72,256]{1,0:T(8,128)S(1)} %collective-permute-done.7.refs_0_), channel_id=1, source_target_pairs={{0,2},{2,0},{1,3},{3,1},{4,6},{6,4},{5,7},{7,5},{8,10},{10,8},{9,1... | collective-permute-start | bytes 221192 | tf_op jit(solution)/shard_map/ppermute | solution.py:598
  28.0 1.2 %collective-permute-start.12 = (f32[8,128]{1,0:T(8,128)S(1)}, f32[8,128]{1,0:T(8,128)S(1)}, u32[]{:S(2)}, u32[]{:S(2)}) collective-permute-start(f32[8,128]{1,0:T(8,128)S(1)} %fusion), channel_id=1, source_target_pairs={{0,2},{2,0},{1,3},{3,1},{4,6},{6,4},{5,7},{7,5},{8,10},{10,8},{9,1... | collective-permute-start | bytes 12296 | tf_op jit(solution)/shard_map/ppermute | solution.py:600

commit v6 on v5

--- a/solution.py
+++ b/solution.py
@@ -412,7 +412,10 @@
     height, width = detection.shape
     half = inner.shape[0] // 2
     lanes = pl.ds(pl.multiple_of(lax.axis_index("band") * width, width), width)
-    scales = [1.0 / (jnp.sum(sums[i]) / pixels + EPSILON) for i in range(others + 1)]
+    scales = []
+    for i in range(others + 1):
+        whole = jnp.sum(jnp.sum(sums[i], axis=0, keepdims=True), axis=1, keepdims=True)
+        scales.append(1.0 / (whole / pixels + EPSILON))
     core = lax.axis_index("exp")
     for place, parts in ((core, mine), (1 - core, theirs)):
         for own, rows, to, start in (

time: 30.2 us -> 30.1 us (level)
  no operation moved by 1% of the time
where the time goes in v6:
time: 30.1 us; the launch traced here: 30 us
  starting transfers between devices  11.9 us (40%)
  Pallas kernels  8.78 us (29%)
  waiting for transfers between devices  7.52 us (25%)
  local copies, waits for them, and re-layouts  1.04 us (3%)
  between operations  0.74 us (2%)
    pallas_call x1, Pallas kernels, on_device(): pl.pallas_call(inner_kernel, in_specs=[HBM] * 6, out_specs=[VMEM] * 6, ou...  5.26 us
    ppermute x4, starting transfers between devices, paired(): return lax.ppermute(value, ('sky', 'exp'), pairs)  5.18 us
    ppermute x3, starting transfers between devices, on_device(): total = total + lax.ppermute(power, ('sky', 'exp', 'band'), pairs)  4.39 us
    ppermute x3, waiting for transfers between devices, on_device(): total = total + lax.ppermute(power, ('sky', 'exp', 'band'), pairs)  2.69 us
    ppermute x1, waiting for transfers between devices, on_device(): edge_other = lax.ppermute(edge_lists, 'exp', swap)  1.59 us
    ppermute x1, starting transfers between devices, turned(): lax.ppermute(value, axis, [(i, (i + step) % size) for i in range(size)])  1.56 us
    ppermute x1, waiting for transfers between devices, on_device(): late_other = lax.ppermute(held, 'exp', swap)  1.41 us
    pallas_call x1, Pallas kernels, on_device(): pl.pallas_call(inner_psf_kernel, in_specs=[VMEM] * 7, out_specs=[VMEM] *...  1.22 us
  transfers between devices with their start and end apart: 13, of which 7 were waited for; matrix products, arithmetic and copies ran while one was open for 0% of the time, Pallas kernels for 22%

profile of v6, /device:TPU:0, one launch (start us, length us, event | category | flops | bytes accessed | tf_op | source)
XLA Modules:
  0.0 30.0 jit_solution(3464519059904857701)
XLA Ops:
  0.6 1.0 %dynamic-slice_bitcast_fusion = (bf16[10,16,512]{2,1,0:T(8,128)(2,1)S(1)}, bf16[10,16,512]{2,1,0:T(8,128)(2,1)S(1)}) fusion(bf16[1,10,128,512]{3,2,1,0:T(8,128)(2,1)} %images_h.1, s32[]{:T(128)S(6)} %select_n.25, s32[]{:T(128)S(6)} %select_n.24), kind=kLoop, calls=%fused_computation | loop fusion | bytes 655368 | tf_op jit(solution)/shard_map/dynamic_slice | solution.py:471
  1.7 0.5 %collective-permute-start.1 = (bf16[10,16,512]{2,1,0:T(8,128)(2,1)S(1)}, bf16[10,16,512]{2,1,0:T(8,128)(2,1)S(1)}, u32[]{:S(2)}, u32[]{:S(2)}) collective-permute-start(bf16[10,16,512]{2,1,0:T(8,128)(2,1)S(1)} %get-tuple-element.48), channel_id=1, source_target_pairs={{0,2},{2,0},{4,8},{6,10},{8,4},{10,6},{12,14},{14,12},{1,3},{3,1},... | collective-permute-start | bytes 491528 | tf_op jit(solution)/shard_map/ppermute | solution.py:451
  2.2 4.1 %collective-permute-start = (bf16[10,16,512]{2,1,0:T(8,128)(2,1)S(1)}, bf16[10,16,512]{2,1,0:T(8,128)(2,1)S(1)}, u32[]{:S(2)}, u32[]{:S(2)}) collective-permute-start(bf16[10,16,512]{2,1,0:T(8,128)(2,1)S(1)} %get-tuple-element.49), channel_id=1, source_target_pairs={{0,4},{2,6},{4,0},{6,2},{8,12},{10,14},{12,8},{14,10},{1,5},{3,7},... | collective-permute-start | bytes 491528 | tf_op jit(solution)/shard_map/ppermute | solution.py:451
  6.3 5.3 %inner_visits.1 = (f32[10,48,512]{2,1,0:T(8,128)S(1)}, f32[10,48,512]{2,1,0:T(8,128)S(1)}, f32[10,32,512]{2,1,0:T(8,128)S(1)}, bf16[10,64,128]{2,1,0:T(8,128)(2,...) custom-call(s32[1,10]{1,0:T(1,128)} %groups_h.1, f32[1,16]{1,0:T(1,128)} %points_h.1, ...), custom_call_target="tpu_custom_call" | custom-call | flops 2684354560 | bytes 3932160 | tf_op jit(solution)/shard_map/inner_visits/pallas_call | solution.py:475
  11.6 1.0 %edge_visits.1.mine = f32[10,32,512]{2,1,0:T(8,128)S(1)} custom-call(bf16[10,16,512]{2,1,0:T(8,128)(2,1)S(1)} %collective-permute-done.first, bf16[10,16,512]{2,1,0:T(8,128)(2,1)S(1)} %collective-permute-done.1.second, f32[10,32,512]{2,1,0:T(8,128)S(1)} %get-tuple-element.30.part, bf16[10,64,128]{2,1,0:T(8,128)(2,1)S(1)} %get-tuple-element.31.edge_m, ...), custom_call_target="tpu_custom_call" | custom-call | flops 4026531840 | bytes 1310720 | tf_op jit(solution)/shard_map/edge_visits/pallas_call | solution.py:528
  12.8 0.5 %collective-permute-start.2 = (f32[10,48,512]{2,1,0:T(8,128)S(1)}, f32[10,48,512]{2,1,0:T(8,128)S(1)}, u32[]{:S(2)}, u32[]{:S(2)}) collective-permute-start(f32[10,48,512]{2,1,0:T(8,128)S(1)} %get-tuple-element.26.early_mine), channel_id=1, source_target_pairs={{0,2},{2,0},{1,3},{3,1},{4,6},{6,4},{5,7},{7,5},{8,10},{10,8},{9,1... | collective-permute-start | bytes 2949128 | tf_op jit(solution)/shard_map/ppermute | solution.py:527
  13.3 1.6 %collective-permute-done.3.other = f32[10,32,512]{2,1,0:T(8,128)S(1)} collective-permute-done((f32[10,32,512]{2,1,0:T(8,128)S(1)}, f32[10,32,512]{2,1,0:T(8,128)S(1)}, u32[]{:S(2)}, u32[]{:S(2)}) %collective-permute-start.3) | collective-permute-done | bytes 655392 | tf_op jit(solution)/shard_map/ppermute | solution.py:541
  14.8 0.1 collective-permute-start.4
  15.0 0.1 edge_merge.1
  15.1 0.4 %collective-permute-start.5 = (bf16[16,512]{1,0:T(8,128)(2,1)S(1)}, bf16[16,512]{1,0:T(8,128)(2,1)S(1)}, u32[]{:S(2)}, u32[]{:S(2)}) collective-permute-start(bf16[16,512]{1,0:T(8,128)(2,1)S(1)} %get-tuple-element.37), channel_id=1, source_target_pairs={{0,4},{2,6},{4,0},{6,2},{8,12},{10,14},{12,8},{14,10},{1,5},{3,7},... | collective-permute-start | bytes 49160 | tf_op jit(solution)/shard_map/ppermute | solution.py:451
  15.5 0.1 collective-permute-start.6
  15.6 0.6 %collective-permute-done.2.early_other = f32[10,48,512]{2,1,0:T(8,128)S(1)} collective-permute-done((f32[10,48,512]{2,1,0:T(8,128)S(1)}, f32[10,48,512]{2,1,0:T(8,128)S(1)}, u32[]{:S(2)}, u32[]{:S(2)}) %collective-permute-start.2) | collective-permute-done | bytes 983072 | tf_op jit(solution)/shard_map/ppermute | solution.py:527
  16.2 1.4 %collective-permute-done.4.late_other = f32[10,48,512]{2,1,0:T(8,128)S(1)} collective-permute-done((f32[10,48,512]{2,1,0:T(8,128)S(1)}, f32[10,48,512]{2,1,0:T(8,128)S(1)}, u32[]{:S(2)}, u32[]{:S(2)}) %collective-permute-start.4) | collective-permute-done | bytes 983072 | tf_op jit(solution)/shard_map/ppermute | solution.py:544
  17.7 1.2 %inner_psf.1 = (f32[1,128,512]{2,1,0:T(8,128)}, f32[96,512]{1,0:T(8,128)S(1)}, f32[8,128]{1,0:T(8,128)S(1)}, f32[32,512]{1,0:T(8,128)S(1)}, bf16[64,128]{1,0:T(8,128)(2,1)S(1)}, /*index=5*/bf16[256,256]{1,0:T(8,128)(2,1)S(1)}) custom-call(f32[10,48,512]{2,1,0:T(8,128)S(1)} %get-tuple-element.26.early_mine, ...), custom_call_target="tpu_custom_call" | custom-call | tf_op jit(solution)/shard_map/inner_psf/pallas_call | solution.py:556
  18.9 0.4 %edge_psf.1 = (f32[32,512]{1,0:T(8,128)S(1)}, f32[8,128]{1,0:T(8,128)S(1)}, f32[1,72,256]{2,1,0:T(8,128)S(1)}) custom-call(bf16[16,512]{1,0:T(8,128)(2,1)S(1)} %collective-permute-done.5.first, bf16[16,512]{1,0:T(8,128)(2,1)S(1)} %collective-permute-done.6.second, f32[32,512]{1,0:T(8,128)S(1)} %get-tuple-element.39.part, ...), custom_call_target="tpu_custom_call" | custom-call | tf_op jit(solution)/shard_map/edge_psf/pallas_call | solution.py:574
  19.3 1.6 %collective-permute-start.7 = (f32[72,256]{1,0:T(8,128)S(1)}, f32[72,256]{1,0:T(8,128)S(1)}, u32[]{:S(2)}, u32[]{:S(2)}) collective-permute-start(f32[72,256]{1,0:T(8,128)S(1)} %bitcast.9), channel_id=1, source_target_pairs={{0,1},{1,0},{2,3},{3,2},{4,5},{5,4},{6,7},{7,6},{8,9},{9,8},{10,11... | collective-permute-start | bytes 221192 | tf_op jit(solution)/shard_map/ppermute | solution.py:460
  20.9 1.8 %collective-permute-start.11 = (f32[8,128]{1,0:T(8,128)S(1)}, f32[8,128]{1,0:T(8,128)S(1)}, u32[]{:S(2)}, u32[]{:S(2)}) collective-permute-start(f32[8,128]{1,0:T(8,128)S(1)} %get-tuple-element.46), channel_id=1, source_target_pairs={{0,12},{1,13},{2,15},{3,14},{4,8},{5,9},{6,11},{7,10},{8,4},{9,5},... | collective-permute-start | bytes 12296 | tf_op jit(solution)/shard_map/ppermute | solution.py:599
  22.7 1.7 %collective-permute-start.10 = (f32[8,128]{1,0:T(8,128)S(1)}, f32[8,128]{1,0:T(8,128)S(1)}, u32[]{:S(2)}, u32[]{:S(2)}) collective-permute-start(f32[8,128]{1,0:T(8,128)S(1)} %get-tuple-element.46), channel_id=1, source_target_pairs={{0,8},{1,9},{2,11},{3,10},{4,12},{5,13},{6,15},{7,14},{8,0},{9,1},... | collective-permute-start | bytes 12296 | tf_op jit(solution)/shard_map/ppermute | solution.py:599
  24.4 0.9 %collective-permute-start.9 = (f32[8,128]{1,0:T(8,128)S(1)}, f32[8,128]{1,0:T(8,128)S(1)}, u32[]{:S(2)}, u32[]{:S(2)}) collective-permute-start(f32[8,128]{1,0:T(8,128)S(1)} %get-tuple-element.46), channel_id=1, source_target_pairs={{0,4},{1,5},{2,7},{3,6},{4,0},{5,1},{6,3},{7,2},{8,12},{9,13},{10,... | collective-permute-start | bytes 12296 | tf_op jit(solution)/shard_map/ppermute | solution.py:599
  25.3 1.0 %collective-permute-done.11 = f32[8,128]{1,0:T(8,128)S(1)} collective-permute-done((f32[8,128]{1,0:T(8,128)S(1)}, f32[8,128]{1,0:T(8,128)S(1)}, u32[]{:S(2)}, u32[]{:S(2)}) %collective-permute-start.11) | collective-permute-done | bytes 4128 | tf_op jit(solution)/shard_map/ppermute | solution.py:599
  26.3 0.9 %collective-permute-done.10 = f32[8,128]{1,0:T(8,128)S(1)} collective-permute-done((f32[8,128]{1,0:T(8,128)S(1)}, f32[8,128]{1,0:T(8,128)S(1)}, u32[]{:S(2)}, u32[]{:S(2)}) %collective-permute-start.10) | collective-permute-done | bytes 4128 | tf_op jit(solution)/shard_map/ppermute | solution.py:599
  27.2 0.8 %collective-permute-done.9 = f32[8,128]{1,0:T(8,128)S(1)} collective-permute-done((f32[8,128]{1,0:T(8,128)S(1)}, f32[8,128]{1,0:T(8,128)S(1)}, u32[]{:S(2)}, u32[]{:S(2)}) %collective-permute-start.9) | collective-permute-done | bytes 4128 | tf_op jit(solution)/shard_map/ppermute | solution.py:599
  28.1 1.2 %collective-permute-done.12 = f32[8,128]{1,0:T(8,128)S(1)} collective-permute-done((f32[8,128]{1,0:T(8,128)S(1)}, f32[8,128]{1,0:T(8,128)S(1)}, u32[]{:S(2)}, u32[]{:S(2)}) %collective-permute-start.12) | collective-permute-done | bytes 4128 | tf_op jit(solution)/shard_map/ppermute | solution.py:603
  29.2 0.8 %detection.1 = f32[128,256]{1,0:T(8,128)} custom-call(f32[32,512]{1,0:T(8,128)S(1)} %get-tuple-element.44.edges, f32[96,512]{1,0:T(8,128)S(1)} %get-tuple-element.42.inner, f32[72,256]{1,0:T(8,128)S(1)} %collective-permute-done.7.refs_0_, f32[72,256]{1,0:T(8,128)S(1)} %collective-permute-done.8.refs_1_, f32[2,8,128]{2,1,0:T(8,128)S(1)} %maximum_select_fusion.refs_2_), custom_call_target="tpu_custom_call" | custom-call | tf_op jit(solution)/shard_map/detection/pallas_call | solution.py:609
  (15 shorter events, 0.2 us)
Async XLA Ops:
  1.7 9.9 %collective-permute-start.1 = (bf16[10,16,512]{2,1,0:T(8,128)(2,1)S(1)}, bf16[10,16,512]{2,1,0:T(8,128)(2,1)S(1)}, u32[]{:S(2)}, u32[]{:S(2)}) collective-permute-start(bf16[10,16,512]{2,1,0:T(8,128)(2,1)S(1)} %get-tuple-element.48), channel_id=1, source_target_pairs={{0,2},{2,0},{4,8},{6,10},{8,4},{10,6},{12,14},{14,12},{1,3},{3,1},... | collective-permute-start | bytes 491528 | tf_op jit(solution)/shard_map/ppermute | solution.py:451
  2.2 9.4 %collective-permute-start = (bf16[10,16,512]{2,1,0:T(8,128)(2,1)S(1)}, bf16[10,16,512]{2,1,0:T(8,128)(2,1)S(1)}, u32[]{:S(2)}, u32[]{:S(2)}) collective-permute-start(bf16[10,16,512]{2,1,0:T(8,128)(2,1)S(1)} %get-tuple-element.49), channel_id=1, source_target_pairs={{0,4},{2,6},{4,0},{6,2},{8,12},{10,14},{12,8},{14,10},{1,5},{3,7},... | collective-permute-start | bytes 491528 | tf_op jit(solution)/shard_map/ppermute | solution.py:451
  12.7 5.0 %copy-start = (f32[1,31]{1,0:T(1,128)S(1)}, f32[1,31]{1,0:T(1,128)}, u32[]{:S(2)}) copy-start(f32[1,31]{1,0:T(1,128)} %row_taps.1) | copy-start | bytes 376
  12.7 5.0 %copy-start.1 = (f32[1,31]{1,0:T(1,128)S(1)}, f32[1,31]{1,0:T(1,128)}, u32[]{:S(2)}) copy-start(f32[1,31]{1,0:T(1,128)} %col_taps.1) | copy-start | bytes 376
  12.7 2.2 %collective-permute-start.3 = (f32[10,32,512]{2,1,0:T(8,128)S(1)}, f32[10,32,512]{2,1,0:T(8,128)S(1)}, u32[]{:S(2)}, u32[]{:S(2)}) collective-permute-start(f32[10,32,512]{2,1,0:T(8,128)S(1)} %edge_visits.1.mine), channel_id=1, source_target_pairs={{0,2},{2,0},{1,3},{3,1},{4,6},{6,4},{5,7},{7,5},{8,10},{10,8},{9,1... | collective-permute-start | bytes 1966088 | tf_op jit(solution)/shard_map/ppermute | solution.py:541
  12.8 3.5 %collective-permute-start.2 = (f32[10,48,512]{2,1,0:T(8,128)S(1)}, f32[10,48,512]{2,1,0:T(8,128)S(1)}, u32[]{:S(2)}, u32[]{:S(2)}) collective-permute-start(f32[10,48,512]{2,1,0:T(8,128)S(1)} %get-tuple-element.26.early_mine), channel_id=1, source_target_pairs={{0,2},{2,0},{1,3},{3,1},{4,6},{6,4},{5,7},{7,5},{8,10},{10,8},{9,1... | collective-permute-start | bytes 2949128 | tf_op jit(solution)/shard_map/ppermute | solution.py:527
  14.8 2.8 %collective-permute-start.4 = (f32[10,48,512]{2,1,0:T(8,128)S(1)}, f32[10,48,512]{2,1,0:T(8,128)S(1)}, u32[]{:S(2)}, u32[]{:S(2)}) collective-permute-start(f32[10,48,512]{2,1,0:T(8,128)S(1)} %get-tuple-element.34.late_mine), channel_id=1, source_target_pairs={{0,2},{2,0},{1,3},{3,1},{4,6},{6,4},{5,7},{7,5},{8,10},{10,8},{9,1... | collective-permute-start | bytes 2949128 | tf_op jit(solution)/shard_map/ppermute | solution.py:544
  15.1 3.8 %collective-permute-start.5 = (bf16[16,512]{1,0:T(8,128)(2,1)S(1)}, bf16[16,512]{1,0:T(8,128)(2,1)S(1)}, u32[]{:S(2)}, u32[]{:S(2)}) collective-permute-start(bf16[16,512]{1,0:T(8,128)(2,1)S(1)} %get-tuple-element.37), channel_id=1, source_target_pairs={{0,4},{2,6},{4,0},{6,2},{8,12},{10,14},{12,8},{14,10},{1,5},{3,7},... | collective-permute-start | bytes 49160 | tf_op jit(solution)/shard_map/ppermute | solution.py:451
  15.5 3.4 %collective-permute-start.6 = (bf16[16,512]{1,0:T(8,128)(2,1)S(1)}, bf16[16,512]{1,0:T(8,128)(2,1)S(1)}, u32[]{:S(2)}, u32[]{:S(2)}) collective-permute-start(bf16[16,512]{1,0:T(8,128)(2,1)S(1)} %get-tuple-element.38), channel_id=1, source_target_pairs={{0,2},{2,0},{4,8},{6,10},{8,4},{10,6},{12,14},{14,12},{1,3},{3,1},... | collective-permute-start | bytes 49160 | tf_op jit(solution)/shard_map/ppermute | solution.py:451
  19.3 6.0 %collective-permute-start.7 = (f32[72,256]{1,0:T(8,128)S(1)}, f32[72,256]{1,0:T(8,128)S(1)}, u32[]{:S(2)}, u32[]{:S(2)}) collective-permute-start(f32[72,256]{1,0:T(8,128)S(1)} %bitcast.9), channel_id=1, source_target_pairs={{0,1},{1,0},{2,3},{3,2},{4,5},{5,4},{6,7},{7,6},{8,9},{9,8},{10,11... | collective-permute-start | bytes 221192 | tf_op jit(solution)/shard_map/ppermute | solution.py:460
  20.9 5.4 %collective-permute-start.11 = (f32[8,128]{1,0:T(8,128)S(1)}, f32[8,128]{1,0:T(8,128)S(1)}, u32[]{:S(2)}, u32[]{:S(2)}) collective-permute-start(f32[8,128]{1,0:T(8,128)S(1)} %get-tuple-element.46), channel_id=1, source_target_pairs={{0,12},{1,13},{2,15},{3,14},{4,8},{5,9},{6,11},{7,10},{8,4},{9,5},... | collective-permute-start | bytes 12296 | tf_op jit(solution)/shard_map/ppermute | solution.py:599
  22.7 4.5 %collective-permute-start.10 = (f32[8,128]{1,0:T(8,128)S(1)}, f32[8,128]{1,0:T(8,128)S(1)}, u32[]{:S(2)}, u32[]{:S(2)}) collective-permute-start(f32[8,128]{1,0:T(8,128)S(1)} %get-tuple-element.46), channel_id=1, source_target_pairs={{0,8},{1,9},{2,11},{3,10},{4,12},{5,13},{6,15},{7,14},{8,0},{9,1},... | collective-permute-start | bytes 12296 | tf_op jit(solution)/shard_map/ppermute | solution.py:599
  24.4 3.6 %collective-permute-start.9 = (f32[8,128]{1,0:T(8,128)S(1)}, f32[8,128]{1,0:T(8,128)S(1)}, u32[]{:S(2)}, u32[]{:S(2)}) collective-permute-start(f32[8,128]{1,0:T(8,128)S(1)} %get-tuple-element.46), channel_id=1, source_target_pairs={{0,4},{1,5},{2,7},{3,6},{4,0},{5,1},{6,3},{7,2},{8,12},{9,13},{10,... | collective-permute-start | bytes 12296 | tf_op jit(solution)/shard_map/ppermute | solution.py:599
  25.3 2.7 %collective-permute-start.8 = (f32[72,256]{1,0:T(8,128)S(1)}, f32[72,256]{1,0:T(8,128)S(1)}, u32[]{:S(2)}, u32[]{:S(2)}) collective-permute-start(f32[72,256]{1,0:T(8,128)S(1)} %collective-permute-done.7.refs_0_), channel_id=1, source_target_pairs={{0,2},{2,0},{1,3},{3,1},{4,6},{6,4},{5,7},{7,5},{8,10},{10,8},{9,1... | collective-permute-start | bytes 221192 | tf_op jit(solution)/shard_map/ppermute | solution.py:601
  28.0 1.2 %collective-permute-start.12 = (f32[8,128]{1,0:T(8,128)S(1)}, f32[8,128]{1,0:T(8,128)S(1)}, u32[]{:S(2)}, u32[]{:S(2)}) collective-permute-start(f32[8,128]{1,0:T(8,128)S(1)} %fusion), channel_id=1, source_target_pairs={{0,2},{2,0},{1,3},{3,1},{4,6},{6,4},{5,7},{7,5},{8,10},{10,8},{9,1... | collective-permute-start | bytes 12296 | tf_op jit(solution)/shard_map/ppermute | solution.py:603

commit v7 on v6

--- a/solution.py
+++ b/solution.py
@@ -150,6 +150,22 @@
         return carry
 
     lax.fori_loop(0, rows // 8, body, 0)
+
+
+def rim_kernel(images, first, second, sems):
+    rows = first.shape[1]
+    last = images.shape[2] - rows
+    far = jnp.where(lax.rem(lax.axis_index("sky"), 2) == 0, last, 0)
+    copies = [
+        pltpu.make_async_copy(
+            images.at[0, :, pl.ds(pl.multiple_of(start, EDGE), rows)], target, sems.at[i]
+        )
+        for i, (start, target) in enumerate(((far, first), (last - far, second)))
+    ]
+    for copy in copies:
+        copy.start()
+    for copy in copies:
+        copy.wait()
 
 
 def inner_kernel(
@@ -465,13 +481,19 @@
     inner = height - 2 * EDGE
     bands = lax.axis_size("band")
     strips = lax.axis_size("sky")
-    even = lax.rem(lax.axis_index("sky"), 2) == 0
-    far = jnp.where(even, height - EDGE, 0)
-    first = paired(lax.dynamic_slice_in_dim(images[0], far, EDGE, 1), 0)
-    second = paired(lax.dynamic_slice_in_dim(images[0], height - EDGE - far, EDGE, 1), 1)
+    first, second = pl.pallas_call(
+        rim_kernel,
+        in_specs=[HBM],
+        out_specs=[VMEM] * 2,
+        out_shape=[vmem((visits, EDGE, cols), BF16)] * 2,
+        scratch_shapes=[pltpu.SemaphoreType.DMA((2,))],
+        compiler_params=PARAMS,
+        name="rims",
+    )(pltpu.with_memory_space_constraint(images, pltpu.HBM))
+    first, second = paired(first, 0), paired(second, 1)
 
     lists = 2 * REJECT + 2
-    early = inner // 16 * 8
+    early = inner * 5 // 8 // 8 * 8
     early_lists, late_lists, part, edge_m, col_m, edge_mask = pl.pallas_call(
         inner_kernel,
         in_specs=[HBM] * 6,
@@ -589,7 +611,7 @@
     if strips == 4 and bands == 2 and lax.axis_size("exp") == 2:
         first_core = lax.axis_index("exp") == 0
         total = 0.0
-        for bits in range(1, strips):
+        for bits in (1, 3, 2):
             pairs = []
             for strip in range(strips):
                 for core in range(2):

time: 30.1 us -> 29.8 us (0.990)
  waiting for transfers between devices: 7.52 us -> 5.97 us
  starting transfers between devices: 11.9 us -> 13.1 us
  Pallas kernels: 8.78 us -> 9.82 us
  local copies, waits for them, and re-layouts: 1.04 us -> 0.01 us
    ppermute x1, waiting for transfers between devices: 1.41 us -> 0.01 us  [on_device(): late_other = lax.ppermute(held, 'exp', swap)]
    dynamic_slice x1 -> x0, local copies, waits for them, and re-layouts: 1.03 us -> none  [on_device(): lax.dynamic_slice_in_dim(images[0], height - EDGE - far, EDGE, 1)]
    pallas_call x0 -> x1, Pallas kernels: none -> 1.03 us  [on_device(): pl.pallas_call(rim_kernel, in_specs=[HBM], out_specs=[VMEM] * 2, out_shap...]
    ppermute x4, starting transfers between devices: 5.18 us -> 6.03 us  [paired(): return lax.ppermute(value, ('sky', 'exp'), pairs)]
    ppermute x1, waiting for transfers between devices: 0.62 us -> 0.01 us  [on_device(): early_other = lax.ppermute(held, 'exp', swap)]
    ppermute x1, starting transfers between devices: 0.07 us -> 0.57 us  [on_device(): edge_other = lax.ppermute(edge_lists, 'exp', swap)]
    ppermute x1, starting transfers between devices: 0.5 us -> 0.08 us  [on_device(): early_other = lax.ppermute(held, 'exp', swap)]
    ppermute x4, waiting for transfers between devices: 0.06 us -> 0.38 us  [paired(): return lax.ppermute(value, ('sky', 'exp'), pairs)]
  transfers between devices with their start and end apart: 13 -> 13, of which waited for: 7 -> 6; matrix products, arithmetic and copies ran while one was open for 0% -> 0% of each run, Pallas kernels for 22% -> 22%
where the time goes in v7:
time: 29.8 us; the launch traced here: 29.6 us
  starting transfers between devices  13.1 us (44%)
  Pallas kernels  9.82 us (33%)
  waiting for transfers between devices  5.97 us (20%)
  between operations  0.73 us (2%)
    ppermute x4, starting transfers between devices, paired(): return lax.ppermute(value, ('sky', 'exp'), pairs)  6.03 us
    pallas_call x1, Pallas kernels, on_device(): pl.pallas_call(inner_kernel, in_specs=[HBM] * 6, out_specs=[VMEM] * 6, ou...  5.26 us
    ppermute x3, starting transfers between devices, on_device(): total = total + lax.ppermute(power, ('sky', 'exp', 'band'), pairs)  4.39 us
    ppermute x3, waiting for transfers between devices, on_device(): total = total + lax.ppermute(power, ('sky', 'exp', 'band'), pairs)  2.78 us
    ppermute x1, waiting for transfers between devices, on_device(): edge_other = lax.ppermute(edge_lists, 'exp', swap)  1.65 us
    ppermute x1, starting transfers between devices, turned(): lax.ppermute(value, axis, [(i, (i + step) % size) for i in range(size)])  1.56 us
    pallas_call x1, Pallas kernels, on_device(): pl.pallas_call(inner_psf_kernel, in_specs=[VMEM] * 7, out_specs=[VMEM] *...  1.23 us
    ppermute x1, waiting for transfers between devices, on_device(): other = lax.ppermute(total, 'exp', swap)  1.15 us
  transfers between devices with their start and end apart: 13, of which 6 were waited for; matrix products, arithmetic and copies ran while one was open for 0% of the time, Pallas kernels for 22%

profile of v7, /device:TPU:0, one launch (start us, length us, event | category | flops | bytes accessed | tf_op | source)
XLA Modules:
  0.0 29.6 jit_solution(14172312202661196144)
XLA Ops:
  0.6 1.0 %rims.1 = (bf16[10,16,512]{2,1,0:T(8,128)(2,1)S(1)}, bf16[10,16,512]{2,1,0:T(8,128)(2,1)S(1)}) custom-call(bf16[1,10,128,512]{3,2,1,0:T(8,128)(2,1)} %images.1), custom_call_target="tpu_custom_call" | custom-call | tf_op jit(solution)/shard_map/rims/pallas_call | solution.py:484
  1.7 3.1 %collective-permute-start = (bf16[10,16,512]{2,1,0:T(8,128)(2,1)S(1)}, bf16[10,16,512]{2,1,0:T(8,128)(2,1)S(1)}, u32[]{:S(2)}, u32[]{:S(2)}) collective-permute-start(bf16[10,16,512]{2,1,0:T(8,128)(2,1)S(1)} %get-tuple-element.28), channel_id=1, source_target_pairs={{0,4},{2,6},{4,0},{6,2},{8,12},{10,14},{12,8},{14,10},{1,5},{3,7},... | collective-permute-start | bytes 491528 | tf_op jit(solution)/shard_map/ppermute | solution.py:467
  4.8 5.3 %inner_visits.1 = (f32[10,56,512]{2,1,0:T(8,128)S(1)}, f32[10,40,512]{2,1,0:T(8,128)S(1)}, f32[10,32,512]{2,1,0:T(8,128)S(1)}, bf16[10,64,128]{2,1,0:T(8,128)(2,...) custom-call(s32[1,10]{1,0:T(1,128)} %groups_h.1, f32[1,16]{1,0:T(1,128)} %points_h.1, ...), custom_call_target="tpu_custom_call" | custom-call | flops 2684354560 | bytes 3932160 | tf_op jit(solution)/shard_map/inner_visits/pallas_call | solution.py:497
  10.0 1.0 %edge_visits.1.mine = f32[10,32,512]{2,1,0:T(8,128)S(1)} custom-call(bf16[10,16,512]{2,1,0:T(8,128)(2,1)S(1)} %collective-permute-done.first, bf16[10,16,512]{2,1,0:T(8,128)(2,1)S(1)} %collective-permute-done.1.second, f32[10,32,512]{2,1,0:T(8,128)S(1)} %get-tuple-element.34.part, bf16[10,64,128]{2,1,0:T(8,128)(2,1)S(1)} %get-tuple-element.35.edge_m, ...), custom_call_target="tpu_custom_call" | custom-call | flops 4026531840 | bytes 1310720 | tf_op jit(solution)/shard_map/edge_visits/pallas_call | solution.py:550
  11.1 0.6 %collective-permute-start.3 = (f32[10,32,512]{2,1,0:T(8,128)S(1)}, f32[10,32,512]{2,1,0:T(8,128)S(1)}, u32[]{:S(2)}, u32[]{:S(2)}) collective-permute-start(f32[10,32,512]{2,1,0:T(8,128)S(1)} %edge_visits.1.mine), channel_id=1, source_target_pairs={{0,2},{2,0},{1,3},{3,1},{4,6},{6,4},{5,7},{7,5},{8,10},{10,8},{9,1... | collective-permute-start | bytes 1966088 | tf_op jit(solution)/shard_map/ppermute | solution.py:563
  11.7 0.1 collective-permute-start.2
  11.7 1.6 %collective-permute-done.3.other = f32[10,32,512]{2,1,0:T(8,128)S(1)} collective-permute-done((f32[10,32,512]{2,1,0:T(8,128)S(1)}, f32[10,32,512]{2,1,0:T(8,128)S(1)}, u32[]{:S(2)}, u32[]{:S(2)}) %collective-permute-start.3) | collective-permute-done | bytes 655392 | tf_op jit(solution)/shard_map/ppermute | solution.py:563
  13.4 0.4 %collective-permute-start.4 = (f32[10,40,512]{2,1,0:T(8,128)S(1)}, f32[10,40,512]{2,1,0:T(8,128)S(1)}, u32[]{:S(2)}, u32[]{:S(2)}) collective-permute-start(f32[10,40,512]{2,1,0:T(8,128)S(1)} %get-tuple-element.38.late_mine), channel_id=1, source_target_pairs={{0,2},{2,0},{1,3},{3,1},{4,6},{6,4},{5,7},{7,5},{8,10},{10,8},{9,1... | collective-permute-start | bytes 2457608 | tf_op jit(solution)/shard_map/ppermute | solution.py:566
  13.8 0.1 edge_merge.1
  13.9 2.9 %collective-permute-start.5 = (bf16[16,512]{1,0:T(8,128)(2,1)S(1)}, bf16[16,512]{1,0:T(8,128)(2,1)S(1)}, u32[]{:S(2)}, u32[]{:S(2)}) collective-permute-start(bf16[16,512]{1,0:T(8,128)(2,1)S(1)} %get-tuple-element.41), channel_id=1, source_target_pairs={{0,4},{2,6},{4,0},{6,2},{8,12},{10,14},{12,8},{14,10},{1,5},{3,7},... | collective-permute-start | bytes 49160 | tf_op jit(solution)/shard_map/ppermute | solution.py:467
  16.8 0.1 collective-permute-start.6
  16.9 1.2 %inner_psf.1 = (f32[1,128,512]{2,1,0:T(8,128)}, f32[96,512]{1,0:T(8,128)S(1)}, f32[8,128]{1,0:T(8,128)S(1)}, f32[32,512]{1,0:T(8,128)S(1)}, bf16[64,128]{1,0:T(8,128)(2,1)S(1)}, /*index=5*/bf16[256,256]{1,0:T(8,128)(2,1)S(1)}) custom-call(f32[10,56,512]{2,1,0:T(8,128)S(1)} %get-tuple-element.30.early_mine, ...), custom_call_target="tpu_custom_call" | custom-call | tf_op jit(solution)/shard_map/inner_psf/pallas_call | solution.py:578
  18.1 0.4 %collective-permute-done.5.first = bf16[16,512]{1,0:T(8,128)(2,1)S(1)} collective-permute-done((bf16[16,512]{1,0:T(8,128)(2,1)S(1)}, bf16[16,512]{1,0:T(8,128)(2,1)S(1)}, u32[]{:S(2)}, u32[]{:S(2)}) %collective-permute-start.5) | collective-permute-done | bytes 16416 | tf_op jit(solution)/shard_map/ppermute | solution.py:467
  18.5 0.4 %edge_psf.1 = (f32[32,512]{1,0:T(8,128)S(1)}, f32[8,128]{1,0:T(8,128)S(1)}, f32[1,72,256]{2,1,0:T(8,128)S(1)}) custom-call(bf16[16,512]{1,0:T(8,128)(2,1)S(1)} %collective-permute-done.5.first, bf16[16,512]{1,0:T(8,128)(2,1)S(1)} %collective-permute-done.6.second, f32[32,512]{1,0:T(8,128)S(1)} %get-tuple-element.43.part, ...), custom_call_target="tpu_custom_call" | custom-call | tf_op jit(solution)/shard_map/edge_psf/pallas_call | solution.py:596
  18.9 1.6 %collective-permute-start.7 = (f32[72,256]{1,0:T(8,128)S(1)}, f32[72,256]{1,0:T(8,128)S(1)}, u32[]{:S(2)}, u32[]{:S(2)}) collective-permute-start(f32[72,256]{1,0:T(8,128)S(1)} %bitcast.5), channel_id=1, source_target_pairs={{0,1},{1,0},{2,3},{3,2},{4,5},{5,4},{6,7},{7,6},{8,9},{9,8},{10,11... | collective-permute-start | bytes 221192 | tf_op jit(solution)/shard_map/ppermute | solution.py:476
  20.4 1.7 %collective-permute-start.10 = (f32[8,128]{1,0:T(8,128)S(1)}, f32[8,128]{1,0:T(8,128)S(1)}, u32[]{:S(2)}, u32[]{:S(2)}) collective-permute-start(f32[8,128]{1,0:T(8,128)S(1)} %get-tuple-element.50), channel_id=1, source_target_pairs={{0,12},{1,13},{2,15},{3,14},{4,8},{5,9},{6,11},{7,10},{8,4},{9,5},... | collective-permute-start | bytes 12296 | tf_op jit(solution)/shard_map/ppermute | solution.py:621
  22.1 1.9 %collective-permute-start.11 = (f32[8,128]{1,0:T(8,128)S(1)}, f32[8,128]{1,0:T(8,128)S(1)}, u32[]{:S(2)}, u32[]{:S(2)}) collective-permute-start(f32[8,128]{1,0:T(8,128)S(1)} %get-tuple-element.50), channel_id=1, source_target_pairs={{0,8},{1,9},{2,11},{3,10},{4,12},{5,13},{6,15},{7,14},{8,0},{9,1},... | collective-permute-start | bytes 12296 | tf_op jit(solution)/shard_map/ppermute | solution.py:621
  24.0 0.8 %collective-permute-start.9 = (f32[8,128]{1,0:T(8,128)S(1)}, f32[8,128]{1,0:T(8,128)S(1)}, u32[]{:S(2)}, u32[]{:S(2)}) collective-permute-start(f32[8,128]{1,0:T(8,128)S(1)} %get-tuple-element.50), channel_id=1, source_target_pairs={{0,4},{1,5},{2,7},{3,6},{4,0},{5,1},{6,3},{7,2},{8,12},{9,13},{10,... | collective-permute-start | bytes 12296 | tf_op jit(solution)/shard_map/ppermute | solution.py:621
  24.8 1.0 %collective-permute-done.10 = f32[8,128]{1,0:T(8,128)S(1)} collective-permute-done((f32[8,128]{1,0:T(8,128)S(1)}, f32[8,128]{1,0:T(8,128)S(1)}, u32[]{:S(2)}, u32[]{:S(2)}) %collective-permute-start.10) | collective-permute-done | bytes 4128 | tf_op jit(solution)/shard_map/ppermute | solution.py:621
  25.8 0.8 %collective-permute-done.11 = f32[8,128]{1,0:T(8,128)S(1)} collective-permute-done((f32[8,128]{1,0:T(8,128)S(1)}, f32[8,128]{1,0:T(8,128)S(1)}, u32[]{:S(2)}, u32[]{:S(2)}) %collective-permute-start.11) | collective-permute-done | bytes 4128 | tf_op jit(solution)/shard_map/ppermute | solution.py:621
  26.6 1.0 %collective-permute-done.9 = f32[8,128]{1,0:T(8,128)S(1)} collective-permute-done((f32[8,128]{1,0:T(8,128)S(1)}, f32[8,128]{1,0:T(8,128)S(1)}, u32[]{:S(2)}, u32[]{:S(2)}) %collective-permute-start.9) | collective-permute-done | bytes 4128 | tf_op jit(solution)/shard_map/ppermute | solution.py:621
  27.6 0.1 collective-permute-start.12
  27.7 1.2 %collective-permute-done.12 = f32[8,128]{1,0:T(8,128)S(1)} collective-permute-done((f32[8,128]{1,0:T(8,128)S(1)}, f32[8,128]{1,0:T(8,128)S(1)}, u32[]{:S(2)}, u32[]{:S(2)}) %collective-permute-start.12) | collective-permute-done | bytes 4128 | tf_op jit(solution)/shard_map/ppermute | solution.py:625
  28.9 0.8 %detection.1 = f32[128,256]{1,0:T(8,128)} custom-call(f32[32,512]{1,0:T(8,128)S(1)} %get-tuple-element.48.edges, f32[96,512]{1,0:T(8,128)S(1)} %get-tuple-element.46.inner, f32[72,256]{1,0:T(8,128)S(1)} %collective-permute-done.7.refs_0_, f32[72,256]{1,0:T(8,128)S(1)} %collective-permute-done.8.refs_1_, f32[2,8,128]{2,1,0:T(8,128)S(1)} %maximum_select_fusion.refs_2_), custom_call_target="tpu_custom_call" | custom-call | tf_op jit(solution)/shard_map/detection/pallas_call | solution.py:631
  (15 shorter events, 0.0 us)
Async XLA Ops:
  1.7 8.4 %collective-permute-start = (bf16[10,16,512]{2,1,0:T(8,128)(2,1)S(1)}, bf16[10,16,512]{2,1,0:T(8,128)(2,1)S(1)}, u32[]{:S(2)}, u32[]{:S(2)}) collective-permute-start(bf16[10,16,512]{2,1,0:T(8,128)(2,1)S(1)} %get-tuple-element.28), channel_id=1, source_target_pairs={{0,4},{2,6},{4,0},{6,2},{8,12},{10,14},{12,8},{14,10},{1,5},{3,7},... | collective-permute-start | bytes 491528 | tf_op jit(solution)/shard_map/ppermute | solution.py:467
  4.8 5.3 %collective-permute-start.1 = (bf16[10,16,512]{2,1,0:T(8,128)(2,1)S(1)}, bf16[10,16,512]{2,1,0:T(8,128)(2,1)S(1)}, u32[]{:S(2)}, u32[]{:S(2)}) collective-permute-start(bf16[10,16,512]{2,1,0:T(8,128)(2,1)S(1)} %get-tuple-element.29), channel_id=1, source_target_pairs={{0,2},{2,0},{4,8},{6,10},{8,4},{10,6},{12,14},{14,12},{1,3},{3,1},... | collective-permute-start | bytes 491528 | tf_op jit(solution)/shard_map/ppermute | solution.py:467
  11.1 5.8 %copy-start = (f32[1,31]{1,0:T(1,128)S(1)}, f32[1,31]{1,0:T(1,128)}, u32[]{:S(2)}) copy-start(f32[1,31]{1,0:T(1,128)} %row_taps.1) | copy-start | bytes 376
  11.1 5.8 %copy-start.1 = (f32[1,31]{1,0:T(1,128)S(1)}, f32[1,31]{1,0:T(1,128)}, u32[]{:S(2)}) copy-start(f32[1,31]{1,0:T(1,128)} %col_taps.1) | copy-start | bytes 376
  11.1 2.3 %collective-permute-start.3 = (f32[10,32,512]{2,1,0:T(8,128)S(1)}, f32[10,32,512]{2,1,0:T(8,128)S(1)}, u32[]{:S(2)}, u32[]{:S(2)}) collective-permute-start(f32[10,32,512]{2,1,0:T(8,128)S(1)} %edge_visits.1.mine), channel_id=1, source_target_pairs={{0,2},{2,0},{1,3},{3,1},{4,6},{6,4},{5,7},{7,5},{8,10},{10,8},{9,1... | collective-permute-start | bytes 1966088 | tf_op jit(solution)/shard_map/ppermute | solution.py:563
  11.7 5.2 %collective-permute-start.2 = (f32[10,56,512]{2,1,0:T(8,128)S(1)}, f32[10,56,512]{2,1,0:T(8,128)S(1)}, u32[]{:S(2)}, u32[]{:S(2)}) collective-permute-start(f32[10,56,512]{2,1,0:T(8,128)S(1)} %get-tuple-element.30.early_mine), channel_id=1, source_target_pairs={{0,2},{2,0},{1,3},{3,1},{4,6},{6,4},{5,7},{7,5},{8,10},{10,8},{9,1... | collective-permute-start | bytes 3440648 | tf_op jit(solution)/shard_map/ppermute | solution.py:549
  13.4 3.5 %collective-permute-start.4 = (f32[10,40,512]{2,1,0:T(8,128)S(1)}, f32[10,40,512]{2,1,0:T(8,128)S(1)}, u32[]{:S(2)}, u32[]{:S(2)}) collective-permute-start(f32[10,40,512]{2,1,0:T(8,128)S(1)} %get-tuple-element.38.late_mine), channel_id=1, source_target_pairs={{0,2},{2,0},{1,3},{3,1},{4,6},{6,4},{5,7},{7,5},{8,10},{10,8},{9,1... | collective-permute-start | bytes 2457608 | tf_op jit(solution)/shard_map/ppermute | solution.py:566
  13.9 4.6 %collective-permute-start.5 = (bf16[16,512]{1,0:T(8,128)(2,1)S(1)}, bf16[16,512]{1,0:T(8,128)(2,1)S(1)}, u32[]{:S(2)}, u32[]{:S(2)}) collective-permute-start(bf16[16,512]{1,0:T(8,128)(2,1)S(1)} %get-tuple-element.41), channel_id=1, source_target_pairs={{0,4},{2,6},{4,0},{6,2},{8,12},{10,14},{12,8},{14,10},{1,5},{3,7},... | collective-permute-start | bytes 49160 | tf_op jit(solution)/shard_map/ppermute | solution.py:467
  16.8 1.7 %collective-permute-start.6 = (bf16[16,512]{1,0:T(8,128)(2,1)S(1)}, bf16[16,512]{1,0:T(8,128)(2,1)S(1)}, u32[]{:S(2)}, u32[]{:S(2)}) collective-permute-start(bf16[16,512]{1,0:T(8,128)(2,1)S(1)} %get-tuple-element.42), channel_id=1, source_target_pairs={{0,2},{2,0},{4,8},{6,10},{8,4},{10,6},{12,14},{14,12},{1,3},{3,1},... | collective-permute-start | bytes 49160 | tf_op jit(solution)/shard_map/ppermute | solution.py:467
  18.9 6.0 %collective-permute-start.7 = (f32[72,256]{1,0:T(8,128)S(1)}, f32[72,256]{1,0:T(8,128)S(1)}, u32[]{:S(2)}, u32[]{:S(2)}) collective-permute-start(f32[72,256]{1,0:T(8,128)S(1)} %bitcast.5), channel_id=1, source_target_pairs={{0,1},{1,0},{2,3},{3,2},{4,5},{5,4},{6,7},{7,6},{8,9},{9,8},{10,11... | collective-permute-start | bytes 221192 | tf_op jit(solution)/shard_map/ppermute | solution.py:476
  20.4 5.4 %collective-permute-start.10 = (f32[8,128]{1,0:T(8,128)S(1)}, f32[8,128]{1,0:T(8,128)S(1)}, u32[]{:S(2)}, u32[]{:S(2)}) collective-permute-start(f32[8,128]{1,0:T(8,128)S(1)} %get-tuple-element.50), channel_id=1, source_target_pairs={{0,12},{1,13},{2,15},{3,14},{4,8},{5,9},{6,11},{7,10},{8,4},{9,5},... | collective-permute-start | bytes 12296 | tf_op jit(solution)/shard_map/ppermute | solution.py:621
  22.1 4.5 %collective-permute-start.11 = (f32[8,128]{1,0:T(8,128)S(1)}, f32[8,128]{1,0:T(8,128)S(1)}, u32[]{:S(2)}, u32[]{:S(2)}) collective-permute-start(f32[8,128]{1,0:T(8,128)S(1)} %get-tuple-element.50), channel_id=1, source_target_pairs={{0,8},{1,9},{2,11},{3,10},{4,12},{5,13},{6,15},{7,14},{8,0},{9,1},... | collective-permute-start | bytes 12296 | tf_op jit(solution)/shard_map/ppermute | solution.py:621
  24.0 3.6 %collective-permute-start.9 = (f32[8,128]{1,0:T(8,128)S(1)}, f32[8,128]{1,0:T(8,128)S(1)}, u32[]{:S(2)}, u32[]{:S(2)}) collective-permute-start(f32[8,128]{1,0:T(8,128)S(1)} %get-tuple-element.50), channel_id=1, source_target_pairs={{0,4},{1,5},{2,7},{3,6},{4,0},{5,1},{6,3},{7,2},{8,12},{9,13},{10,... | collective-permute-start | bytes 12296 | tf_op jit(solution)/shard_map/ppermute | solution.py:621
  24.8 2.8 %collective-permute-start.8 = (f32[72,256]{1,0:T(8,128)S(1)}, f32[72,256]{1,0:T(8,128)S(1)}, u32[]{:S(2)}, u32[]{:S(2)}) collective-permute-start(f32[72,256]{1,0:T(8,128)S(1)} %collective-permute-done.7.refs_0_), channel_id=1, source_target_pairs={{0,2},{2,0},{1,3},{3,1},{4,6},{6,4},{5,7},{7,5},{8,10},{10,8},{9,1... | collective-permute-start | bytes 221192 | tf_op jit(solution)/shard_map/ppermute | solution.py:623
  27.6 1.2 %collective-permute-start.12 = (f32[8,128]{1,0:T(8,128)S(1)}, f32[8,128]{1,0:T(8,128)S(1)}, u32[]{:S(2)}, u32[]{:S(2)}) collective-permute-start(f32[8,128]{1,0:T(8,128)S(1)} %fusion), channel_id=1, source_target_pairs={{0,2},{2,0},{1,3},{3,1},{4,6},{6,4},{5,7},{7,5},{8,10},{10,8},{9,1... | collective-permute-start | bytes 12296 | tf_op jit(solution)/shard_map/ppermute | solution.py:625

commit v8 on v7

--- a/solution.py
+++ b/solution.py
@@ -272,9 +272,9 @@
         for i in range(at_once):
             build(step * at_once + i, 16 * i)
     image_copy(0).wait()
-    mask_copy(0).wait()
     for i in range(at_once):
         smear(i)
+    mask_copy(0).wait()
     ready = max(min(middle // at_once - 1, steps - 2), 0)
 
     def body(step, carry):

time: 29.8 us -> 29.8 us (level)
  no operation moved by 1% of the time
where the time goes in v8:
time: 29.8 us; the launch traced here: 29.7 us
  starting transfers between devices  13.1 us (44%)
  Pallas kernels  9.88 us (33%)
  waiting for transfers between devices  5.97 us (20%)
  between operations  0.73 us (2%)
    ppermute x4, starting transfers between devices, paired(): return lax.ppermute(value, ('sky', 'exp'), pairs)  6.03 us
    pallas_call x1, Pallas kernels, on_device(): pl.pallas_call(inner_kernel, in_specs=[HBM] * 6, out_specs=[VMEM] * 6, ou...  5.32 us
    ppermute x3, starting transfers between devices, on_device(): total = total + lax.ppermute(power, ('sky', 'exp', 'band'), pairs)  4.39 us
    ppermute x3, waiting for transfers between devices, on_device(): total = total + lax.ppermute(power, ('sky', 'exp', 'band'), pairs)  2.78 us
    ppermute x1, waiting for transfers between devices, on_device(): edge_other = lax.ppermute(edge_lists, 'exp', swap)  1.65 us
    ppermute x1, starting transfers between devices, turned(): lax.ppermute(value, axis, [(i, (i + step) % size) for i in range(size)])  1.55 us
    pallas_call x1, Pallas kernels, on_device(): pl.pallas_call(inner_psf_kernel, in_specs=[VMEM] * 7, out_specs=[VMEM] *...  1.23 us
    ppermute x1, waiting for transfers between devices, on_device(): other = lax.ppermute(total, 'exp', swap)  1.15 us
  transfers between devices with their start and end apart: 13, of which 6 were waited for; matrix products, arithmetic and copies ran while one was open for 0% of the time, Pallas kernels for 22%

profile of v8, /device:TPU:0, one launch (start us, length us, event | category | flops | bytes accessed | tf_op | source)
XLA Modules:
  0.0 29.7 jit_solution(10865406106999475102)
XLA Ops:
  0.6 1.0 %rims.1 = (bf16[10,16,512]{2,1,0:T(8,128)(2,1)S(1)}, bf16[10,16,512]{2,1,0:T(8,128)(2,1)S(1)}) custom-call(bf16[1,10,128,512]{3,2,1,0:T(8,128)(2,1)} %images.1), custom_call_target="tpu_custom_call" | custom-call | tf_op jit(solution)/shard_map/rims/pallas_call | solution.py:484
  1.7 3.1 %collective-permute-start = (bf16[10,16,512]{2,1,0:T(8,128)(2,1)S(1)}, bf16[10,16,512]{2,1,0:T(8,128)(2,1)S(1)}, u32[]{:S(2)}, u32[]{:S(2)}) collective-permute-start(bf16[10,16,512]{2,1,0:T(8,128)(2,1)S(1)} %get-tuple-element.28), channel_id=1, source_target_pairs={{0,4},{2,6},{4,0},{6,2},{8,12},{10,14},{12,8},{14,10},{1,5},{3,7},... | collective-permute-start | bytes 491528 | tf_op jit(solution)/shard_map/ppermute | solution.py:467
  4.8 5.3 %inner_visits.1 = (f32[10,56,512]{2,1,0:T(8,128)S(1)}, f32[10,40,512]{2,1,0:T(8,128)S(1)}, f32[10,32,512]{2,1,0:T(8,128)S(1)}, bf16[10,64,128]{2,1,0:T(8,128)(2,...) custom-call(s32[1,10]{1,0:T(1,128)} %groups_h.1, f32[1,16]{1,0:T(1,128)} %points_h.1, ...), custom_call_target="tpu_custom_call" | custom-call | flops 2684354560 | bytes 3932160 | tf_op jit(solution)/shard_map/inner_visits/pallas_call | solution.py:497
  10.1 1.0 %edge_visits.1.mine = f32[10,32,512]{2,1,0:T(8,128)S(1)} custom-call(bf16[10,16,512]{2,1,0:T(8,128)(2,1)S(1)} %collective-permute-done.first, bf16[10,16,512]{2,1,0:T(8,128)(2,1)S(1)} %collective-permute-done.1.second, f32[10,32,512]{2,1,0:T(8,128)S(1)} %get-tuple-element.34.part, bf16[10,64,128]{2,1,0:T(8,128)(2,1)S(1)} %get-tuple-element.35.edge_m, ...), custom_call_target="tpu_custom_call" | custom-call | flops 4026531840 | bytes 1310720 | tf_op jit(solution)/shard_map/edge_visits/pallas_call | solution.py:550
  11.2 0.6 %collective-permute-start.3 = (f32[10,32,512]{2,1,0:T(8,128)S(1)}, f32[10,32,512]{2,1,0:T(8,128)S(1)}, u32[]{:S(2)}, u32[]{:S(2)}) collective-permute-start(f32[10,32,512]{2,1,0:T(8,128)S(1)} %edge_visits.1.mine), channel_id=1, source_target_pairs={{0,2},{2,0},{1,3},{3,1},{4,6},{6,4},{5,7},{7,5},{8,10},{10,8},{9,1... | collective-permute-start | bytes 1966088 | tf_op jit(solution)/shard_map/ppermute | solution.py:563
  11.7 0.1 collective-permute-start.2
  11.8 1.6 %collective-permute-done.3.other = f32[10,32,512]{2,1,0:T(8,128)S(1)} collective-permute-done((f32[10,32,512]{2,1,0:T(8,128)S(1)}, f32[10,32,512]{2,1,0:T(8,128)S(1)}, u32[]{:S(2)}, u32[]{:S(2)}) %collective-permute-start.3) | collective-permute-done | bytes 655392 | tf_op jit(solution)/shard_map/ppermute | solution.py:563
  13.5 0.4 %collective-permute-start.4 = (f32[10,40,512]{2,1,0:T(8,128)S(1)}, f32[10,40,512]{2,1,0:T(8,128)S(1)}, u32[]{:S(2)}, u32[]{:S(2)}) collective-permute-start(f32[10,40,512]{2,1,0:T(8,128)S(1)} %get-tuple-element.38.late_mine), channel_id=1, source_target_pairs={{0,2},{2,0},{1,3},{3,1},{4,6},{6,4},{5,7},{7,5},{8,10},{10,8},{9,1... | collective-permute-start | bytes 2457608 | tf_op jit(solution)/shard_map/ppermute | solution.py:566
  13.8 0.1 edge_merge.1
  14.0 2.9 %collective-permute-start.5 = (bf16[16,512]{1,0:T(8,128)(2,1)S(1)}, bf16[16,512]{1,0:T(8,128)(2,1)S(1)}, u32[]{:S(2)}, u32[]{:S(2)}) collective-permute-start(bf16[16,512]{1,0:T(8,128)(2,1)S(1)} %get-tuple-element.41), channel_id=1, source_target_pairs={{0,4},{2,6},{4,0},{6,2},{8,12},{10,14},{12,8},{14,10},{1,5},{3,7},... | collective-permute-start | bytes 49160 | tf_op jit(solution)/shard_map/ppermute | solution.py:467
  16.8 0.1 collective-permute-start.6
  16.9 1.2 %inner_psf.1 = (f32[1,128,512]{2,1,0:T(8,128)}, f32[96,512]{1,0:T(8,128)S(1)}, f32[8,128]{1,0:T(8,128)S(1)}, f32[32,512]{1,0:T(8,128)S(1)}, bf16[64,128]{1,0:T(8,128)(2,1)S(1)}, /*index=5*/bf16[256,256]{1,0:T(8,128)(2,1)S(1)}) custom-call(f32[10,56,512]{2,1,0:T(8,128)S(1)} %get-tuple-element.30.early_mine, ...), custom_call_target="tpu_custom_call" | custom-call | tf_op jit(solution)/shard_map/inner_psf/pallas_call | solution.py:578
  18.2 0.4 %collective-permute-done.5.first = bf16[16,512]{1,0:T(8,128)(2,1)S(1)} collective-permute-done((bf16[16,512]{1,0:T(8,128)(2,1)S(1)}, bf16[16,512]{1,0:T(8,128)(2,1)S(1)}, u32[]{:S(2)}, u32[]{:S(2)}) %collective-permute-start.5) | collective-permute-done | bytes 16416 | tf_op jit(solution)/shard_map/ppermute | solution.py:467
  18.5 0.4 %edge_psf.1 = (f32[32,512]{1,0:T(8,128)S(1)}, f32[8,128]{1,0:T(8,128)S(1)}, f32[1,72,256]{2,1,0:T(8,128)S(1)}) custom-call(bf16[16,512]{1,0:T(8,128)(2,1)S(1)} %collective-permute-done.5.first, bf16[16,512]{1,0:T(8,128)(2,1)S(1)} %collective-permute-done.6.second, f32[32,512]{1,0:T(8,128)S(1)} %get-tuple-element.43.part, ...), custom_call_target="tpu_custom_call" | custom-call | tf_op jit(solution)/shard_map/edge_psf/pallas_call | solution.py:596
  18.9 1.6 %collective-permute-start.7 = (f32[72,256]{1,0:T(8,128)S(1)}, f32[72,256]{1,0:T(8,128)S(1)}, u32[]{:S(2)}, u32[]{:S(2)}) collective-permute-start(f32[72,256]{1,0:T(8,128)S(1)} %bitcast.5), channel_id=1, source_target_pairs={{0,1},{1,0},{2,3},{3,2},{4,5},{5,4},{6,7},{7,6},{8,9},{9,8},{10,11... | collective-permute-start | bytes 221192 | tf_op jit(solution)/shard_map/ppermute | solution.py:476
  20.5 1.7 %collective-permute-start.10 = (f32[8,128]{1,0:T(8,128)S(1)}, f32[8,128]{1,0:T(8,128)S(1)}, u32[]{:S(2)}, u32[]{:S(2)}) collective-permute-start(f32[8,128]{1,0:T(8,128)S(1)} %get-tuple-element.50), channel_id=1, source_target_pairs={{0,12},{1,13},{2,15},{3,14},{4,8},{5,9},{6,11},{7,10},{8,4},{9,5},... | collective-permute-start | bytes 12296 | tf_op jit(solution)/shard_map/ppermute | solution.py:621
  22.2 1.9 %collective-permute-start.11 = (f32[8,128]{1,0:T(8,128)S(1)}, f32[8,128]{1,0:T(8,128)S(1)}, u32[]{:S(2)}, u32[]{:S(2)}) collective-permute-start(f32[8,128]{1,0:T(8,128)S(1)} %get-tuple-element.50), channel_id=1, source_target_pairs={{0,8},{1,9},{2,11},{3,10},{4,12},{5,13},{6,15},{7,14},{8,0},{9,1},... | collective-permute-start | bytes 12296 | tf_op jit(solution)/shard_map/ppermute | solution.py:621
  24.0 0.8 %collective-permute-start.9 = (f32[8,128]{1,0:T(8,128)S(1)}, f32[8,128]{1,0:T(8,128)S(1)}, u32[]{:S(2)}, u32[]{:S(2)}) collective-permute-start(f32[8,128]{1,0:T(8,128)S(1)} %get-tuple-element.50), channel_id=1, source_target_pairs={{0,4},{1,5},{2,7},{3,6},{4,0},{5,1},{6,3},{7,2},{8,12},{9,13},{10,... | collective-permute-start | bytes 12296 | tf_op jit(solution)/shard_map/ppermute | solution.py:621
  24.9 1.0 %collective-permute-done.10 = f32[8,128]{1,0:T(8,128)S(1)} collective-permute-done((f32[8,128]{1,0:T(8,128)S(1)}, f32[8,128]{1,0:T(8,128)S(1)}, u32[]{:S(2)}, u32[]{:S(2)}) %collective-permute-start.10) | collective-permute-done | bytes 4128 | tf_op jit(solution)/shard_map/ppermute | solution.py:621
  25.9 0.8 %collective-permute-done.11 = f32[8,128]{1,0:T(8,128)S(1)} collective-permute-done((f32[8,128]{1,0:T(8,128)S(1)}, f32[8,128]{1,0:T(8,128)S(1)}, u32[]{:S(2)}, u32[]{:S(2)}) %collective-permute-start.11) | collective-permute-done | bytes 4128 | tf_op jit(solution)/shard_map/ppermute | solution.py:621
  26.7 1.0 %collective-permute-done.9 = f32[8,128]{1,0:T(8,128)S(1)} collective-permute-done((f32[8,128]{1,0:T(8,128)S(1)}, f32[8,128]{1,0:T(8,128)S(1)}, u32[]{:S(2)}, u32[]{:S(2)}) %collective-permute-start.9) | collective-permute-done | bytes 4128 | tf_op jit(solution)/shard_map/ppermute | solution.py:621
  27.7 0.1 collective-permute-start.12
  27.7 1.2 %collective-permute-done.12 = f32[8,128]{1,0:T(8,128)S(1)} collective-permute-done((f32[8,128]{1,0:T(8,128)S(1)}, f32[8,128]{1,0:T(8,128)S(1)}, u32[]{:S(2)}, u32[]{:S(2)}) %collective-permute-start.12) | collective-permute-done | bytes 4128 | tf_op jit(solution)/shard_map/ppermute | solution.py:625
  28.9 0.8 %detection.1 = f32[128,256]{1,0:T(8,128)} custom-call(f32[32,512]{1,0:T(8,128)S(1)} %get-tuple-element.48.edges, f32[96,512]{1,0:T(8,128)S(1)} %get-tuple-element.46.inner, f32[72,256]{1,0:T(8,128)S(1)} %collective-permute-done.7.refs_0_, f32[72,256]{1,0:T(8,128)S(1)} %collective-permute-done.8.refs_1_, f32[2,8,128]{2,1,0:T(8,128)S(1)} %maximum_select_fusion.refs_2_), custom_call_target="tpu_custom_call" | custom-call | tf_op jit(solution)/shard_map/detection/pallas_call | solution.py:631
  (15 shorter events, 0.0 us)
Async XLA Ops:
  1.7 8.4 %collective-permute-start = (bf16[10,16,512]{2,1,0:T(8,128)(2,1)S(1)}, bf16[10,16,512]{2,1,0:T(8,128)(2,1)S(1)}, u32[]{:S(2)}, u32[]{:S(2)}) collective-permute-start(bf16[10,16,512]{2,1,0:T(8,128)(2,1)S(1)} %get-tuple-element.28), channel_id=1, source_target_pairs={{0,4},{2,6},{4,0},{6,2},{8,12},{10,14},{12,8},{14,10},{1,5},{3,7},... | collective-permute-start | bytes 491528 | tf_op jit(solution)/shard_map/ppermute | solution.py:467
  4.8 5.3 %collective-permute-start.1 = (bf16[10,16,512]{2,1,0:T(8,128)(2,1)S(1)}, bf16[10,16,512]{2,1,0:T(8,128)(2,1)S(1)}, u32[]{:S(2)}, u32[]{:S(2)}) collective-permute-start(bf16[10,16,512]{2,1,0:T(8,128)(2,1)S(1)} %get-tuple-element.29), channel_id=1, source_target_pairs={{0,2},{2,0},{4,8},{6,10},{8,4},{10,6},{12,14},{14,12},{1,3},{3,1},... | collective-permute-start | bytes 491528 | tf_op jit(solution)/shard_map/ppermute | solution.py:467
  11.1 5.8 %copy-start = (f32[1,31]{1,0:T(1,128)S(1)}, f32[1,31]{1,0:T(1,128)}, u32[]{:S(2)}) copy-start(f32[1,31]{1,0:T(1,128)} %row_taps.1) | copy-start | bytes 376
  11.1 5.8 %copy-start.1 = (f32[1,31]{1,0:T(1,128)S(1)}, f32[1,31]{1,0:T(1,128)}, u32[]{:S(2)}) copy-start(f32[1,31]{1,0:T(1,128)} %col_taps.1) | copy-start | bytes 376
  11.2 2.3 %collective-permute-start.3 = (f32[10,32,512]{2,1,0:T(8,128)S(1)}, f32[10,32,512]{2,1,0:T(8,128)S(1)}, u32[]{:S(2)}, u32[]{:S(2)}) collective-permute-start(f32[10,32,512]{2,1,0:T(8,128)S(1)} %edge_visits.1.mine), channel_id=1, source_target_pairs={{0,2},{2,0},{1,3},{3,1},{4,6},{6,4},{5,7},{7,5},{8,10},{10,8},{9,1... | collective-permute-start | bytes 1966088 | tf_op jit(solution)/shard_map/ppermute | solution.py:563
  11.7 5.2 %collective-permute-start.2 = (f32[10,56,512]{2,1,0:T(8,128)S(1)}, f32[10,56,512]{2,1,0:T(8,128)S(1)}, u32[]{:S(2)}, u32[]{:S(2)}) collective-permute-start(f32[10,56,512]{2,1,0:T(8,128)S(1)} %get-tuple-element.30.early_mine), channel_id=1, source_target_pairs={{0,2},{2,0},{1,3},{3,1},{4,6},{6,4},{5,7},{7,5},{8,10},{10,8},{9,1... | collective-permute-start | bytes 3440648 | tf_op jit(solution)/shard_map/ppermute | solution.py:549
  13.5 3.5 %collective-permute-start.4 = (f32[10,40,512]{2,1,0:T(8,128)S(1)}, f32[10,40,512]{2,1,0:T(8,128)S(1)}, u32[]{:S(2)}, u32[]{:S(2)}) collective-permute-start(f32[10,40,512]{2,1,0:T(8,128)S(1)} %get-tuple-element.38.late_mine), channel_id=1, source_target_pairs={{0,2},{2,0},{1,3},{3,1},{4,6},{6,4},{5,7},{7,5},{8,10},{10,8},{9,1... | collective-permute-start | bytes 2457608 | tf_op jit(solution)/shard_map/ppermute | solution.py:566
  14.0 4.6 %collective-permute-start.5 = (bf16[16,512]{1,0:T(8,128)(2,1)S(1)}, bf16[16,512]{1,0:T(8,128)(2,1)S(1)}, u32[]{:S(2)}, u32[]{:S(2)}) collective-permute-start(bf16[16,512]{1,0:T(8,128)(2,1)S(1)} %get-tuple-element.41), channel_id=1, source_target_pairs={{0,4},{2,6},{4,0},{6,2},{8,12},{10,14},{12,8},{14,10},{1,5},{3,7},... | collective-permute-start | bytes 49160 | tf_op jit(solution)/shard_map/ppermute | solution.py:467
  16.8 1.7 %collective-permute-start.6 = (bf16[16,512]{1,0:T(8,128)(2,1)S(1)}, bf16[16,512]{1,0:T(8,128)(2,1)S(1)}, u32[]{:S(2)}, u32[]{:S(2)}) collective-permute-start(bf16[16,512]{1,0:T(8,128)(2,1)S(1)} %get-tuple-element.42), channel_id=1, source_target_pairs={{0,2},{2,0},{4,8},{6,10},{8,4},{10,6},{12,14},{14,12},{1,3},{3,1},... | collective-permute-start | bytes 49160 | tf_op jit(solution)/shard_map/ppermute | solution.py:467
  18.9 5.9 %collective-permute-start.7 = (f32[72,256]{1,0:T(8,128)S(1)}, f32[72,256]{1,0:T(8,128)S(1)}, u32[]{:S(2)}, u32[]{:S(2)}) collective-permute-start(f32[72,256]{1,0:T(8,128)S(1)} %bitcast.5), channel_id=1, source_target_pairs={{0,1},{1,0},{2,3},{3,2},{4,5},{5,4},{6,7},{7,6},{8,9},{9,8},{10,11... | collective-permute-start | bytes 221192 | tf_op jit(solution)/shard_map/ppermute | solution.py:476
  20.5 5.4 %collective-permute-start.10 = (f32[8,128]{1,0:T(8,128)S(1)}, f32[8,128]{1,0:T(8,128)S(1)}, u32[]{:S(2)}, u32[]{:S(2)}) collective-permute-start(f32[8,128]{1,0:T(8,128)S(1)} %get-tuple-element.50), channel_id=1, source_target_pairs={{0,12},{1,13},{2,15},{3,14},{4,8},{5,9},{6,11},{7,10},{8,4},{9,5},... | collective-permute-start | bytes 12296 | tf_op jit(solution)/shard_map/ppermute | solution.py:621
  22.2 4.5 %collective-permute-start.11 = (f32[8,128]{1,0:T(8,128)S(1)}, f32[8,128]{1,0:T(8,128)S(1)}, u32[]{:S(2)}, u32[]{:S(2)}) collective-permute-start(f32[8,128]{1,0:T(8,128)S(1)} %get-tuple-element.50), channel_id=1, source_target_pairs={{0,8},{1,9},{2,11},{3,10},{4,12},{5,13},{6,15},{7,14},{8,0},{9,1},... | collective-permute-start | bytes 12296 | tf_op jit(solution)/shard_map/ppermute | solution.py:621
  24.0 3.6 %collective-permute-start.9 = (f32[8,128]{1,0:T(8,128)S(1)}, f32[8,128]{1,0:T(8,128)S(1)}, u32[]{:S(2)}, u32[]{:S(2)}) collective-permute-start(f32[8,128]{1,0:T(8,128)S(1)} %get-tuple-element.50), channel_id=1, source_target_pairs={{0,4},{1,5},{2,7},{3,6},{4,0},{5,1},{6,3},{7,2},{8,12},{9,13},{10,... | collective-permute-start | bytes 12296 | tf_op jit(solution)/shard_map/ppermute | solution.py:621
  24.9 2.8 %collective-permute-start.8 = (f32[72,256]{1,0:T(8,128)S(1)}, f32[72,256]{1,0:T(8,128)S(1)}, u32[]{:S(2)}, u32[]{:S(2)}) collective-permute-start(f32[72,256]{1,0:T(8,128)S(1)} %collective-permute-done.7.refs_0_), channel_id=1, source_target_pairs={{0,2},{2,0},{1,3},{3,1},{4,6},{6,4},{5,7},{7,5},{8,10},{10,8},{9,1... | collective-permute-start | bytes 221192 | tf_op jit(solution)/shard_map/ppermute | solution.py:623
  27.7 1.2 %collective-permute-start.12 = (f32[8,128]{1,0:T(8,128)S(1)}, f32[8,128]{1,0:T(8,128)S(1)}, u32[]{:S(2)}, u32[]{:S(2)}) collective-permute-start(f32[8,128]{1,0:T(8,128)S(1)} %fusion), channel_id=1, source_target_pairs={{0,2},{2,0},{1,3},{3,1},{4,6},{6,4},{5,7},{7,5},{8,10},{10,8},{9,1... | collective-permute-start | bytes 12296 | tf_op jit(solution)/shard_map/ppermute | solution.py:625
